TPU v7x, 32 devices: a whole 2x2x4 slice. The times are simulated.
32 devices in a mesh: fsdp: 8 (over z, x), tok: 4 (over y, core).
Axes of the slice: x: 2, y: 2, z: 4, core: 2. Of those that a mesh axis runs over, the one named last changes fastest.
Arguments:
- tokens: bfloat16 [2, 8, 1024, 1024], P(None, 'fsdp', 'tok'), may hold values from -6 to 6
- cotangent: bfloat16 [2, 8, 1024, 1024], P(None, 'fsdp', 'tok'), may hold values from -6 to 6
- doc_lengths: int32 [2, 8, 4], P(None, 'fsdp'), may hold values from 0 to 1024, as said below
- norm1_gain: bfloat16 [1024], P('fsdp'), may hold values from 0.099609375 to 1.8984375
- norm1_shift: bfloat16 [1024], P('fsdp'), may hold values from -1.75 to 1.75
- w_qkv: bfloat16 [1024, 3072], P('fsdp'), may hold values from -0.1875 to 0.1875
- bias_query: bfloat16 [1024], P('fsdp'), may hold values from -1.75 to 1.75
- bias_value: bfloat16 [1024], P('fsdp'), may hold values from -1.75 to 1.75
- w_out: bfloat16 [1024, 1024], P('fsdp'), may hold values from -3 to 3
- bias_out: bfloat16 [1024], P('fsdp'), may hold values from -1.75 to 1.75
- norm2_gain: bfloat16 [1024], P('fsdp'), may hold values from 0.099609375 to 1.8984375
- norm2_shift: bfloat16 [1024], P('fsdp'), may hold values from -1.75 to 1.75
- w_fc1: bfloat16 [1024, 4096], P('fsdp'), may hold values from -0.1875 to 0.1875
- bias_fc1: bfloat16 [4096], P('fsdp'), may hold values from -1.75 to 1.75
- w_fc2: bfloat16 [4096, 1024], P('fsdp'), may hold values from -0.09375 to 0.09375
- bias_fc2: bfloat16 [1024], P('fsdp'), may hold values from -1.75 to 1.75
Outputs:
- output: bfloat16 [2, 8, 1024, 1024], P(None, 'fsdp', 'tok')
- grad_tokens: bfloat16 [2, 8, 1024, 1024], P(None, 'fsdp', 'tok')
- grad_norm1_gain: float32 [1024], P(('fsdp', 'tok'))
- grad_norm1_shift: float32 [1024], P(('fsdp', 'tok'))
- grad_w_qkv: float32 [1024, 3072], P(('fsdp', 'tok'))
- grad_bias_query: float32 [1024], P(('fsdp', 'tok'))
- grad_bias_value: float32 [1024], P(('fsdp', 'tok'))
- grad_w_out: float32 [1024, 1024], P(('fsdp', 'tok'))
- grad_bias_out: float32 [1024], P(('fsdp', 'tok'))
- grad_norm2_gain: float32 [1024], P(('fsdp', 'tok'))
- grad_norm2_shift: float32 [1024], P(('fsdp', 'tok'))
- grad_w_fc1: float32 [1024, 4096], P(('fsdp', 'tok'))
- grad_bias_fc1: float32 [4096], P(('fsdp', 'tok'))
- grad_w_fc2: float32 [4096, 1024], P(('fsdp', 'tok'))
- grad_bias_fc2: float32 [1024], P(('fsdp', 'tok'))
Inputs may be any that keep to these rules, and one draw needn't show every extreme that they name: `doc_lengths`: each sequence's 4 lengths sum to 1024; a length 0 is an empty document. Among the 2 sequences of each index of fsdp, one is a single document.
All inputs are finite; a program needn't handle non-finite values.
Results may differ from a plain program's by a relative error of at most 0.013.
Values may be sent and summed in bfloat16 or wider, within the bound.
No kernel may reach another device: no remote copies, remote signals or barrier semaphores. Data moves between devices by JAX's collectives and lax.ppermute only.
A program may use at most 256 MiB of HBM per device.

v0:
```python
import jax
import jax.numpy as jnp
from jax import lax
from jax.sharding import PartitionSpec as P

DH = 64


eps = 1e-05
masked_value = -1e30


def layer_norm(values, gain, shift):
    mean = jnp.mean(values, axis=-1, keepdims=True)
    centered = values - mean
    spread = jnp.mean(centered * centered, axis=-1, keepdims=True)
    return centered * lax.rsqrt(spread + eps) * gain + shift


def norm_back(values, gain, shift, upstream):
    result, pull = jax.vjp(layer_norm, values, gain, shift)
    return pull(upstream)


def smooth_gate(values):
    return jax.nn.gelu(values, approximate=True)


def doc_mask(lengths, first, count, total):
    ends = jnp.cumsum(lengths, axis=-1)
    query_pos = first + jnp.arange(count, dtype=jnp.int32)
    key_pos = jnp.arange(total, dtype=jnp.int32)
    query_doc = jnp.sum((query_pos[None, :, None] >= ends[:, None, :]).astype(jnp.int32), axis=-1)
    key_doc = jnp.sum((key_pos[None, :, None] >= ends[:, None, :]).astype(jnp.int32), axis=-1)
    causal = key_pos[None, None, :] <= query_pos[None, :, None]
    return causal & (query_doc[:, :, None] == key_doc[:, None, :])


def split_heads(values):
    return values.reshape(values.shape[0], values.shape[1], values.shape[2] // DH, DH)


def masked_scores(query_h, key_h, mask):
    scores = jnp.einsum(
        "sqhd,skhd->shqk", query_h, key_h, preferred_element_type=jnp.float32
    ) * DH ** (-0.5)
    return jnp.where(mask[:, None], scores, masked_value)


def forward(params, rows, lengths, tok_index):
    (
        norm1_gain,
        norm1_shift,
        w_qkv,
        bias_query,
        bias_value,
        w_out,
        bias_out,
        norm2_gain,
        norm2_shift,
        w_fc1,
        bias_fc1,
        w_fc2,
        bias_fc2,
    ) = params
    width = rows.shape[-1]
    inputs = rows.astype(jnp.float32)
    normed = layer_norm(
        inputs, norm1_gain.astype(jnp.float32), norm1_shift.astype(jnp.float32)
    ).astype(jnp.bfloat16)
    mixed = jnp.einsum("sqd,de->sqe", normed, w_qkv, preferred_element_type=jnp.float32)
    query = (mixed[..., :width] + bias_query).astype(jnp.bfloat16)
    key = mixed[..., width : 2 * width].astype(jnp.bfloat16)
    value = (mixed[..., 2 * width :] + bias_value).astype(jnp.bfloat16)
    keys, values = (
        lax.all_gather(key, "tok", axis=1, tiled=True),
        lax.all_gather(value, "tok", axis=1, tiled=True),
    )
    local_len = rows.shape[1]
    mask = doc_mask(lengths, tok_index * local_len, local_len, keys.shape[1])
    scores = masked_scores(split_heads(query), split_heads(keys), mask)
    top = jnp.max(scores, axis=-1, keepdims=True)
    log_total = top + jnp.log(jnp.sum(jnp.exp(scores - top), axis=-1, keepdims=True))
    probs_low = jnp.exp(scores - log_total).astype(jnp.bfloat16)
    attended = jnp.einsum(
        "shqk,skhd->sqhd", probs_low, split_heads(values), preferred_element_type=jnp.float32
    )
    attended = attended.reshape(rows.shape).astype(jnp.bfloat16)
    middle = (
        inputs
        + jnp.einsum("sqd,de->sqe", attended, w_out, preferred_element_type=jnp.float32)
        + bias_out
    )
    normed2 = layer_norm(
        middle, norm2_gain.astype(jnp.float32), norm2_shift.astype(jnp.float32)
    ).astype(jnp.bfloat16)
    hidden = (
        jnp.einsum("sqd,df->sqf", normed2, w_fc1, preferred_element_type=jnp.float32) + bias_fc1
    )
    active = smooth_gate(hidden).astype(jnp.bfloat16)
    result = (
        middle
        + jnp.einsum("sqf,fd->sqd", active, w_fc2, preferred_element_type=jnp.float32)
        + bias_fc2
    )
    stored = (
        inputs,
        normed,
        query,
        keys,
        values,
        mask,
        log_total,
        attended,
        middle,
        normed2,
        hidden,
        active,
    )
    return (result.astype(jnp.bfloat16), stored)


def backward(params, stored, upstream):
    (
        norm1_gain,
        norm1_shift,
        w_qkv,
        bias_query,
        bias_value,
        w_out,
        bias_out,
        norm2_gain,
        norm2_shift,
        w_fc1,
        bias_fc1,
        w_fc2,
        bias_fc2,
    ) = params
    (
        inputs,
        normed,
        query,
        keys,
        values,
        mask,
        log_total,
        attended,
        middle,
        normed2,
        hidden,
        active,
    ) = stored
    grad_out = upstream.astype(jnp.float32)
    grad_fc2 = jnp.einsum("sqf,sqd->fd", active, upstream, preferred_element_type=jnp.float32)
    grad_bias_fc2 = jnp.sum(grad_out, axis=(0, 1))
    grad_active = jnp.einsum("sqd,fd->sqf", upstream, w_fc2, preferred_element_type=jnp.float32)
    unused, gate_pull = jax.vjp(smooth_gate, hidden)
    grad_hidden = gate_pull(grad_active)[0].astype(jnp.bfloat16)
    grad_fc1 = jnp.einsum("sqd,sqf->df", normed2, grad_hidden, preferred_element_type=jnp.float32)
    grad_bias_fc1 = jnp.sum(grad_hidden.astype(jnp.float32), axis=(0, 1))
    grad_normed2 = jnp.einsum("sqf,df->sqd", grad_hidden, w_fc1, preferred_element_type=jnp.float32)
    grad_mid_norm, grad_gain2, grad_shift2 = norm_back(
        middle, norm2_gain.astype(jnp.float32), norm2_shift.astype(jnp.float32), grad_normed2
    )
    grad_middle = grad_out + grad_mid_norm
    grad_branch = grad_middle.astype(jnp.bfloat16)
    grad_w_out = jnp.einsum(
        "sqd,sqe->de", attended, grad_branch, preferred_element_type=jnp.float32
    )
    grad_bias_out = jnp.sum(grad_branch.astype(jnp.float32), axis=(0, 1))
    grad_attended = jnp.einsum(
        "sqe,de->sqd", grad_branch, w_out, preferred_element_type=jnp.float32
    ).astype(jnp.bfloat16)
    query_h = split_heads(query)
    key_h = split_heads(keys)
    value_h = split_heads(values)
    grad_h = split_heads(grad_attended)
    probs = jnp.exp(masked_scores(query_h, key_h, mask) - log_total)
    probs_low = probs.astype(jnp.bfloat16)
    grad_probs = jnp.einsum("sqhd,skhd->shqk", grad_h, value_h, preferred_element_type=jnp.float32)
    inner = jnp.sum(probs * grad_probs, axis=-1, keepdims=True)
    grad_scores = (probs * (grad_probs - inner)).astype(jnp.bfloat16)
    scale = DH ** (-0.5)
    grad_query = (
        jnp.einsum("shqk,skhd->sqhd", grad_scores, key_h, preferred_element_type=jnp.float32)
        * scale
    )
    grad_query = grad_query.reshape(inputs.shape).astype(jnp.bfloat16)
    part_key = (
        jnp.einsum("shqk,sqhd->skhd", grad_scores, query_h, preferred_element_type=jnp.float32)
        * scale
    )
    part_value = jnp.einsum(
        "shqk,sqhd->skhd", probs_low, grad_h, preferred_element_type=jnp.float32
    )
    part_key = part_key.reshape(keys.shape)
    part_value = part_value.reshape(keys.shape)
    grad_key, grad_value = (
        lax.psum_scatter(
            part_key.astype(jnp.bfloat16), "tok", scatter_dimension=1, tiled=True
        ).astype(jnp.float32),
        lax.psum_scatter(
            part_value.astype(jnp.bfloat16), "tok", scatter_dimension=1, tiled=True
        ).astype(jnp.float32),
    )
    grad_key = grad_key.astype(jnp.bfloat16)
    grad_value = grad_value.astype(jnp.bfloat16)
    grad_mixed = jnp.concatenate([grad_query, grad_key, grad_value], axis=-1)
    grad_qkv = jnp.einsum("sqd,sqe->de", normed, grad_mixed, preferred_element_type=jnp.float32)
    grad_bias_query = jnp.sum(grad_query.astype(jnp.float32), axis=(0, 1))
    grad_bias_value = jnp.sum(grad_value.astype(jnp.float32), axis=(0, 1))
    grad_normed = jnp.einsum("sqe,de->sqd", grad_mixed, w_qkv, preferred_element_type=jnp.float32)
    grad_in_norm, grad_gain1, grad_shift1 = norm_back(
        inputs, norm1_gain.astype(jnp.float32), norm1_shift.astype(jnp.float32), grad_normed
    )
    grad_inputs = (grad_middle + grad_in_norm).astype(jnp.bfloat16)
    grads = (
        grad_gain1,
        grad_shift1,
        grad_qkv,
        grad_bias_query,
        grad_bias_value,
        grad_w_out,
        grad_bias_out,
        grad_gain2,
        grad_shift2,
        grad_fc1,
        grad_bias_fc1,
        grad_fc2,
        grad_bias_fc2,
    )
    return (grad_inputs, grads)


def local(
    tokens,
    cotangent,
    doc_lengths,
    norm1_gain,
    norm1_shift,
    w_qkv,
    bias_query,
    bias_value,
    w_out,
    bias_out,
    norm2_gain,
    norm2_shift,
    w_fc1,
    bias_fc1,
    w_fc2,
    bias_fc2,
):
    tok_index = lax.axis_index("tok")
    results = []
    input_grads = []
    summed = None
    for micro_step in range(tokens.shape[0]):
        gathered = (
            lax.all_gather(norm1_gain, "fsdp", axis=0, tiled=True),
            lax.all_gather(norm1_shift, "fsdp", axis=0, tiled=True),
            lax.all_gather(w_qkv, "fsdp", axis=0, tiled=True),
            lax.all_gather(bias_query, "fsdp", axis=0, tiled=True),
            lax.all_gather(bias_value, "fsdp", axis=0, tiled=True),
            lax.all_gather(w_out, "fsdp", axis=0, tiled=True),
            lax.all_gather(bias_out, "fsdp", axis=0, tiled=True),
            lax.all_gather(norm2_gain, "fsdp", axis=0, tiled=True),
            lax.all_gather(norm2_shift, "fsdp", axis=0, tiled=True),
            lax.all_gather(w_fc1, "fsdp", axis=0, tiled=True),
            lax.all_gather(bias_fc1, "fsdp", axis=0, tiled=True),
            lax.all_gather(w_fc2, "fsdp", axis=0, tiled=True),
            lax.all_gather(bias_fc2, "fsdp", axis=0, tiled=True),
        )
        result, stored = forward(gathered, tokens[micro_step], doc_lengths[micro_step], tok_index)
        regathered = (
            lax.all_gather(norm1_gain, "fsdp", axis=0, tiled=True),
            lax.all_gather(norm1_shift, "fsdp", axis=0, tiled=True),
            lax.all_gather(w_qkv, "fsdp", axis=0, tiled=True),
            lax.all_gather(bias_query, "fsdp", axis=0, tiled=True),
            lax.all_gather(bias_value, "fsdp", axis=0, tiled=True),
            lax.all_gather(w_out, "fsdp", axis=0, tiled=True),
            lax.all_gather(bias_out, "fsdp", axis=0, tiled=True),
            lax.all_gather(norm2_gain, "fsdp", axis=0, tiled=True),
            lax.all_gather(norm2_shift, "fsdp", axis=0, tiled=True),
            lax.all_gather(w_fc1, "fsdp", axis=0, tiled=True),
            lax.all_gather(bias_fc1, "fsdp", axis=0, tiled=True),
            lax.all_gather(w_fc2, "fsdp", axis=0, tiled=True),
            lax.all_gather(bias_fc2, "fsdp", axis=0, tiled=True),
        )
        grad_inputs, grads = backward(regathered, stored, cotangent[micro_step])
        results.append(result)
        input_grads.append(grad_inputs)
        if summed is None:
            summed = grads
        else:
            summed = tuple((a + b for a, b in zip(summed, grads)))
    owned = (
        lax.psum_scatter(summed[0], ("fsdp", "tok"), scatter_dimension=0, tiled=True),
        lax.psum_scatter(summed[1], ("fsdp", "tok"), scatter_dimension=0, tiled=True),
        lax.psum_scatter(summed[2], ("fsdp", "tok"), scatter_dimension=0, tiled=True),
        lax.psum_scatter(summed[3], ("fsdp", "tok"), scatter_dimension=0, tiled=True),
        lax.psum_scatter(summed[4], ("fsdp", "tok"), scatter_dimension=0, tiled=True),
        lax.psum_scatter(summed[5], ("fsdp", "tok"), scatter_dimension=0, tiled=True),
        lax.psum_scatter(summed[6], ("fsdp", "tok"), scatter_dimension=0, tiled=True),
        lax.psum_scatter(summed[7], ("fsdp", "tok"), scatter_dimension=0, tiled=True),
        lax.psum_scatter(summed[8], ("fsdp", "tok"), scatter_dimension=0, tiled=True),
        lax.psum_scatter(summed[9], ("fsdp", "tok"), scatter_dimension=0, tiled=True),
        lax.psum_scatter(summed[10], ("fsdp", "tok"), scatter_dimension=0, tiled=True),
        lax.psum_scatter(summed[11], ("fsdp", "tok"), scatter_dimension=0, tiled=True),
        lax.psum_scatter(summed[12], ("fsdp", "tok"), scatter_dimension=0, tiled=True),
    )
    return (
        jnp.stack(results),
        jnp.stack(input_grads),
        owned[0],
        owned[1],
        owned[2],
        owned[3],
        owned[4],
        owned[5],
        owned[6],
        owned[7],
        owned[8],
        owned[9],
        owned[10],
        owned[11],
        owned[12],
    )


def solution(mesh):
    placed = (
        P(None, "fsdp", "tok", None),
        P(None, "fsdp", "tok", None),
        P(None, "fsdp", None),
        P("fsdp"),
        P("fsdp"),
        P("fsdp", None),
        P("fsdp"),
        P("fsdp"),
        P("fsdp", None),
        P("fsdp"),
        P("fsdp"),
        P("fsdp"),
        P("fsdp", None),
        P("fsdp"),
        P("fsdp", None),
        P("fsdp"),
    )
    return jax.shard_map(
        local,
        mesh=mesh,
        in_specs=placed,
        out_specs=(
            P(None, "fsdp", "tok", None),
            P(None, "fsdp", "tok", None),
            P(("fsdp", "tok")),
            P(("fsdp", "tok")),
            P(("fsdp", "tok"), None),
            P(("fsdp", "tok")),
            P(("fsdp", "tok")),
            P(("fsdp", "tok"), None),
            P(("fsdp", "tok")),
            P(("fsdp", "tok")),
            P(("fsdp", "tok")),
            P(("fsdp", "tok"), None),
            P(("fsdp", "tok")),
            P(("fsdp", "tok"), None),
            P(("fsdp", "tok")),
        ),
        check_vma=False,
    )
```

profile of v0, /device:TPU:0, one launch (start us, length us, event | category | flops | bytes accessed | tf_op | source)
XLA Modules:
  0.0 1381.4 jit_solution(9547170866594629085)
XLA Ops:
  8.0 22.5 %all-gather.1 = bf16[8,1,128]{2,1,0:T(2,128)(2,1)S(1)} all-gather(bf16[1,1,128]{2,1,0:T(2,128)(2,1)} %bitcast.310), channel_id=1, replica_groups=mesh['fsdp'=8,'tok'=4] {'fsdp'}, dimensions={0}, use_global_device_ids=true | all-gather | bytes 2304 | tf_op jit(solution)/shard_map/all_gather | solution.py:260
  30.5 16.7 %all-gather = bf16[8,1,128]{2,1,0:T(2,128)(2,1)S(1)} all-gather(bf16[1,1,128]{2,1,0:T(2,128)(2,1)} %bitcast.311), channel_id=1, replica_groups=mesh['fsdp'=8,'tok'=4] {'fsdp'}, dimensions={0}, use_global_device_ids=true | all-gather | bytes 2304 | tf_op jit(solution)/shard_map/all_gather | solution.py:259
  47.2 18.4 %all-gather.3 = bf16[8,1,128]{2,1,0:T(2,128)(2,1)S(1)} all-gather(bf16[1,1,128]{2,1,0:T(2,128)(2,1)} %bitcast.312), channel_id=1, replica_groups=mesh['fsdp'=8,'tok'=4] {'fsdp'}, dimensions={0}, use_global_device_ids=true | all-gather | bytes 2304 | tf_op jit(solution)/shard_map/all_gather | solution.py:262
  65.5 16.7 %all-gather.2 = bf16[8,1,128]{2,1,0:T(2,128)(2,1)S(1)} all-gather(bf16[1,1,128]{2,1,0:T(2,128)(2,1)} %bitcast.313), channel_id=1, replica_groups=mesh['fsdp'=8,'tok'=4] {'fsdp'}, dimensions={0}, use_global_device_ids=true | all-gather | bytes 2304 | tf_op jit(solution)/shard_map/all_gather | solution.py:263
  85.9 26.1 %all-gather.18.cloned.1.call-done = bf16[1024,3072]{1,0:T(8,128)(2,1)} async-done(((bf16[128,3072]{1,0:T(8,128)(2,1)}), bf16[1024,3072]{1,0:T(8,128)(2,1)}) %all-gather.18.cloned.1.call-update) | async-done | bytes 6291472 | tf_op jit(solution)/shard_map/all_gather | solution.py:261
  129.5 17.6 %all-gather.4 = bf16[8,1,128]{2,1,0:T(2,128)(2,1)S(1)} all-gather(bf16[1,1,128]{2,1,0:T(2,128)(2,1)S(1)} %bitcast.314), channel_id=1, replica_groups=mesh['fsdp'=8,'tok'=4] {'fsdp'}, dimensions={0}, use_global_device_ids=true | all-gather | bytes 2304 | tf_op jit(solution)/shard_map/all_gather | solution.py:265
  147.5 26.0 %all-gather.7 = bf16[8,1,512]{2,1,0:T(2,128)(2,1)S(1)} all-gather(bf16[1,1,512]{2,1,0:T(2,128)(2,1)S(1)} %reshape.1448), channel_id=1, replica_groups=mesh['fsdp'=8,'tok'=4] {'fsdp'}, dimensions={0}, use_global_device_ids=true | all-gather | bytes 9216 | tf_op jit(solution)/shard_map/all_gather | solution.py:269
  173.5 16.2 %all-gather.6 = bf16[8,1,128]{2,1,0:T(2,128)(2,1)S(1)} all-gather(bf16[1,1,128]{2,1,0:T(2,128)(2,1)S(1)} %bitcast.315), channel_id=1, replica_groups=mesh['fsdp'=8,'tok'=4] {'fsdp'}, dimensions={0}, use_global_device_ids=true | all-gather | bytes 2304 | tf_op jit(solution)/shard_map/all_gather | solution.py:267
  189.7 18.6 %all-gather.5 = bf16[8,1,128]{2,1,0:T(2,128)(2,1)S(1)} all-gather(bf16[1,1,128]{2,1,0:T(2,128)(2,1)S(1)} %bitcast.316), channel_id=1, replica_groups=mesh['fsdp'=8,'tok'=4] {'fsdp'}, dimensions={0}, use_global_device_ids=true | all-gather | bytes 2304 | tf_op jit(solution)/shard_map/all_gather | solution.py:266
  242.1 26.8 %all-gather.24.cloned.1.call-done = bf16[1024,1024]{1,0:T(8,128)(2,1)} async-done(((bf16[128,1024]{1,0:T(8,128)(2,1)}), bf16[1024,1024]{1,0:T(8,128)(2,1)}) %all-gather.24.cloned.1.call-update) | async-done | bytes 2097168 | tf_op jit(solution)/shard_map/all_gather | solution.py:264
  291.5 102.9 %all-gather.26.cloned.1.call-done = bf16[1024,4096]{1,0:T(8,128)(2,1)} async-done(((bf16[128,4096]{1,0:T(8,128)(2,1)}), bf16[1024,4096]{1,0:T(8,128)(2,1)}) %all-gather.26.cloned.1.call-update) | async-done | bytes 8388624 | tf_op jit(solution)/shard_map/all_gather | solution.py:268
  394.4 7.9 convolution_add_fusion.3
  406.8 112.9 %all-gather.28.cloned.1.call-done = bf16[4096,1024]{1,0:T(8,128)(2,1)} async-done(((bf16[512,1024]{1,0:T(8,128)(2,1)}), bf16[4096,1024]{1,0:T(8,128)(2,1)}) %all-gather.28.cloned.1.call-update) | async-done | bytes 8388624 | tf_op jit(solution)/shard_map/all_gather | solution.py:270
  519.7 8.3 convert_reduce_fusion
  541.9 7.9 multiply_reduce_fusion.3
  557.2 11.4 convolution_convert_fusion.1
  568.7 14.3 %multiply_reduce_fusion.1 = (f32[16,256]{1,0:T(8,128)S(1)}, f32[16,256,1024]{2,1,0:T(8,128)}) fusion(f32[16,256,1024]{2,1,0:T(8,128)} %copy-done.1, f32[16,256]{1,0:T(8,128)S(1)} %log_add_fusion.1, pred[256,1024]{1,0:T(8,128)(4,1)S(1)} %copy-done.25, bf16[256,16,64]{0,2,1:T(8,128)(2,1)} %bitcast.274, bf16[1024,16,64]{0,2,1:T(8,128)(2,1)} %bitcast.257), kind=kOutput, calls=%fused_computation.3 | convolution fusion | flops 557838336 | bytes 36470784 | tf_op jit(solution)/shard_map/sqhd,skhd->shqk/dot_general | solution.py:180
  583.0 12.4 multiply_convert_fusion.1
  601.9 10.1 convolution_convert_fusion
  612.1 13.6 multiply_reduce_fusion
  625.8 12.2 multiply_convert_fusion
  661.8 7.8 fusion.71
  669.6 30.8 %reduce-scatter.13.cloned.1.call-done = bf16[1,256,1024]{1,2,0:T(8,128)(2,1)} async-done(((bf16[1,1024,1024]{1,2,0:T(8,128)(2,1)}), bf16[1,256,1024]{1,2,0:T(8,128)(2,1)}) %reduce-scatter.13.cloned.1.call-update) | async-done | bytes 524304 | tf_op jit(solution)/shard_map/reduce_scatter | solution.py:199
  700.5 11.6 convolution_add_fusion.2
  717.0 10.1 convolution_add_fusion.1
  727.1 11.2 fusion.86
  738.3 11.1 convolution_add_fusion
  750.1 20.6 %all-gather.8 = bf16[8,1,128]{2,1,0:T(2,128)(2,1)S(1)} all-gather(bf16[1,1,128]{2,1,0:T(2,128)(2,1)S(1)} %bitcast.317), channel_id=1, replica_groups=mesh['fsdp'=8,'tok'=4] {'fsdp'}, dimensions={0}, use_global_device_ids=true | all-gather | bytes 2304 | tf_op jit(solution)/shard_map/all_gather | solution.py:271
  793.3 38.2 %all-reduce.9 = (f32[1024]{0:T(1024)S(1)}, f32[1024]{0:T(1024)S(1)}, f32[1024]{0:T(1024)S(1)}, f32[1024]{0:T(1024)S(1)}, f32[1024]{0:T(1024)S(1)}, /*index=5*/f3...) all-reduce(f32[1024]{0:T(1024)S(1)} %add.371, ...), channel_id=6, replica_groups=mesh['fsdp'=8,'tok'=4] {'fsdp','tok'}, use_global_device_ids=true, to_apply=%region_34.35.clone | all-reduce | flops 12288 | bytes 98304
  844.5 157.7 %reduce-scatter.17.cloned.1.call-done = f32[32,3072]{1,0:T(8,128)} async-done(((f32[1024,3072]{1,0:T(8,128)}), f32[32,3072]{1,0:T(8,128)}) %reduce-scatter.17.cloned.1.call-update) | async-done | bytes 393232 | tf_op jit(solution)/shard_map/reduce_scatter | solution.py:299
  1002.2 185.0 %reduce-scatter.21.cloned.1.call-done = f32[32,4096]{1,0:T(8,128)} async-done(((f32[1024,4096]{1,0:T(8,128)}), f32[32,4096]{1,0:T(8,128)}) %reduce-scatter.21.cloned.1.call-update) | async-done | bytes 524304 | tf_op jit(solution)/shard_map/reduce_scatter | solution.py:306
  1187.2 187.4 %reduce-scatter.23.cloned.1.call-done = f32[128,1024]{1,0:T(8,128)} async-done(((f32[4096,1024]{1,0:T(8,128)}), f32[128,1024]{1,0:T(8,128)}) %reduce-scatter.23.cloned.1.call-update) | async-done | bytes 524304 | tf_op jit(solution)/shard_map/reduce_scatter | solution.py:308
  (326 shorter events, 174.7 us)
Async XLA Ops:
  7.2 104.9 %all-gather.18.cloned.1.call-start = ((), (), s32[]{:S(2)}) async-start(), calls=%async_computation.8 | async-start | bytes 7077888 | tf_op jit(solution)/shard_map/all_gather | solution.py:261
  7.9 202.3 %all-gather.30.cloned.1.call-start = ((), (), s32[]{:S(2)}) async-start(), calls=%async_computation.14 | async-start | bytes 2621440 | tf_op jit(solution)/shard_map/all_gather | solution.py:77
  30.5 86.6 %copy-start.47 = (f32[8,1,128]{2,1,0:T(1,128)}, f32[8,1,128]{2,1,0:T(1,128)S(1)}, u32[]{:S(2)}) copy-start(f32[8,1,128]{2,1,0:T(1,128)S(1)} %convert_element_type.590) | copy-start | bytes 12292
  47.2 70.0 %copy-start.45 = (f32[8,1,128]{2,1,0:T(1,128)}, f32[8,1,128]{2,1,0:T(1,128)S(1)}, u32[]{:S(2)}) copy-start(f32[8,1,128]{2,1,0:T(1,128)S(1)} %convert_element_type.589) | copy-start | bytes 12292
  83.7 33.4 %copy-start.49 = (f32[256]{0:T(256)}, f32[256]{0:T(256)S(1)}, u32[]{:S(2)}) copy-start(f32[256]{0:T(256)S(1)} %get-tuple-element.98) | copy-start | bytes 3076
  83.7 33.4 %copy-start.55 = (f32[256]{0:T(256)}, f32[256]{0:T(256)S(1)}, u32[]{:S(2)}) copy-start(f32[256]{0:T(256)S(1)} %get-tuple-element.97) | copy-start | bytes 3076
  85.9 31.2 %copy-start.60 = (f32[256]{0:T(256)}, f32[256]{0:T(256)S(1)}, u32[]{:S(2)}) copy-start(f32[256]{0:T(256)S(1)} %fusion.122) | copy-start | bytes 3076
  122.4 51.1 %copy-start.83 = (bf16[128]{0:T(256)(128)(2,1)S(1)}, bf16[128]{0:T(256)(128)(2,1)}, u32[]{:S(2)}) copy-start(bf16[128]{0:T(256)(128)(2,1)} %param.27) | copy-start | bytes 772
  122.4 67.3 %copy-start.84 = (bf16[128]{0:T(256)(128)(2,1)S(1)}, bf16[128]{0:T(256)(128)(2,1)}, u32[]{:S(2)}) copy-start(bf16[128]{0:T(256)(128)(2,1)} %param.26) | copy-start | bytes 772
  122.5 91.7 %all-gather.32.cloned.1.call-start = ((), (), s32[]{:S(2)}) async-start(), calls=%async_computation.15 | async-start | bytes 2621440 | tf_op jit(solution)/shard_map/all_gather | solution.py:76
  124.6 93.5 %all-gather.20.cloned.1.call-start = ((), (), s32[]{:S(2)}) async-start(), calls=%async_computation.9 | async-start | bytes 2621440 | tf_op jit(solution)/shard_map/all_gather | solution.py:77
  125.2 96.8 %all-gather.22.cloned.1.call-start = ((), (), s32[]{:S(2)}) async-start(), calls=%async_computation.10 | async-start | bytes 2621440 | tf_op jit(solution)/shard_map/all_gather | solution.py:76
  127.4 141.5 %all-gather.24.cloned.1.call-start = ((), (), s32[]{:S(2)}) async-start(), calls=%async_computation.11 | async-start | bytes 2359296 | tf_op jit(solution)/shard_map/all_gather | solution.py:264
  128.0 266.5 %all-gather.26.cloned.1.call-start = ((), (), s32[]{:S(2)}) async-start(), calls=%async_computation.12 | async-start | bytes 9437184 | tf_op jit(solution)/shard_map/all_gather | solution.py:268
  128.7 391.0 %all-gather.28.cloned.1.call-start = ((), (), s32[]{:S(2)}) async-start(), calls=%async_computation.13 | async-start | bytes 9437184 | tf_op jit(solution)/shard_map/all_gather | solution.py:270
  129.5 532.3 %reduce-scatter.11.cloned.1.call-start = ((), (), s32[]{:S(2)}) async-start(), calls=%async_computation.17 | async-start | bytes 2621440 | tf_op jit(solution)/shard_map/reduce_scatter | solution.py:202
  271.6 278.3 %copy-start.58 = (f32[256]{0:T(256)}, f32[256]{0:T(256)S(1)}, u32[]{:S(2)}) copy-start(f32[256]{0:T(256)S(1)} %broadcast_multiply_fusion) | copy-start | bytes 3076
  291.5 258.4 %copy-start.67 = (f32[256]{0:T(256)}, f32[256]{0:T(256)S(1)}, u32[]{:S(2)}) copy-start(f32[256]{0:T(256)S(1)} %fusion.123) | copy-start | bytes 3076
  291.5 258.4 %copy-start.59 = (f32[256]{0:T(256)}, f32[256]{0:T(256)S(1)}, u32[]{:S(2)}) copy-start(f32[256]{0:T(256)S(1)} %fusion.121) | copy-start | bytes 3076
  568.7 93.1 %reduce-scatter.9.cloned.1.call-start = ((), (), s32[]{:S(2)}) async-start(), calls=%async_computation.16 | async-start | bytes 2621440 | tf_op jit(solution)/shard_map/reduce_scatter | solution.py:199
  599.3 70.3 %reduce-scatter.15.cloned.1.call-start = ((), (), s32[]{:S(2)}) async-start(), calls=%async_computation.19 | async-start | bytes 2621440 | tf_op jit(solution)/shard_map/reduce_scatter | solution.py:202
  612.1 88.4 %reduce-scatter.13.cloned.1.call-start = ((), (), s32[]{:S(2)}) async-start(), calls=%async_computation.18 | async-start | bytes 2621440 | tf_op jit(solution)/shard_map/reduce_scatter | solution.py:199
  642.2 202.3 %reduce-scatter.19.cloned.1.call-start = ((), (), s32[]{:S(2)}) async-start(), calls=%async_computation.21 | async-start | bytes 4325376 | tf_op jit(solution)/shard_map/reduce_scatter | solution.py:302
  646.9 355.3 %reduce-scatter.17.cloned.1.call-start = ((), (), s32[]{:S(2)}) async-start(), calls=%async_computation.20 | async-start | bytes 12976128 | tf_op jit(solution)/shard_map/reduce_scatter | solution.py:299
  654.7 45.8 %copy-start.35 = (bf16[16,64,256]{2,1,0:T(8,128)(2,1)}, bf16[16,64,256]{2,1,0:T(8,128)(2,1)S(1)}, u32[]{:S(2)}) copy-start(bf16[16,64,256]{2,1,0:T(8,128)(2,1)S(1)} %get-tuple-element.92) | copy-start | bytes 1572868
  661.8 38.7 %copy-start.56 = (f32[256]{0:T(256)S(1)}, f32[256]{0:T(256)}, u32[]{:S(2)}) copy-start(f32[256]{0:T(256)} %copy-done.55) | copy-start | bytes 3076
  661.8 38.7 %copy-start.61 = (f32[256]{0:T(256)S(1)}, f32[256]{0:T(256)}, u32[]{:S(2)}) copy-start(f32[256]{0:T(256)} %copy-done.60) | copy-start | bytes 3076
  712.1 475.2 %reduce-scatter.21.cloned.1.call-start = ((), (), s32[]{:S(2)}) async-start(), calls=%async_computation.22 | async-start | bytes 17301504 | tf_op jit(solution)/shard_map/reduce_scatter | solution.py:306
  727.1 647.6 %reduce-scatter.23.cloned.1.call-start = ((), (), s32[]{:S(2)}) async-start(), calls=%async_computation.23 | async-start | bytes 17301504 | tf_op jit(solution)/shard_map/reduce_scatter | solution.py:308
  791.7 45.1 %copy-start.13 = (bf16[2,1,256,1024]{3,2,1,0:T(8,128)(2,1)S(1)}, bf16[2,1,256,1024]{3,2,1,0:T(8,128)(2,1)}, u32[]{:S(2)}) copy-start(bf16[2,1,256,1024]{3,2,1,0:T(8,128)(2,1)} %param.17) | copy-start | bytes 3145732
  791.7 45.1 %copy-start.73 = (f32[256]{0:T(256)S(1)}, f32[256]{0:T(256)}, u32[]{:S(2)}) copy-start(f32[256]{0:T(256)} %copy-done.72) | copy-start | bytes 3076
  791.7 45.1 %copy-start.75 = (f32[256]{0:T(256)S(1)}, f32[256]{0:T(256)}, u32[]{:S(2)}) copy-start(f32[256]{0:T(256)} %copy-done.74) | copy-start | bytes 3076
  (75 other events, 669.8 us)
Sparse Core Ops, SparseCore 0:
  10.2 101.8 all-gather.17
  122.6 20.7 all-gather.29
  145.5 22.5 all-gather.31
  170.2 22.5 all-gather.19
  194.8 22.5 all-gather.21
  219.4 49.4 all-gather.23
  271.0 123.4 all-gather.25
  396.5 123.1 all-gather.27
  568.8 29.5 reduce-scatter.10
  601.0 31.4 reduce-scatter.8
  635.0 31.4 reduce-scatter.14
  669.0 31.4 reduce-scatter.12
  703.3 141.1 reduce-scatter.18
  851.0 151.2 reduce-scatter.16
  1005.1 182.1 reduce-scatter.20
  1190.1 184.5 reduce-scatter.22
where the time goes:
time: 1390 us; the launch traced here: 1380 us
  waiting for transfers between devices  837 us (60%)
  matrix products  225 us (16%)
  blocking collectives  211 us (15%)
  other arithmetic  50.9 us (4%)
  local copies, waits for them, and re-layouts  40 us (3%)
  between operations  15.4 us (1%)
    reduce_scatter x1, waiting for transfers between devices, local(): lax.psum_scatter(summed[11], ('fsdp', 'tok'), scatter_dimension=0, tiled=...  187 us
    reduce_scatter x1, waiting for transfers between devices, local(): lax.psum_scatter(summed[9], ('fsdp', 'tok'), scatter_dimension=0, tiled=T...  185 us
    reduce_scatter x1, waiting for transfers between devices, local(): lax.psum_scatter(summed[2], ('fsdp', 'tok'), scatter_dimension=0, tiled=T...  158 us
    all_gather x1, waiting for transfers between devices, local(): lax.all_gather(w_fc2, 'fsdp', axis=0, tiled=True)  113 us
    all_gather x1, waiting for transfers between devices, local(): lax.all_gather(w_fc1, 'fsdp', axis=0, tiled=True)  103 us
    unnamed x1, blocking collectives  38.2 us
    reduce_scatter x2, waiting for transfers between devices, backward(): lax.psum_scatter(part_key.astype(jnp.bfloat16), 'tok', scatter_dimension=...  30.8 us
    dot_general x2, matrix products, backward(): jnp.einsum('sqhd,skhd->shqk', grad_h, value_h, preferred_element_type=jnp...  27.9 us
  transfers between devices with their start and end apart: 16, of which 9 were waited for; matrix products, arithmetic and copies ran while one was open for 18% of the time, Pallas kernels for 0%

commit v1 on v0

v1 whole, which is shorter than its diff:
```python
import functools

import jax
import jax.numpy as jnp
from jax import lax
from jax.experimental import pallas as pl
from jax.experimental.pallas import tpu as pltpu
from jax.sharding import PartitionSpec as P

DH = 64
PAIR = 2 * DH
eps = 1e-05
masked_value = -1e30
f32 = jnp.float32
bf16 = jnp.bfloat16
AXES = ("fsdp", "tok")


class Grid:
    def __init__(self, n_fsdp, n_tok):
        self.n_fsdp, self.n_tok = n_fsdp, n_tok
        self.nz, self.ny = n_fsdp // 2, n_tok // 2
        self.f, self.t = lax.axis_index("fsdp"), lax.axis_index("tok")
        self.z, self.x = self.f // 2, self.f % 2
        self.y, self.c = self.t // 2, self.t % 2

    def send(self, value, place):
        pairs = []
        for f in range(self.n_fsdp):
            for t in range(self.n_tok):
                z, x, y, c = place(f // 2, f % 2, t // 2, t % 2)
                pairs.append((f * self.n_tok + t, (z * 2 + x) * self.n_tok + y * 2 + c))
        return lax.ppermute(value, AXES, pairs)

    def over_core(self, value):
        return self.send(value, lambda z, x, y, c: (z, x, y, 1 - c))

    def over_x(self, value):
        return self.send(value, lambda z, x, y, c: (z, 1 - x, y, c))

    def over_y(self, value):
        return self.send(value, lambda z, x, y, c: (z, x, 1 - y, c))

    def over_yc(self, value):
        return self.send(value, lambda z, x, y, c: (z, x, 1 - y, 1 - c))

    def over_z(self, value, shift):
        return self.send(value, lambda z, x, y, c: ((z + shift) % self.nz, x, y, c))


def pick(values, index, axis):
    return lax.dynamic_index_in_dim(values, index, axis, keepdims=False)


def both(a, b):
    return (a.astype(f32) + b.astype(f32)).astype(bf16)


def place_kernel(rows, offsets, *refs):
    pieces, out, sem = refs[:-2], refs[-2], refs[-1]
    copies = []
    at = 0
    for piece in pieces:
        for j in range(piece.shape[0]):
            first = pl.multiple_of(offsets[at], rows)
            copies.append(pltpu.make_async_copy(piece.at[j], out.at[pl.ds(first, rows)], sem.at[at]))
            at += 1
    for copy in copies:
        copy.start()
    for copy in copies:
        copy.wait()


def gather_weight(grid, shard):
    shard_rows, width = shard.shape
    rows = shard_rows // grid.n_tok
    if grid.nz != 4 or grid.ny != 2 or rows % 16:
        return lax.all_gather(shard, "fsdp", axis=0, tiled=True)
    own = lax.dynamic_slice_in_dim(shard, grid.t * rows, rows, 0)
    steps = [own] + [grid.over_z(own, k) for k in (1, 2, 3)]
    qa, qb = jnp.stack(steps[:2]), jnp.stack(steps[2:])
    xa, yb = grid.over_x(qa), grid.over_y(qb)
    ya, xb = grid.over_y(qa), grid.over_x(qb)
    xya, xyb = grid.over_y(xa), grid.over_x(yb)
    have = [
        (qa, 0, 0, 0), (qb, 2, 0, 0), (xa, 0, 1, 0), (yb, 2, 0, 1),
        (ya, 0, 0, 1), (xb, 2, 1, 0), (xya, 0, 1, 1), (xyb, 2, 1, 1),
    ]
    pieces, offsets = [], []
    for piece, k, dx, dy in have:
        for dc in (0, 1):
            pieces.append(grid.over_core(piece) if dc else piece)
            for j in range(2):
                z = (grid.z + 4 - k - j) % 4
                x, y, c = grid.x ^ dx, grid.y ^ dy, grid.c ^ dc
                offsets.append((z * 2 + x) * shard_rows + (y * 2 + c) * rows)
    total = grid.n_fsdp * shard_rows
    return pl.pallas_call(
        functools.partial(place_kernel, rows),
        out_shape=jax.ShapeDtypeStruct((total, width), shard.dtype),
        in_specs=[pl.BlockSpec(memory_space=pltpu.SMEM)]
        + [pl.BlockSpec(memory_space=pl.ANY)] * len(pieces),
        out_specs=pl.BlockSpec(memory_space=pltpu.VMEM),
        scratch_shapes=[pltpu.SemaphoreType.DMA((len(offsets),))],
        compiler_params=pltpu.CompilerParams(vmem_limit_bytes=20 * 2**20),
        cost_estimate=pl.CostEstimate(
            flops=0, bytes_accessed=4 * total * width, transcendentals=0
        ),
        name="place",
    )(jnp.stack(offsets).astype(jnp.int32), *pieces)


def gather_vectors(grid, packed):
    if grid.nz != 4:
        return lax.all_gather(packed, "fsdp", axis=0)
    whole = jnp.zeros((grid.n_fsdp,) + packed.shape, packed.dtype)
    whole = lax.dynamic_update_index_in_dim(whole, packed, grid.f, 0)
    whole = whole + grid.over_x(whole)
    whole = whole + grid.over_z(whole, 1)
    return whole + grid.over_z(whole, 2)


def scatter_grad(grid, grad):
    rows = grad.shape[0] // (grid.n_fsdp * grid.n_tok)
    if grid.nz != 4 or grid.ny != 2 or rows % 16:
        return lax.psum_scatter(grad.astype(f32), AXES, scatter_dimension=0, tiled=True)
    grad = grad.astype(bf16)
    width = grad.shape[1]
    parts = grad.reshape(4, 2, 2, 2, rows, width)
    z, x, y, c = grid.z, grid.x, grid.y, grid.c
    pa, pb = parts[:2], parts[2:]
    ha = both(pick(pa, c, 3), grid.over_core(pick(pa, 1 - c, 3)))
    hb = both(pick(pb, c, 3), grid.over_core(pick(pb, 1 - c, 3)))
    a1 = both(pick(ha, x, 1), grid.over_x(pick(ha, 1 - x, 1)))
    b1 = both(pick(hb, y, 2), grid.over_y(pick(hb, 1 - y, 2)))
    a2 = both(pick(a1, y, 1), grid.over_y(pick(a1, 1 - y, 1)))
    b2 = both(pick(b1, x, 1), grid.over_x(pick(b1, 1 - x, 1)))
    last = jnp.concatenate([a2, b2], axis=0)
    total = pick(last, z, 0).astype(f32)
    for shift in (1, 2, 3):
        total = total + grid.over_z(pick(last, (z + shift) % 4, 0), shift).astype(f32)
    return total


def sum_vectors(grid, packed):
    if grid.nz != 4 or grid.ny != 2:
        return lax.psum(packed, AXES)
    packed = packed + grid.over_core(packed)
    packed = packed + grid.over_x(packed)
    packed = packed + grid.over_y(packed)
    return packed + grid.over_z(packed, 1) + grid.over_z(packed, 2) + grid.over_z(packed, 3)


def layer_norm(values, gain, shift):
    mean = jnp.mean(values, axis=-1, keepdims=True)
    centered = values - mean
    spread = jnp.mean(centered * centered, axis=-1, keepdims=True)
    return centered * lax.rsqrt(spread + eps) * gain + shift


def norm_back(values, gain, shift, upstream):
    result, pull = jax.vjp(layer_norm, values, gain, shift)
    return pull(upstream)


def smooth_gate(values):
    return jax.nn.gelu(values, approximate=True)


def by_rows(a, b):
    return lax.dot_general(a, b, (((1,), (1,)), ((), ())), preferred_element_type=f32)


def by_columns(a, b):
    return lax.dot_general(a, b, (((0,), (0,)), ((), ())), preferred_element_type=f32)


def fill(info, own, other, whole, block):
    for j in range(2):
        rows = slice(j * block, (j + 1) * block)
        whole[pl.ds(pl.multiple_of(info[j] * block, block), block), :] = own[rows, :]
        whole[pl.ds(pl.multiple_of(info[2 + j] * block, block), block), :] = other[rows, :]


def head_part(values, h):
    lane = lax.broadcasted_iota(jnp.int32, values.shape, 1)
    return jnp.where(lane // DH == h, values, jnp.zeros_like(values))


def keep_mask(starts, index, first, keys, block):
    key_pos = lax.broadcasted_iota(jnp.int32, (keys, block), 0)
    query_pos = first + lax.broadcasted_iota(jnp.int32, (1, block), 1)
    start = starts[pl.ds(index, 1), :]
    return (key_pos >= start) & (key_pos <= query_pos)


def attend_kernel(block, info, starts, q, k, v, ko, vo, out, lse, kn, vn):
    fill(info, k, ko, kn, block)
    fill(info, v, vo, vn, block)

    def run(index, count):
        at = pl.ds(pl.multiple_of(index * block, block), block)
        keys, vals = kn[: count * block, :], vn[: count * block, :]
        query = q[at, :] * jnp.asarray(DH**-0.5, bf16)
        keep = keep_mask(starts, index, info[index] * block, count * block, block)
        sides = []
        for h in range(2):
            scores = jnp.where(keep, by_rows(keys, head_part(query, h)), masked_value)
            top = jnp.max(scores, axis=0, keepdims=True)
            expo = jnp.exp(scores - top)
            total = jnp.sum(expo, axis=0, keepdims=True)
            lse[0, pl.ds(2 * h + index, 1), :] = top + jnp.log(total)
            side = by_columns(vals, expo.astype(bf16)) / total
            sides.append(side[h * DH : (h + 1) * DH])
        out[at, :] = jnp.concatenate(sides, axis=0).T.astype(bf16)

    low = info[4]
    for index, counts in ((low, (1, 2)), (1 - low, (3, 4))):
        for count in counts:
            pl.when(info[index] == count - 1)(functools.partial(run, index, count))


def attend_back_kernel(
    block, info, starts, q, k, v, ko, vo, out, lse, grad, dq, dk, dv, dko, dvo, kn, vn, dkn, dvn
):
    fill(info, k, ko, kn, block)
    fill(info, v, vo, vn, block)
    dkn[...] = jnp.zeros_like(dkn)
    dvn[...] = jnp.zeros_like(dvn)

    def run(index, count):
        at = pl.ds(pl.multiple_of(index * block, block), block)
        keys, vals = kn[: count * block, :], vn[: count * block, :]
        query = q[at, :] * jnp.asarray(DH**-0.5, bf16)
        up = grad[at, :]
        product = (up.astype(f32) * out[at, :].astype(f32)).T
        keep = keep_mask(starts, index, info[index] * block, count * block, block)
        sides = []
        for h in range(2):
            query_h, up_h = head_part(query, h), head_part(up, h)
            inner = jnp.sum(product[h * DH : (h + 1) * DH], axis=0, keepdims=True)
            scores = jnp.where(keep, by_rows(keys, query_h), masked_value)
            probs = jnp.exp(scores - lse[0, pl.ds(2 * h + index, 1), :])
            grad_scores = (probs * (by_rows(vals, up_h) - inner)).astype(bf16)
            dvn[: count * block, :] += jnp.dot(
                probs.astype(bf16), up_h, preferred_element_type=f32
            )
            dkn[: count * block, :] += jnp.dot(grad_scores, query_h, preferred_element_type=f32)
            side = by_columns(keys, grad_scores) * DH**-0.5
            sides.append(side[h * DH : (h + 1) * DH])
        dq[at, :] = jnp.concatenate(sides, axis=0).T.astype(bf16)

    low = info[4]
    for index, counts in ((low, (1, 2)), (1 - low, (3, 4))):
        for count in counts:
            pl.when(info[index] == count - 1)(functools.partial(run, index, count))
    for j in range(2):
        rows = slice(j * block, (j + 1) * block)
        own = pl.ds(pl.multiple_of(info[j] * block, block), block)
        other = pl.ds(pl.multiple_of(info[2 + j] * block, block), block)
        dk[rows, :], dv[rows, :] = dkn[own, :], dvn[own, :]
        dko[rows, :], dvo[rows, :] = dkn[other, :].astype(bf16), dvn[other, :].astype(bf16)


def attend_specs(count, width):
    pairs = width // PAIR
    return [
        pl.BlockSpec(starts_shape, lambda h, info: (0, 0)) for starts_shape in ((2, count // 2),)
    ] + [
        pl.BlockSpec((count, PAIR), lambda h, info: (0, h)),
        pl.BlockSpec((count, PAIR), lambda h, info: (0, pairs + h)),
        pl.BlockSpec((count, PAIR), lambda h, info: (0, 2 * pairs + h)),
        pl.BlockSpec((count, PAIR), lambda h, info: (0, h)),
        pl.BlockSpec((count, PAIR), lambda h, info: (0, pairs + h)),
    ]


def attend(info, starts, mixed, other):
    count, width = mixed.shape[0], mixed.shape[1] // 3
    pairs, block = width // PAIR, count // 2
    column = pl.BlockSpec((count, PAIR), lambda h, info: (0, h))
    return pl.pallas_call(
        functools.partial(attend_kernel, block),
        out_shape=(
            jax.ShapeDtypeStruct((count, width), bf16),
            jax.ShapeDtypeStruct((pairs, 4, block), f32),
        ),
        grid_spec=pltpu.PrefetchScalarGridSpec(
            num_scalar_prefetch=1,
            grid=(pairs,),
            in_specs=attend_specs(count, width),
            out_specs=[column, pl.BlockSpec((1, 4, block), lambda h, info: (h, 0, 0))],
            scratch_shapes=[pltpu.VMEM((2 * count, PAIR), bf16)] * 2,
        ),
        compiler_params=pltpu.CompilerParams(vmem_limit_bytes=32 * 2**20),
        cost_estimate=pl.CostEstimate(
            flops=8 * count * count * width, bytes_accessed=12 * count * width,
            transcendentals=20 * count * count,
        ),
        name="attend",
    )(info, starts, mixed, mixed, mixed, other, other)


def attend_back(info, starts, mixed, other, attended, lse, grad):
    count, width = attended.shape
    pairs, block = width // PAIR, count // 2
    column = pl.BlockSpec((count, PAIR), lambda h, info: (0, h))
    return pl.pallas_call(
        functools.partial(attend_back_kernel, block),
        out_shape=tuple(
            jax.ShapeDtypeStruct((count, width), kind) for kind in (bf16, f32, f32, bf16, bf16)
        ),
        grid_spec=pltpu.PrefetchScalarGridSpec(
            num_scalar_prefetch=1,
            grid=(pairs,),
            in_specs=attend_specs(count, width)
            + [column, pl.BlockSpec((1, 4, block), lambda h, info: (h, 0, 0)), column],
            out_specs=[column] * 5,
            scratch_shapes=[pltpu.VMEM((2 * count, PAIR), bf16)] * 2
            + [pltpu.VMEM((2 * count, PAIR), f32)] * 2,
        ),
        compiler_params=pltpu.CompilerParams(vmem_limit_bytes=32 * 2**20),
        cost_estimate=pl.CostEstimate(
            flops=20 * count * count * width, bytes_accessed=28 * count * width,
            transcendentals=20 * count * count,
        ),
        name="attend_back",
    )(info, starts, mixed, mixed, mixed, other, other, attended, lse, grad)


def local(
    n_fsdp,
    n_tok,
    tokens,
    cotangent,
    doc_lengths,
    norm1_gain,
    norm1_shift,
    w_qkv,
    bias_query,
    bias_value,
    w_out,
    bias_out,
    norm2_gain,
    norm2_shift,
    w_fc1,
    bias_fc1,
    w_fc2,
    bias_fc2,
):
    grid = Grid(n_fsdp, n_tok)
    y, t = grid.y, grid.t
    block, width = tokens.shape[2:]
    hidden_width = w_fc1.shape[1]

    def swap(values):
        mine, theirs = pick(values, y, 0)[0], pick(values, 1 - y, 0)[0]
        return jnp.concatenate([mine, grid.over_yc(theirs)], axis=0)

    def swap_back(values):
        mine, back = values[:block], grid.over_yc(values[block:])
        first, second = jnp.where(y == 0, mine, back), jnp.where(y == 0, back, mine)
        return jnp.stack([first, second])[:, None]

    rows = swap(tokens)
    full_qkv = gather_weight(grid, w_qkv)
    vectors = (
        norm1_gain, norm1_shift, bias_query, bias_value, bias_out, norm2_gain, norm2_shift, bias_fc2
    )
    part = norm1_gain.shape[0]
    packed = jnp.concatenate([v[None] for v in vectors] + [bias_fc1.reshape(-1, part)], axis=0)
    packed = gather_vectors(grid, packed)
    gain1, shift1, b_query, b_value, b_out, gain2, shift2, b_fc2 = (
        packed[:, i].reshape(width).astype(f32) for i in range(8)
    )
    b_fc1 = packed[:, 8:].reshape(hidden_width).astype(f32)
    upstream = swap(cotangent)
    full_out = gather_weight(grid, w_out)
    full_fc1 = gather_weight(grid, w_fc1)
    full_fc2 = gather_weight(grid, w_fc2)

    mine, across = jnp.stack([t, 3 - t]), jnp.stack([t ^ 1, 3 - (t ^ 1)])
    info = jnp.concatenate([mine, across, y[None]]).astype(jnp.int32)
    lengths = pick(doc_lengths, y, 0)[0]
    ends = jnp.cumsum(lengths)
    place = mine[:, None] * block + jnp.arange(block, dtype=jnp.int32)[None]
    starts = jnp.max(
        jnp.where(place[..., None] >= ends, ends, 0), axis=-1
    ).astype(jnp.int32)

    inputs = rows.astype(f32)
    normed = layer_norm(inputs, gain1, shift1).astype(bf16)
    b_qkv = jnp.concatenate([b_query, jnp.zeros_like(b_query), b_value])
    mixed = (jnp.dot(normed, full_qkv, preferred_element_type=f32) + b_qkv).astype(bf16)
    other = grid.over_core(mixed[:, width:])
    attended, lse = attend(info, starts, mixed, other)
    middle = inputs + jnp.dot(attended, full_out, preferred_element_type=f32) + b_out
    normed2 = layer_norm(middle, gain2, shift2).astype(bf16)
    hidden = jnp.dot(normed2, full_fc1, preferred_element_type=f32) + b_fc1
    active = smooth_gate(hidden).astype(bf16)
    result = middle + jnp.dot(active, full_fc2, preferred_element_type=f32) + b_fc2
    output = swap_back(result.astype(bf16))

    def weight_grad(left, right):
        return lax.dot_general(
            left, right, (((0,), (0,)), ((), ())), preferred_element_type=f32
        ).astype(bf16)

    def back(left, weight):
        return lax.dot_general(
            left, weight, (((1,), (1,)), ((), ())), preferred_element_type=f32
        )

    grad_out = upstream.astype(f32)
    grad_fc2 = scatter_grad(grid, weight_grad(active, upstream))
    grad_bias_fc2 = jnp.sum(grad_out, axis=0)
    unused, gate_pull = jax.vjp(smooth_gate, hidden)
    grad_hidden = gate_pull(back(upstream, full_fc2))[0].astype(bf16)
    grad_fc1 = scatter_grad(grid, weight_grad(normed2, grad_hidden))
    grad_bias_fc1 = jnp.sum(grad_hidden.astype(f32), axis=0)
    grad_mid_norm, grad_gain2, grad_shift2 = norm_back(
        middle, gain2, shift2, back(grad_hidden, full_fc1)
    )
    grad_middle = grad_out + grad_mid_norm
    grad_branch = grad_middle.astype(bf16)
    grad_w_out = scatter_grad(grid, weight_grad(attended, grad_branch))
    grad_bias_out = jnp.sum(grad_branch.astype(f32), axis=0)
    grad_attended = back(grad_branch, full_out).astype(bf16)
    dq, dk, dv, dko, dvo = attend_back(
        info, starts, mixed, other, attended, lse, grad_attended
    )
    dk = (dk + grid.over_core(dko).astype(f32)).astype(bf16)
    dv = (dv + grid.over_core(dvo).astype(f32)).astype(bf16)
    grad_mixed = jnp.concatenate([dq, dk, dv], axis=1)
    grad_qkv = scatter_grad(grid, weight_grad(normed, grad_mixed))
    grad_bias_query = jnp.sum(dq.astype(f32), axis=0)
    grad_bias_value = jnp.sum(dv.astype(f32), axis=0)
    grad_in_norm, grad_gain1, grad_shift1 = norm_back(
        inputs, gain1, shift1, back(grad_mixed, full_qkv)
    )
    grad_tokens = swap_back((grad_middle + grad_in_norm).astype(bf16))

    sums = jnp.concatenate(
        [
            v.reshape(-1, width)
            for v in (
                grad_gain1, grad_shift1, grad_bias_query, grad_bias_value, grad_bias_out,
                grad_gain2, grad_shift2, grad_bias_fc2, grad_bias_fc1,
            )
        ],
        axis=0,
    )
    sums = sum_vectors(grid, sums)
    device, devices = grid.f * n_tok + t, n_fsdp * n_tok

    def owned(vector):
        count = vector.shape[0] // devices
        return lax.dynamic_slice_in_dim(vector, device * count, count, 0)

    return (
        output,
        grad_tokens,
        owned(sums[0]),
        owned(sums[1]),
        grad_qkv,
        owned(sums[2]),
        owned(sums[3]),
        grad_w_out,
        owned(sums[4]),
        owned(sums[5]),
        owned(sums[6]),
        grad_fc1,
        owned(sums[8:].reshape(hidden_width)),
        grad_fc2,
        owned(sums[7]),
    )


def solution(mesh):
    vector, matrix = P("fsdp"), P("fsdp", None)
    rows = P(None, "fsdp", "tok", None)
    own_vector, own_matrix = P(("fsdp", "tok")), P(("fsdp", "tok"), None)
    return jax.shard_map(
        functools.partial(local, mesh.shape["fsdp"], mesh.shape["tok"]),
        mesh=mesh,
        in_specs=(
            rows, rows, P(None, "fsdp", None), vector, vector, matrix, vector, vector,
            matrix, vector, vector, vector, matrix, vector, matrix, vector,
        ),
        out_specs=(
            rows, rows, own_vector, own_vector, own_matrix, own_vector, own_vector,
            own_matrix, own_vector, own_vector, own_vector, own_matrix, own_vector,
            own_matrix, own_vector,
        ),
        check_vma=False,
    )
```

time: 1390 us -> 629 us (0.45)
  waiting for transfers between devices: 837 us -> 241 us
  blocking collectives: 211 us -> 0 us
  matrix products: 225 us -> 84.1 us
  starting transfers between devices: 1.26 us -> 110 us
  Pallas kernels: 0 us -> 70.8 us
  local copies, waits for them, and re-layouts: 40 us -> 66.2 us
    reduce_scatter x8 -> x0, waiting for transfers between devices: 565 us -> none  [the longest x1 187 us: local(): lax.psum_scatter(summed[11], ('fsdp', 'tok'), scatter_dimension=0, tiled=...]
    all_gather x8 -> x0, waiting for transfers between devices: 269 us -> none  [the longest x1 113 us: local(): lax.all_gather(w_fc2, 'fsdp', axis=0, tiled=True)]
    ppermute x0 -> x120, waiting for transfers between devices: none -> 241 us  [send(): return lax.ppermute(value, AXES, pairs)]
    all_gather x9 -> x0, blocking collectives: 173 us -> none  [the longest x1 26 us: local(): lax.all_gather(bias_fc1, 'fsdp', axis=0, tiled=True)]
    dot_general x36 -> x12, matrix products: 225 us -> 84.1 us  [the longest x4 30.8 us: weight_grad(): lax.dot_general(left, right, (((0,), (0,)), ((), ())), preferred_element_...]
    ppermute x0 -> x120, starting transfers between devices: none -> 110 us  [send(): return lax.ppermute(value, AXES, pairs)]
    pallas_call x0 -> x6, Pallas kernels: none -> 70.8 us  [the longest x1 26 us: attend_back(): pl.pallas_call(functools.partial(attend_back_kernel, block), out_shape=tu...]
    unnamed x1 -> x0, blocking collectives: 38.2 us -> none
  transfers between devices with their start and end apart: 16 -> 120, of which waited for: 9 -> 42; matrix products, arithmetic and copies ran while one was open for 18% -> 20% of each run, Pallas kernels for 0% -> 11%
where the time goes in v1:
time: 629 us; the launch traced here: 622 us
  waiting for transfers between devices  241 us (38%)
  starting transfers between devices  110 us (17%)
  matrix products  84.1 us (13%)
  Pallas kernels  70.8 us (11%)
  local copies, waits for them, and re-layouts  66.2 us (11%)
  other arithmetic  47 us (7%)
    ppermute x120, waiting for transfers between devices, send(): return lax.ppermute(value, AXES, pairs)  241 us
    ppermute x120, starting transfers between devices, send(): return lax.ppermute(value, AXES, pairs)  110 us
    dot_general x4, matrix products, weight_grad(): lax.dot_general(left, right, (((0,), (0,)), ((), ())), preferred_element_...  30.8 us
    dot_general x4, matrix products, back(): lax.dot_general(left, weight, (((1,), (1,)), ((), ())), preferred_element...  29.3 us
    pallas_call x1, Pallas kernels, attend_back(): pl.pallas_call(functools.partial(attend_back_kernel, block), out_shape=tu...  26 us
    pallas_call x1, Pallas kernels, attend(): pl.pallas_call(functools.partial(attend_kernel, block), out_shape=(jax.Sh...  23.3 us
    unnamed x268, local copies, waits for them, and re-layouts  21.7 us
    pallas_call x4, Pallas kernels, gather_weight(): pl.pallas_call(functools.partial(place_kernel, rows), out_shape=jax.Shape...  21.5 us
  transfers between devices with their start and end apart: 120, of which 42 were waited for; matrix products, arithmetic and copies ran while one was open for 20% of the time, Pallas kernels for 11%

profile of v1, /device:TPU:0, one launch (start us, length us, event | category | flops | bytes accessed | tf_op | source)
XLA Modules:
  0.0 621.9 jit_solution(2260547183279977204)
XLA Ops:
  45.4 6.4 %collective-permute-done.6 = bf16[32,3072]{1,0:T(8,128)(2,1)} collective-permute-done((bf16[32,3072]{1,0:T(8,128)(2,1)}, bf16[32,3072]{1,0:T(8,128)(2,1)}, u32[]{:S(2)}, u32[]{:S(2)}) %collective-permute-start.6) | collective-permute-done | bytes 196640 | tf_op jit(solution)/shard_map/ppermute | solution.py:33
  52.5 10.1 %collective-permute-start.41 = (bf16[32,4096]{1,0:T(8,128)(2,1)S(1)}, bf16[32,4096]{1,0:T(8,128)(2,1)S(1)}, u32[]{:S(2)}, u32[]{:S(2)}) collective-permute-start(bf16[32,4096]{1,0:T(8,128)(2,1)S(1)} %constant_dynamic-slice_fusion.25), channel_id=1, source_target_pairs={{0,16},{1,17},{2,18},{3,19},{4,20},{5,21},{6,22},{7,23},{8,24},{9,... | collective-permute-start | bytes 786440 | tf_op jit(solution)/shard_map/ppermute | solution.py:33
  63.8 15.2 %collective-permute-done.58 = bf16[128,1024]{1,0:T(8,128)(2,1)S(1)} collective-permute-done((bf16[128,1024]{1,0:T(8,128)(2,1)S(1)}, bf16[128,1024]{1,0:T(8,128)(2,1)S(1)}, u32[]{:S(2)}, u32[]{:S(2)}) %collective-permute-start.58) | collective-permute-done | bytes 262176 | tf_op jit(solution)/shard_map/ppermute | solution.py:33
  80.2 9.2 %collective-permute-done.41 = bf16[32,4096]{1,0:T(8,128)(2,1)S(1)} collective-permute-done((bf16[32,4096]{1,0:T(8,128)(2,1)S(1)}, bf16[32,4096]{1,0:T(8,128)(2,1)S(1)}, u32[]{:S(2)}, u32[]{:S(2)}) %collective-permute-start.41) | collective-permute-done | bytes 262176 | tf_op jit(solution)/shard_map/ppermute | solution.py:33
  104.6 5.4 collective-permute-done.9.refs_4_
  111.2 7.7 %collective-permute-done.13.refs_8_ = bf16[2,32,3072]{2,1,0:T(8,128)(2,1)S(1)} collective-permute-done((bf16[2,32,3072]{2,1,0:T(8,128)(2,1)S(1)}, bf16[2,32,3072]{2,1,0:T(8,128)(2,1)S(1)}, u32[]{:S(2)}, u32[]{:S(2)}) %collective-permute-start.13) | collective-permute-done | bytes 393248 | tf_op jit(solution)/shard_map/ppermute | solution.py:33
  136.6 8.5 %collective-permute-done.65.refs_8_ = bf16[2,128,1024]{2,1,0:T(8,128)(2,1)} collective-permute-done((bf16[2,128,1024]{2,1,0:T(8,128)(2,1)S(1)}, bf16[2,128,1024]{2,1,0:T(8,128)(2,1)}, u32[]{:S(2)}, u32[]{:S(2)}) %collective-permute-start.65) | collective-permute-done | bytes 524320 | tf_op jit(solution)/shard_map/ppermute | solution.py:33
  145.7 6.2 collective-permute-done.17.refs_12_
  160.3 9.9 %place.4 = bf16[1024,3072]{1,0:T(8,128)(2,1)S(1)} custom-call(s32[32]{0:T(128)S(1)} %stack.406.offsets, bf16[2,32,3072]{2,1,0:T(8,128)(2,1)S(1)} %pad_maximum_fusion.9.refs_0_, bf16[2,32,3072]{2,1,0:T(8,128)(2,1)S(1)} %copy-done.40, bf16[2,32,3072]{2,1,0:T(8,128)(2,1)S(1)} %pad_maximum_fusion.10.refs_2_, bf16[2,32,3072]{2,1,0:T(8,128)(2,1)S(1)} %copy-done.42, ...), custom_call_target="tpu_custom_call" | custom-call | bytes 12582912 | tf_op jit(solution)/shard_map/place/pallas_call | solution.py:98
  173.9 8.9 %collective-permute-done.48.refs_8_ = bf16[2,32,4096]{2,1,0:T(8,128)(2,1)} collective-permute-done((bf16[2,32,4096]{2,1,0:T(8,128)(2,1)S(1)}, bf16[2,32,4096]{2,1,0:T(8,128)(2,1)}, u32[]{:S(2)}, u32[]{:S(2)}) %collective-permute-start.48) | collective-permute-done | bytes 524320 | tf_op jit(solution)/shard_map/ppermute | solution.py:33
  198.8 8.2 %collective-permute-done.52.refs_12_ = bf16[2,32,4096]{2,1,0:T(8,128)(2,1)} collective-permute-done((bf16[2,32,4096]{2,1,0:T(8,128)(2,1)S(1)}, bf16[2,32,4096]{2,1,0:T(8,128)(2,1)}, u32[]{:S(2)}, u32[]{:S(2)}) %collective-permute-start.52) | collective-permute-done | bytes 524320 | tf_op jit(solution)/shard_map/ppermute | solution.py:33
  229.4 23.3 %attend.1 = (bf16[512,1024]{1,0:T(8,128)(2,1)S(1)}, f32[8,4,256]{2,1,0:T(4,128)S(1)}) custom-call(s32[5]{0:T(128)S(1)} %concatenate.39.info, s32[2,256]{1,0:T(2,128)S(1)} %select_reduce_fusion.starts, bf16[512,3072]{1,0:T(8,128)(2,1)S(1)} %add_convert_fusion.q.k.v, bf16[512,3072]{1,0:T(8,128)(2,1)S(1)} %add_convert_fusion.q.k.v, ...), custom_call_target="tpu_custom_call" | custom-call | flops 2147483648 | bytes 6291456 | tf_op jit(solution)/shard_map/attend/pallas_call | solution.py:282
  256.3 7.2 %fusion.103 = f32[512,4096]{1,0:T(8,128)} fusion(bf16[1024,4096]{1,0:T(8,128)(2,1)S(1)} %place.6, f32[512,1024]{1,0:T(8,128)S(1)} %get-tuple-element.135, f32[1024]{0:T(1024)S(1)} %bitcast.421, f32[1024]{0:T(1024)S(1)} %bitcast.414, f32[512]{0:T(512)S(1)} %fusion.87, f32[512]{0:T(512)S(1)} %broadcast_multiply_fusion), kind=kOutput, calls=%fused_computation.297 | convolution fusion | flops 4297588736 | bytes 18886656 | tf_op jit(solution)/shard_map/dot_general | solution.py:399
  264.3 13.5 %convert_reduce_fusion = (f32[4096]{0:T(1024)S(1)}, bf16[512,4096]{1,0:T(8,128)(2,1)}) fusion(f32[512,4096]{1,0:T(8,128)} %fusion.103, f32[4096]{0:T(1024)S(1)} %convert.37, bf16[4096,1024]{1,0:T(8,128)(2,1)S(1)} %place.7, bf16[256,1024]{1,0:T(8,128)(2,1)} %copy-done.95, bf16[256,1024]{1,0:T(8,128)(2,1)S(1)} %copy-done.89), kind=kOutput, calls=%fused_computation.9 | convolution fusion | flops 4345294848 | bytes 22052864 | tf_op jit(solution)/shard_map/dot_general | solution.py:410
  277.8 9.7 %multiply_reduce_fusion = (f32[1024]{0:T(1024)}, f32[512]{0:T(512)S(1)}, f32[1024]{0:T(1024)}, f32[512,1024]{1,0:T(8,128)}) fusion(f32[512,1024]{1,0:T(8,128)} %copy-done.87, f32[512]{0:T(512)S(1)} %fusion.87, f32[512]{0:T(512)S(1)} %broadcast_multiply_fusion, f32[1024]{0:T(1024)S(1)} %bitcast.415, bf16[512,4096]{1,0:T(8,128)(2,1)} %get-tuple-element.139, ...), kind=kOutput, calls=%fused_computation.63 | convolution fusion | flops 4299159040 | bytes 16795648 | tf_op jit(solution)/shard_map/dot_general | solution.py:410
  296.8 9.7 %convolution_convert_fusion.1 = bf16[1024,4096]{1,0:T(8,128)(2,1)} fusion(bf16[512,4096]{1,0:T(8,128)(2,1)} %get-tuple-element.139, f32[512,1024]{1,0:T(8,128)S(1)} %copy-done.88, f32[1024]{0:T(1024)S(1)} %bitcast.422, f32[1024]{0:T(1024)S(1)} %bitcast.417, f32[512]{0:T(512)S(1)} %fusion.87, f32[512]{0:T(512)S(1)} %broadcast_multiply_fusion), kind=kOutput, calls=%fused_computation.12 | convolution fusion | flops 4301783040 | bytes 14692352 | tf_op jit(solution)/shard_map/dot_general | solution.py:405
  306.5 9.0 %add_convert_fusion.4 = bf16[512,1024]{1,0:T(8,128)(2,1)S(1)} fusion(f32[512,1024]{1,0:T(8,128)S(1)} %copy-done.88, bf16[4096,1024]{1,0:T(8,128)(2,1)S(1)} %place.7, f32[1024]{0:T(1024)S(1)} %bitcast.420, f32[512,4096]{1,0:T(8,128)} %fusion.103, f32[4096]{0:T(1024)S(1)} %convert.37), kind=kOutput, calls=%fused_computation.71 | convolution fusion | flops 4317511680 | bytes 19943424 | tf_op jit(solution)/shard_map/dot_general | solution.py:401
  317.7 26.0 %attend_back.1 = (bf16[512,1024]{1,0:T(8,128)(2,1)S(1)}, f32[512,1024]{1,0:T(8,128)S(1)}, f32[512,1024]{1,0:T(8,128)S(1)}, bf16[512,1024]{1,0:T(8,128)(2,1)}, bf16[512,1024]{1,0:T(8,128)(2,1)}) custom-call(s32[5]{0:T(128)S(1)} %concatenate.39.info, s32[2,256]{1,0:T(2,128)S(1)} %select_reduce_fusion.starts, bf16[512,3072]{1,0:T(8,128)(2,1)S(1)} %add_convert_fusion.q.k.v, ...), custom_call_target="tpu_custom_call" | custom-call | flops 5368709120 | bytes 14680064 | tf_op jit(solution)/shard_map/attend_back/pallas_call | solution.py:308
  353.8 13.1 %convolution_convert_fusion = bf16[4096,1024]{1,0:T(8,128)(2,1)} fusion(bf16[256,1024]{1,0:T(8,128)(2,1)S(1)} %copy-done.97, bf16[256,1024]{1,0:T(8,128)(2,1)S(1)} %copy-done.90, f32[512,4096]{1,0:T(8,128)} %fusion.103, f32[4096]{0:T(1024)S(1)} %copy-done.121), kind=kOutput, calls=%fused_computation.11 | convolution fusion | flops 4322230272 | bytes 17842176 | tf_op jit(solution)/shard_map/dot_general | solution.py:405
  391.4 5.4 collective-permute-done.94
  397.5 6.9 %collective-permute-done.97 = bf16[2,2,32,1024]{3,2,0,1:T(8,128)(2,1)S(1)} collective-permute-done((bf16[2,2,32,1024]{3,2,0,1:T(8,128)(2,1)S(1)}, bf16[2,2,32,1024]{3,2,0,1:T(8,128)(2,1)S(1)}, u32[]{:S(2)}, u32[]{:S(2)}) %collective-permute-start.97) | collective-permute-done | bytes 262176 | tf_op jit(solution)/shard_map/ppermute | solution.py:33
  433.6 5.4 convolution_convert_fusion.2
  456.5 10.7 %collective-permute-done.77 = bf16[256,1024]{1,0:T(8,128)(2,1)S(1)} collective-permute-done((bf16[256,1024]{1,0:T(8,128)(2,1)S(1)}, bf16[256,1024]{1,0:T(8,128)(2,1)S(1)}, u32[]{:S(2)}, u32[]{:S(2)}) %collective-permute-start.77) | collective-permute-done | bytes 524320 | tf_op jit(solution)/shard_map/ppermute | solution.py:33
  484.6 13.2 %collective-permute-done.103 = bf16[2,2,32,4096]{3,2,0,1:T(8,128)(2,1)S(1)} collective-permute-done((bf16[2,2,32,4096]{3,2,0,1:T(8,128)(2,1)S(1)}, bf16[2,2,32,4096]{3,2,0,1:T(8,128)(2,1)S(1)}, u32[]{:S(2)}, u32[]{:S(2)}) %collective-permute-start.103) | collective-permute-done | bytes 1048608 | tf_op jit(solution)/shard_map/ppermute | solution.py:33
  503.2 17.0 %collective-permute-done.112 = bf16[2,2,128,1024]{3,2,0,1:T(8,128)(2,1)S(1)} collective-permute-done((bf16[2,2,128,1024]{3,2,0,1:T(8,128)(2,1)S(1)}, bf16[2,2,128,1024]{3,2,0,1:T(8,128)(2,1)S(1)}, u32[]{:S(2)}, u32[]{:S(2)}) %collective-permute-start.112) | collective-permute-done | bytes 1048608 | tf_op jit(solution)/shard_map/ppermute | solution.py:33
  525.8 11.3 %collective-permute-done.85 = bf16[2,2,32,3072]{3,2,0,1:T(8,128)(2,1)S(1)} collective-permute-done((bf16[2,2,32,3072]{3,2,0,1:T(8,128)(2,1)S(1)}, bf16[2,2,32,3072]{3,2,0,1:T(8,128)(2,1)S(1)}, u32[]{:S(2)}, u32[]{:S(2)}) %collective-permute-start.85) | collective-permute-done | bytes 786464 | tf_op jit(solution)/shard_map/ppermute | solution.py:33
  542.5 9.9 %collective-permute-done.104 = bf16[2,32,4096]{2,1,0:T(8,128)(2,1)S(1)} collective-permute-done((bf16[2,32,4096]{2,1,0:T(8,128)(2,1)S(1)}, bf16[2,32,4096]{2,1,0:T(8,128)(2,1)S(1)}, u32[]{:S(2)}, u32[]{:S(2)}) %collective-permute-start.104) | collective-permute-done | bytes 524320 | tf_op jit(solution)/shard_map/ppermute | solution.py:33
  554.9 8.7 %collective-permute-done.113 = bf16[2,128,1024]{2,1,0:T(8,128)(2,1)S(1)} collective-permute-done((bf16[2,128,1024]{2,1,0:T(8,128)(2,1)S(1)}, bf16[2,128,1024]{2,1,0:T(8,128)(2,1)S(1)}, u32[]{:S(2)}, u32[]{:S(2)}) %collective-permute-start.113) | collective-permute-done | bytes 524320 | tf_op jit(solution)/shard_map/ppermute | solution.py:33
  565.4 5.3 collective-permute-done.86
  574.1 15.8 %collective-permute-done.109 = bf16[32,4096]{1,0:T(8,128)(2,1)S(1)} collective-permute-done((bf16[32,4096]{1,0:T(8,128)(2,1)S(1)}, bf16[32,4096]{1,0:T(8,128)(2,1)S(1)}, u32[]{:S(2)}, u32[]{:S(2)}) %collective-permute-start.109) | collective-permute-done | bytes 262176 | tf_op jit(solution)/shard_map/ppermute | solution.py:33
  595.9 11.2 %collective-permute-start.90 = (bf16[32,3072]{1,0:T(8,128)(2,1)S(1)}, bf16[32,3072]{1,0:T(8,128)(2,1)S(1)}, u32[]{:S(2)}, u32[]{:S(2)}) collective-permute-start(bf16[32,3072]{1,0:T(8,128)(2,1)S(1)} %get-tuple-element.112), channel_id=1, source_target_pairs={{0,8},{1,9},{2,10},{3,11},{4,12},{5,13},{6,14},{7,15},{8,16},{9,17... | collective-permute-start | bytes 589832 | tf_op jit(solution)/shard_map/ppermute | solution.py:33
  613.3 7.3 %collective-permute-done.91 = bf16[32,3072]{1,0:T(8,128)(2,1)S(1)} collective-permute-done((bf16[32,3072]{1,0:T(8,128)(2,1)S(1)}, bf16[32,3072]{1,0:T(8,128)(2,1)S(1)}, u32[]{:S(2)}, u32[]{:S(2)}) %collective-permute-start.91) | collective-permute-done | bytes 196640 | tf_op jit(solution)/shard_map/ppermute | solution.py:33
  (633 shorter events, 283.2 us)
Async XLA Ops:
  42.4 36.6 %collective-permute-start.58 = (bf16[128,1024]{1,0:T(8,128)(2,1)S(1)}, bf16[128,1024]{1,0:T(8,128)(2,1)S(1)}, u32[]{:S(2)}, u32[]{:S(2)}) collective-permute-start(bf16[128,1024]{1,0:T(8,128)(2,1)S(1)} %constant_dynamic-slice_fusion.24), channel_id=1, source_target_pairs={{0,16},{1,17},{2,18},{3,19},{4,20},{5,21},{6,22},{7,23},{8,24},{9,... | collective-permute-start | bytes 786440 | tf_op jit(solution)/shard_map/ppermute | solution.py:33
  43.5 35.5 %collective-permute-start.39 = (bf16[32,4096]{1,0:T(8,128)(2,1)S(1)}, bf16[32,4096]{1,0:T(8,128)(2,1)S(1)}, u32[]{:S(2)}, u32[]{:S(2)}) collective-permute-start(bf16[32,4096]{1,0:T(8,128)(2,1)S(1)} %constant_dynamic-slice_fusion.25), channel_id=1, source_target_pairs={{0,8},{1,9},{2,10},{3,11},{4,12},{5,13},{6,14},{7,15},{8,16},{9,17... | collective-permute-start | bytes 786440 | tf_op jit(solution)/shard_map/ppermute | solution.py:33
  51.8 27.9 %collective-permute-start.42 = (bf16[32,4096]{1,0:T(8,128)(2,1)S(1)}, bf16[32,4096]{1,0:T(8,128)(2,1)}, u32[]{:S(2)}, u32[]{:S(2)}) collective-permute-start(bf16[32,4096]{1,0:T(8,128)(2,1)S(1)} %constant_dynamic-slice_fusion.25), channel_id=1, source_target_pairs={{0,24},{1,25},{2,26},{3,27},{4,28},{5,29},{6,30},{7,31},{8,0},{9,1... | collective-permute-start | bytes 786440 | tf_op jit(solution)/shard_map/ppermute | solution.py:33
  52.5 36.9 %collective-permute-start.41 = (bf16[32,4096]{1,0:T(8,128)(2,1)S(1)}, bf16[32,4096]{1,0:T(8,128)(2,1)S(1)}, u32[]{:S(2)}, u32[]{:S(2)}) collective-permute-start(bf16[32,4096]{1,0:T(8,128)(2,1)S(1)} %constant_dynamic-slice_fusion.25), channel_id=1, source_target_pairs={{0,16},{1,17},{2,18},{3,19},{4,20},{5,21},{6,22},{7,23},{8,24},{9,... | collective-permute-start | bytes 786440 | tf_op jit(solution)/shard_map/ppermute | solution.py:33
  63.7 35.7 %collective-permute-start = (bf16[256,1024]{1,0:T(8,128)(2,1)S(1)}, bf16[256,1024]{1,0:T(8,128)(2,1)}, u32[]{:S(2)}, u32[]{:S(2)}) collective-permute-start(bf16[256,1024]{1,0:T(8,128)(2,1)S(1)} %get-tuple-element.111), channel_id=1, source_target_pairs={{0,3},{1,2},{2,1},{3,0},{4,7},{5,6},{6,5},{7,4},{8,11},{9,10},{10,... | collective-permute-start | bytes 1572872 | tf_op jit(solution)/shard_map/ppermute | solution.py:33
  157.2 25.6 %collective-permute-start.48 = (bf16[2,32,4096]{2,1,0:T(8,128)(2,1)S(1)}, bf16[2,32,4096]{2,1,0:T(8,128)(2,1)}, u32[]{:S(2)}, u32[]{:S(2)}) collective-permute-start(bf16[2,32,4096]{2,1,0:T(8,128)(2,1)S(1)} %pad_maximum_fusion.5.refs_0_), channel_id=1, source_target_pairs={{0,2},{1,3},{2,0},{3,1},{4,6},{5,7},{6,4},{7,5},{8,10},{9,11},{10,... | collective-permute-start | bytes 1572872 | tf_op jit(solution)/shard_map/ppermute | solution.py:33
  190.0 39.4 %collective-permute-start.21 = (bf16[512,2048]{1,0:T(8,128)(2,1)}, bf16[512,2048]{1,0:T(8,128)(2,1)}, u32[]{:S(2)}, u32[]{:S(2)}) collective-permute-start(bf16[512,2048]{1,0:T(8,128)(2,1)} %slice.160), channel_id=1, source_target_pairs={{0,1},{1,0},{2,3},{3,2},{4,5},{5,4},{6,7},{7,6},{8,9},{9,8},{10,11... | collective-permute-start | bytes 6291464 | tf_op jit(solution)/shard_map/ppermute | solution.py:33
  225.2 38.3 %collective-permute-start.74 = (bf16[256,1024]{1,0:T(8,128)(2,1)S(1)}, bf16[256,1024]{1,0:T(8,128)(2,1)S(1)}, u32[]{:S(2)}, u32[]{:S(2)}) collective-permute-start(bf16[256,1024]{1,0:T(8,128)(2,1)S(1)} %get-tuple-element.109), channel_id=1, source_target_pairs={{0,3},{1,2},{2,1},{3,0},{4,7},{5,6},{6,5},{7,4},{8,11},{9,10},{10,... | collective-permute-start | bytes 1572872 | tf_op jit(solution)/shard_map/ppermute | solution.py:33
  316.4 70.4 %collective-permute-start.73 = (bf16[256,1024]{1,0:T(8,128)(2,1)}, bf16[256,1024]{1,0:T(8,128)(2,1)}, u32[]{:S(2)}, u32[]{:S(2)}) collective-permute-start(bf16[256,1024]{1,0:T(8,128)(2,1)} %slice.167), channel_id=1, source_target_pairs={{0,3},{1,2},{2,1},{3,0},{4,7},{5,6},{6,5},{7,4},{8,11},{9,10},{10,... | collective-permute-start | bytes 1572872 | tf_op jit(solution)/shard_map/ppermute | solution.py:33
  347.3 68.4 %collective-permute-start.76 = (bf16[512,1024]{1,0:T(8,128)(2,1)}, bf16[512,1024]{1,0:T(8,128)(2,1)}, u32[]{:S(2)}, u32[]{:S(2)}) collective-permute-start(bf16[512,1024]{1,0:T(8,128)(2,1)} %get-tuple-element.28), channel_id=1, source_target_pairs={{0,1},{1,0},{2,3},{3,2},{4,5},{5,4},{6,7},{7,6},{8,9},{9,8},{10,11... | collective-permute-start | bytes 3145736 | tf_op jit(solution)/shard_map/ppermute | solution.py:33
  347.3 70.3 %collective-permute-start.75 = (bf16[512,1024]{1,0:T(8,128)(2,1)}, bf16[512,1024]{1,0:T(8,128)(2,1)}, u32[]{:S(2)}, u32[]{:S(2)}) collective-permute-start(bf16[512,1024]{1,0:T(8,128)(2,1)} %get-tuple-element.26), channel_id=1, source_target_pairs={{0,1},{1,0},{2,3},{3,2},{4,5},{5,4},{6,7},{7,6},{8,9},{9,8},{10,11... | collective-permute-start | bytes 3145736 | tf_op jit(solution)/shard_map/ppermute | solution.py:33
  351.7 33.1 %collective-permute-start.93 = (bf16[2,2,2,32,1024]{4,3,0,2,1:T(8,128)(2,1)}, bf16[2,2,2,32,1024]{4,3,0,2,1:T(8,128)(2,1)}, u32[]{:S(2)}, u32[]{:S(2)}) collective-permute-start(bf16[2,2,2,32,1024]{4,3,0,2,1:T(8,128)(2,1)} %bitcast.375), channel_id=1, source_target_pairs={{0,1},{1,0},{2,3},{3,2},{4,5},{5,4},{6,7},{7,6},{8,9},{9,8},{10,11... | collective-permute-start | bytes 1572872 | tf_op jit(solution)/shard_map/ppermute | solution.py:33
  352.6 35.6 %collective-permute-start.96 = (bf16[2,2,2,32,1024]{4,3,0,1,2:T(8,128)(2,1)}, bf16[2,2,2,32,1024]{4,3,0,1,2:T(8,128)(2,1)}, u32[]{:S(2)}, u32[]{:S(2)}) collective-permute-start(bf16[2,2,2,32,1024]{4,3,0,1,2:T(8,128)(2,1)} %bitcast.374), channel_id=1, source_target_pairs={{0,1},{1,0},{2,3},{3,2},{4,5},{5,4},{6,7},{7,6},{8,9},{9,8},{10,11... | collective-permute-start | bytes 1572872 | tf_op jit(solution)/shard_map/ppermute | solution.py:33
  384.9 83.5 %collective-permute-start.102 = (bf16[2,2,2,32,4096]{4,3,0,2,1:T(8,128)(2,1)}, bf16[2,2,2,32,4096]{4,3,0,2,1:T(8,128)(2,1)}, u32[]{:S(2)}, u32[]{:S(2)}) collective-permute-start(bf16[2,2,2,32,4096]{4,3,0,2,1:T(8,128)(2,1)} %bitcast.371), channel_id=1, source_target_pairs={{0,1},{1,0},{2,3},{3,2},{4,5},{5,4},{6,7},{7,6},{8,9},{9,8},{10,11... | collective-permute-start | bytes 6291464 | tf_op jit(solution)/shard_map/ppermute | solution.py:33
  386.8 84.9 %collective-permute-start.105 = (bf16[2,2,2,32,4096]{4,3,0,1,2:T(8,128)(2,1)}, bf16[2,2,2,32,4096]{4,3,0,1,2:T(8,128)(2,1)}, u32[]{:S(2)}, u32[]{:S(2)}) collective-permute-start(bf16[2,2,2,32,4096]{4,3,0,1,2:T(8,128)(2,1)} %bitcast.370), channel_id=1, source_target_pairs={{0,1},{1,0},{2,3},{3,2},{4,5},{5,4},{6,7},{7,6},{8,9},{9,8},{10,11... | collective-permute-start | bytes 6291464 | tf_op jit(solution)/shard_map/ppermute | solution.py:33
  452.3 26.1 %collective-permute-start.114 = (bf16[2,2,2,128,1024]{4,3,0,1,2:T(8,128)(2,1)S(1)}, bf16[2,2,2,128,1024]{4,3,0,1,2:T(8,128)(2,1)S(1)}, u32[]{:S(2)}, u32[]{:S(2)}) collective-permute-start(bf16[2,2,2,128,1024]{4,3,0,1,2:T(8,128)(2,1)S(1)} %bitcast.387), channel_id=1, source_target_pairs={{0,1},{1,0},{2,3},{3,2},{4,5},{5,4},{6,7},{7,6},{8,9},{9,8},{10,11... | collective-permute-start | bytes 6291464 | tf_op jit(solution)/shard_map/ppermute | solution.py:33
  471.7 26.1 %collective-permute-start.103 = (bf16[2,2,32,4096]{3,2,0,1:T(8,128)(2,1)S(1)}, bf16[2,2,32,4096]{3,2,0,1:T(8,128)(2,1)S(1)}, u32[]{:S(2)}, u32[]{:S(2)}) collective-permute-start(bf16[2,2,32,4096]{3,2,0,1:T(8,128)(2,1)S(1)} %dynamic-slice_bitcast_fusion.3), channel_id=1, source_target_pairs={{0,4},{1,5},{2,6},{3,7},{4,0},{5,1},{6,2},{7,3},{8,12},{9,13},{10,... | collective-permute-start | bytes 3145736 | tf_op jit(solution)/shard_map/ppermute | solution.py:33
  475.7 26.1 %collective-permute-start.106 = (bf16[2,2,32,4096]{3,2,0,1:T(8,128)(2,1)S(1)}, bf16[2,2,32,4096]{3,2,0,1:T(8,128)(2,1)S(1)}, u32[]{:S(2)}, u32[]{:S(2)}) collective-permute-start(bf16[2,2,32,4096]{3,2,0,1:T(8,128)(2,1)S(1)} %dynamic-slice_bitcast_fusion.2), channel_id=1, source_target_pairs={{0,2},{1,3},{2,0},{3,1},{4,6},{5,7},{6,4},{7,5},{8,10},{9,11},{10,... | collective-permute-start | bytes 3145736 | tf_op jit(solution)/shard_map/ppermute | solution.py:33
  478.3 41.9 %collective-permute-start.112 = (bf16[2,2,128,1024]{3,2,0,1:T(8,128)(2,1)S(1)}, bf16[2,2,128,1024]{3,2,0,1:T(8,128)(2,1)S(1)}, u32[]{:S(2)}, u32[]{:S(2)}) collective-permute-start(bf16[2,2,128,1024]{3,2,0,1:T(8,128)(2,1)S(1)} %dynamic-slice_bitcast_fusion.1), channel_id=1, source_target_pairs={{0,4},{1,5},{2,6},{3,7},{4,0},{5,1},{6,2},{7,3},{8,12},{9,13},{10,... | collective-permute-start | bytes 3145736 | tf_op jit(solution)/shard_map/ppermute | solution.py:33
  480.9 43.4 %collective-permute-start.115 = (bf16[2,2,128,1024]{3,2,0,1:T(8,128)(2,1)S(1)}, bf16[2,2,128,1024]{3,2,0,1:T(8,128)(2,1)S(1)}, u32[]{:S(2)}, u32[]{:S(2)}) collective-permute-start(bf16[2,2,128,1024]{3,2,0,1:T(8,128)(2,1)S(1)} %dynamic-slice_bitcast_fusion), channel_id=1, source_target_pairs={{0,2},{1,3},{2,0},{3,1},{4,6},{5,7},{6,4},{7,5},{8,10},{9,11},{10,... | collective-permute-start | bytes 3145736 | tf_op jit(solution)/shard_map/ppermute | solution.py:33
  482.8 54.4 %collective-permute-start.85 = (bf16[2,2,32,3072]{3,2,0,1:T(8,128)(2,1)S(1)}, bf16[2,2,32,3072]{3,2,0,1:T(8,128)(2,1)S(1)}, u32[]{:S(2)}, u32[]{:S(2)}) collective-permute-start(bf16[2,2,32,3072]{3,2,0,1:T(8,128)(2,1)S(1)} %dynamic-slice_bitcast_fusion.5), channel_id=1, source_target_pairs={{0,4},{1,5},{2,6},{3,7},{4,0},{5,1},{6,2},{7,3},{8,12},{9,13},{10,... | collective-permute-start | bytes 2359304 | tf_op jit(solution)/shard_map/ppermute | solution.py:33
  497.8 43.4 %collective-permute-start.88 = (bf16[2,2,32,3072]{3,2,0,1:T(8,128)(2,1)S(1)}, bf16[2,2,32,3072]{3,2,0,1:T(8,128)(2,1)S(1)}, u32[]{:S(2)}, u32[]{:S(2)}) collective-permute-start(bf16[2,2,32,3072]{3,2,0,1:T(8,128)(2,1)S(1)} %dynamic-slice_bitcast_fusion.4), channel_id=1, source_target_pairs={{0,2},{1,3},{2,0},{3,1},{4,6},{5,7},{6,4},{7,5},{8,10},{9,11},{10,... | collective-permute-start | bytes 2359304 | tf_op jit(solution)/shard_map/ppermute | solution.py:33
  501.9 50.6 %collective-permute-start.104 = (bf16[2,32,4096]{2,1,0:T(8,128)(2,1)S(1)}, bf16[2,32,4096]{2,1,0:T(8,128)(2,1)S(1)}, u32[]{:S(2)}, u32[]{:S(2)}) collective-permute-start(bf16[2,32,4096]{2,1,0:T(8,128)(2,1)S(1)} %dynamic-slice_bitcast_fusion.9), channel_id=1, source_target_pairs={{0,2},{1,3},{2,0},{3,1},{4,6},{5,7},{6,4},{7,5},{8,10},{9,11},{10,... | collective-permute-start | bytes 1572872 | tf_op jit(solution)/shard_map/ppermute | solution.py:33
  520.3 33.7 %collective-permute-start.107 = (bf16[2,32,4096]{2,1,0:T(8,128)(2,1)S(1)}, bf16[2,32,4096]{2,1,0:T(8,128)(2,1)S(1)}, u32[]{:S(2)}, u32[]{:S(2)}) collective-permute-start(bf16[2,32,4096]{2,1,0:T(8,128)(2,1)S(1)} %dynamic-slice_bitcast_fusion.8), channel_id=1, source_target_pairs={{0,4},{1,5},{2,6},{3,7},{4,0},{5,1},{6,2},{7,3},{8,12},{9,13},{10,... | collective-permute-start | bytes 1572872 | tf_op jit(solution)/shard_map/ppermute | solution.py:33
  524.3 39.3 %collective-permute-start.113 = (bf16[2,128,1024]{2,1,0:T(8,128)(2,1)S(1)}, bf16[2,128,1024]{2,1,0:T(8,128)(2,1)S(1)}, u32[]{:S(2)}, u32[]{:S(2)}) collective-permute-start(bf16[2,128,1024]{2,1,0:T(8,128)(2,1)S(1)} %dynamic-slice_bitcast_fusion.7), channel_id=1, source_target_pairs={{0,2},{1,3},{2,0},{3,1},{4,6},{5,7},{6,4},{7,5},{8,10},{9,11},{10,... | collective-permute-start | bytes 1572872 | tf_op jit(solution)/shard_map/ppermute | solution.py:33
  537.1 27.4 %collective-permute-start.116 = (bf16[2,128,1024]{2,1,0:T(8,128)(2,1)S(1)}, bf16[2,128,1024]{2,1,0:T(8,128)(2,1)S(1)}, u32[]{:S(2)}, u32[]{:S(2)}) collective-permute-start(bf16[2,128,1024]{2,1,0:T(8,128)(2,1)S(1)} %dynamic-slice_bitcast_fusion.6), channel_id=1, source_target_pairs={{0,4},{1,5},{2,6},{3,7},{4,0},{5,1},{6,2},{7,3},{8,12},{9,13},{10,... | collective-permute-start | bytes 1572872 | tf_op jit(solution)/shard_map/ppermute | solution.py:33
  541.2 29.6 %collective-permute-start.86 = (bf16[2,32,3072]{2,1,0:T(8,128)(2,1)S(1)}, bf16[2,32,3072]{2,1,0:T(8,128)(2,1)S(1)}, u32[]{:S(2)}, u32[]{:S(2)}) collective-permute-start(bf16[2,32,3072]{2,1,0:T(8,128)(2,1)S(1)} %dynamic-slice_bitcast_fusion.15), channel_id=1, source_target_pairs={{0,2},{1,3},{2,0},{3,1},{4,6},{5,7},{6,4},{7,5},{8,10},{9,11},{10,... | collective-permute-start | bytes 1179656 | tf_op jit(solution)/shard_map/ppermute | solution.py:33
  563.6 26.2 %collective-permute-start.109 = (bf16[32,4096]{1,0:T(8,128)(2,1)S(1)}, bf16[32,4096]{1,0:T(8,128)(2,1)S(1)}, u32[]{:S(2)}, u32[]{:S(2)}) collective-permute-start(bf16[32,4096]{1,0:T(8,128)(2,1)S(1)} %get-tuple-element.100), channel_id=1, source_target_pairs={{0,16},{1,17},{2,18},{3,19},{4,20},{5,21},{6,22},{7,23},{8,24},{9,... | collective-permute-start | bytes 786440 | tf_op jit(solution)/shard_map/ppermute | solution.py:33
  564.5 25.3 %collective-permute-start.108 = (bf16[32,4096]{1,0:T(8,128)(2,1)S(1)}, bf16[32,4096]{1,0:T(8,128)(2,1)S(1)}, u32[]{:S(2)}, u32[]{:S(2)}) collective-permute-start(bf16[32,4096]{1,0:T(8,128)(2,1)S(1)} %get-tuple-element.99), channel_id=1, source_target_pairs={{0,8},{1,9},{2,10},{3,11},{4,12},{5,13},{6,14},{7,15},{8,16},{9,17... | collective-permute-start | bytes 786440 | tf_op jit(solution)/shard_map/ppermute | solution.py:33
  572.2 40.0 %collective-permute-start.118 = (bf16[128,1024]{1,0:T(8,128)(2,1)S(1)}, bf16[128,1024]{1,0:T(8,128)(2,1)S(1)}, u32[]{:S(2)}, u32[]{:S(2)}) collective-permute-start(bf16[128,1024]{1,0:T(8,128)(2,1)S(1)} %get-tuple-element.97), channel_id=1, source_target_pairs={{0,16},{1,17},{2,18},{3,19},{4,20},{5,21},{6,22},{7,23},{8,24},{9,... | collective-permute-start | bytes 786440 | tf_op jit(solution)/shard_map/ppermute | solution.py:33
  572.7 39.5 %collective-permute-start.117 = (bf16[128,1024]{1,0:T(8,128)(2,1)S(1)}, bf16[128,1024]{1,0:T(8,128)(2,1)S(1)}, u32[]{:S(2)}, u32[]{:S(2)}) collective-permute-start(bf16[128,1024]{1,0:T(8,128)(2,1)S(1)} %get-tuple-element.96), channel_id=1, source_target_pairs={{0,8},{1,9},{2,10},{3,11},{4,12},{5,13},{6,14},{7,15},{8,16},{9,17... | collective-permute-start | bytes 786440 | tf_op jit(solution)/shard_map/ppermute | solution.py:33
  589.9 30.7 %collective-permute-start.91 = (bf16[32,3072]{1,0:T(8,128)(2,1)S(1)}, bf16[32,3072]{1,0:T(8,128)(2,1)S(1)}, u32[]{:S(2)}, u32[]{:S(2)}) collective-permute-start(bf16[32,3072]{1,0:T(8,128)(2,1)S(1)} %get-tuple-element.113), channel_id=1, source_target_pairs={{0,16},{1,17},{2,18},{3,19},{4,20},{5,21},{6,22},{7,23},{8,24},{9,... | collective-permute-start | bytes 589832 | tf_op jit(solution)/shard_map/ppermute | solution.py:33
  (221 other events, 2754.4 us)

commit v2 on v1

v2 whole, which is shorter than its diff:
```python
import functools

import jax
import jax.numpy as jnp
from jax import lax
from jax.experimental import pallas as pl
from jax.experimental.pallas import tpu as pltpu
from jax.sharding import PartitionSpec as P

DH = 64
PAIR = 2 * DH
eps = 1e-05
masked_value = -1e30
f32 = jnp.float32
bf16 = jnp.bfloat16
AXES = ("fsdp", "tok")


class Grid:
    def __init__(self, n_fsdp, n_tok):
        self.n_fsdp, self.n_tok = n_fsdp, n_tok
        self.nz, self.ny = n_fsdp // 2, n_tok // 2
        self.f, self.t = lax.axis_index("fsdp"), lax.axis_index("tok")
        self.z, self.x = self.f // 2, self.f % 2
        self.y, self.c = self.t // 2, self.t % 2

    def staged(self, rows):
        return self.nz == 4 and self.ny == 2 and rows % 16 == 0

    def send(self, value, place):
        pairs = []
        for f in range(self.n_fsdp):
            for t in range(self.n_tok):
                z, x, y, c = place(f // 2, f % 2, t // 2, t % 2)
                pairs.append((f * self.n_tok + t, (z * 2 + x) * self.n_tok + y * 2 + c))
        return lax.ppermute(value, AXES, pairs)

    def over_core(self, value):
        return self.send(value, lambda z, x, y, c: (z, x, y, 1 - c))

    def over_x(self, value):
        return self.send(value, lambda z, x, y, c: (z, 1 - x, y, c))

    def over_y(self, value):
        return self.send(value, lambda z, x, y, c: (z, x, 1 - y, c))

    def over_yc(self, value):
        return self.send(value, lambda z, x, y, c: (z, x, 1 - y, 1 - c))

    def flip_z(self, value, bit):
        return self.send(value, lambda z, x, y, c: (z ^ bit, x, y, c))

    def over_z(self, value, shift):
        return self.send(value, lambda z, x, y, c: ((z + shift) % self.nz, x, y, c))


def pick(values, index, axis):
    return lax.dynamic_index_in_dim(values, index, axis, keepdims=False)


def both(a, b):
    return (a.astype(f32) + b.astype(f32)).astype(bf16)


def halves(a, b, index):
    keep, send = index, 1 - index
    return both(pick(a, keep, 0), pick(b, keep, 0)), both(pick(a, send, 0), pick(b, send, 0))


def place_kernel(rows, widths, offsets, *refs):
    sem, outs, pieces = refs[-1], refs[-1 - len(widths) : -1], refs[: -1 - len(widths)]
    copies = []
    at = 0
    for piece in pieces:
        for j in range(piece.shape[0]):
            first = pl.multiple_of(offsets[at], rows)
            column = 0
            for i, width in enumerate(widths):
                copies.append(
                    pltpu.make_async_copy(
                        piece.at[j, :, pl.ds(column, width)],
                        outs[i].at[pl.ds(first, rows)],
                        sem.at[at * len(widths) + i],
                    )
                )
                column += width
            at += 1
    for copy in copies:
        copy.start()
    for copy in copies:
        copy.wait()


class Gather:
    def __init__(self, grid, *shards):
        self.grid, self.shards = grid, shards
        self.rows = shards[0].shape[0] // grid.n_tok
        self.staged = grid.staged(self.rows)
        self.state = {"shards": list(shards)}
        self.flip = True

    def own(self):
        parts = [
            lax.dynamic_slice_in_dim(w, self.grid.t * self.rows, self.rows, 0)
            for w in self.state["shards"]
        ]
        return jnp.concatenate(parts, axis=1)

    def along_z(self):
        if self.staged:
            own = self.own()
            self.flip = False
            self.state = {"steps": [own] + [self.grid.over_z(own, k) for k in (1, 2, 3)]}

    def near_z(self):
        if self.staged:
            own = self.own()
            self.state = {"steps": [own, self.grid.flip_z(own, 1)]}

    def far_z(self):
        if self.staged:
            two = jnp.stack(self.state["steps"])
            self.state = {"steps": [two, self.grid.flip_z(two, 2)]}

    def first(self):
        if self.staged:
            grid, steps = self.grid, self.state["steps"]
            q = jnp.concatenate(steps) if self.flip else jnp.stack(steps)
            self.state = {
                "q": q, "x": grid.over_x(q), "y": grid.over_y(q), "cq": grid.over_core(q)
            }

    def second(self):
        if self.staged:
            state, grid = self.state, self.grid
            state["a"], state["b"] = grid.over_y(state["x"][:2]), grid.over_x(state["y"][2:])
            state["cxy"] = grid.over_core(jnp.concatenate([state["x"], state["y"]]))

    def last(self):
        if self.staged:
            state = self.state
            state["cab"] = self.grid.over_core(jnp.concatenate([state["a"], state["b"]]))

    def place(self):
        if not self.staged:
            return [lax.all_gather(w, "fsdp", axis=0, tiled=True) for w in self.state["shards"]]
        grid, rows = self.grid, self.rows
        shard_rows, kind = self.shards[0].shape[0], self.shards[0].dtype
        widths = [w.shape[1] for w in self.shards]
        at = lambda dx, dy: [(k, dx, dy) for k in range(4)]
        ab = at(1, 1)
        order = (
            ("q", at(0, 0), 0), ("x", at(1, 0), 0), ("y", at(0, 1), 0), ("a", ab[:2], 0),
            ("b", ab[2:], 0), ("cq", at(0, 0), 1), ("cxy", at(1, 0) + at(0, 1), 1), ("cab", ab, 1),
        )
        offsets = []
        for name, places, dc in order:
            for k, dx, dy in places:
                z = grid.z ^ k if self.flip else (grid.z + 4 - k) % 4
                x, y, c = grid.x ^ dx, grid.y ^ dy, grid.c ^ dc
                offsets.append((z * 2 + x) * shard_rows + (y * 2 + c) * rows)
        total = grid.n_fsdp * shard_rows
        return pl.pallas_call(
            functools.partial(place_kernel, rows, widths),
            out_shape=[jax.ShapeDtypeStruct((total, width), kind) for width in widths],
            in_specs=[pl.BlockSpec(memory_space=pltpu.SMEM)]
            + [pl.BlockSpec(memory_space=pl.ANY)] * len(order),
            out_specs=[pl.BlockSpec(memory_space=pltpu.VMEM)] * len(widths),
            scratch_shapes=[pltpu.SemaphoreType.DMA((len(offsets) * len(widths),))],
            compiler_params=pltpu.CompilerParams(vmem_limit_bytes=24 * 2**20),
            cost_estimate=pl.CostEstimate(
                flops=0, bytes_accessed=4 * total * sum(widths), transcendentals=0
            ),
            name="place",
        )(jnp.stack(offsets).astype(jnp.int32), *(self.state[name] for name, *_ in order))


class GatherVectors:
    def __init__(self, grid, packed):
        self.grid, self.staged = grid, grid.nz == 4
        self.state = packed

    def over_x(self):
        if not self.staged:
            self.state = lax.all_gather(self.state, "fsdp", axis=0)
            return
        whole = jnp.zeros((self.grid.n_fsdp,) + self.state.shape, self.state.dtype)
        whole = lax.dynamic_update_index_in_dim(whole, self.state, self.grid.f, 0)
        self.state = whole + self.grid.over_x(whole)

    def over_z(self, bit):
        if self.staged:
            self.state = self.state + self.grid.flip_z(self.state, bit)


def split_kernel(rows, core, left, right, own, other):
    total = by_columns(left[...], right[...]).astype(bf16)
    first = core[0] == 0

    def put(order):
        for x in range(2):
            for y in range(2):
                at = (x * 2 + y) * 2 * rows
                low, high = total[at : at + rows], total[at + rows : at + 2 * rows]
                i, j = (x, y) if order else (y, x)
                own[0, i, j, 0] = jnp.where(first, low, high)
                other[0, i, j, 0] = jnp.where(first, high, low)

    z = pl.program_id(1)
    pl.when(z < 2)(lambda: put(True))
    pl.when(z >= 2)(lambda: put(False))


class Scatter:
    def __init__(self, grid, left, right):
        self.grid = grid
        count, height, width = left.shape + right.shape[1:]
        rows = height // (grid.n_fsdp * grid.n_tok)
        self.staged = grid.staged(rows)
        if not self.staged:
            self.state = by_columns(left, right)
            return
        tile = min(width, 2**18 // (8 * rows))
        part = jax.ShapeDtypeStruct((2, 2, 2, 2, rows, width), bf16)
        block = pl.BlockSpec(
            (1, 2, 2, 1, rows, tile), lambda n, z, core: (z // 2, 0, 0, z % 2, 0, n)
        )
        self.state = pl.pallas_call(
            functools.partial(split_kernel, rows),
            out_shape=(part, part),
            grid_spec=pltpu.PrefetchScalarGridSpec(
                num_scalar_prefetch=1,
                grid=(width // tile, 4),
                in_specs=[
                    pl.BlockSpec((count, 8 * rows), lambda n, z, core: (0, z)),
                    pl.BlockSpec((count, tile), lambda n, z, core: (0, n)),
                ],
                out_specs=[block, block],
            ),
            compiler_params=pltpu.CompilerParams(vmem_limit_bytes=32 * 2**20),
            cost_estimate=pl.CostEstimate(
                flops=2 * count * height * width,
                bytes_accessed=2 * (height * width + count * (height + width)),
                transcendentals=0,
            ),
            name="grad_split",
        )(grid.c[None].astype(jnp.int32), left, right)

    def core(self):
        if self.staged:
            own, other = self.state
            self.state = (own, self.grid.over_core(other))

    def first(self):
        if self.staged:
            grid, (own, more) = self.grid, self.state
            ka, sa = halves(own[0], more[0], grid.x)
            kb, sb = halves(own[1], more[1], grid.y)
            self.state = (ka, grid.over_x(sa), kb, grid.over_y(sb))

    def second(self):
        if self.staged:
            grid, (ka, ma, kb, mb) = self.grid, self.state
            ka, sa = halves(ka, ma, grid.y)
            kb, sb = halves(kb, mb, grid.x)
            self.state = (ka, grid.over_y(sa), kb, grid.over_x(sb))

    def far_z(self):
        if self.staged:
            low, (ka, ma, kb, mb) = self.grid.z < 2, self.state
            a, b = both(ka, ma), both(kb, mb)
            self.state = (jnp.where(low, a, b), self.grid.flip_z(jnp.where(low, b, a), 2))

    def near_z(self):
        if self.staged:
            keep, send = halves(*self.state, self.grid.z % 2)
            self.state = (keep, self.grid.flip_z(send, 1))

    def along_z(self):
        if self.staged:
            z, (ka, ma, kb, mb) = self.grid.z, self.state
            last = jnp.concatenate([both(ka, ma), both(kb, mb)])
            self.state = (pick(last, z, 0),) + tuple(
                self.grid.over_z(pick(last, (z + shift) % 4, 0), shift) for shift in (1, 2, 3)
            )

    def result(self):
        if not self.staged:
            return lax.psum_scatter(self.state, AXES, scatter_dimension=0, tiled=True)
        total = self.state[0].astype(f32)
        for more in self.state[1:]:
            total = total + more.astype(f32)
        return total


class SumVectors:
    def __init__(self, grid, packed):
        self.grid, self.staged = grid, grid.nz == 4 and grid.ny == 2
        self.state = packed if self.staged else lax.psum(packed, AXES)

    def add(self, over):
        if self.staged:
            self.state = self.state + over(self.state)


def layer_norm(values, gain, shift):
    mean = jnp.mean(values, axis=-1, keepdims=True)
    centered = values - mean
    spread = jnp.mean(centered * centered, axis=-1, keepdims=True)
    return centered * lax.rsqrt(spread + eps) * gain + shift


def norm_back(values, gain, shift, upstream):
    result, pull = jax.vjp(layer_norm, values, gain, shift)
    return pull(upstream)


def smooth_gate(values):
    return jax.nn.gelu(values, approximate=True)


def by_rows(a, b):
    return lax.dot_general(a, b, (((1,), (1,)), ((), ())), preferred_element_type=f32)


def by_columns(a, b):
    return lax.dot_general(a, b, (((0,), (0,)), ((), ())), preferred_element_type=f32)


def fill(info, own, other, whole, block):
    for j in range(2):
        rows = slice(j * block, (j + 1) * block)
        whole[pl.ds(pl.multiple_of(info[j] * block, block), block), :] = own[rows, :]
        whole[pl.ds(pl.multiple_of(info[2 + j] * block, block), block), :] = other[rows, :]


def head_part(values, h):
    lane = lax.broadcasted_iota(jnp.int32, values.shape, 1)
    return jnp.where(lane // DH == h, values, jnp.zeros_like(values))


def keep_mask(starts, index, first, keys, block):
    key_pos = lax.broadcasted_iota(jnp.int32, (keys, block), 0)
    query_pos = first + lax.broadcasted_iota(jnp.int32, (1, block), 1)
    start = starts[pl.ds(index, 1), :]
    return (key_pos >= start) & (key_pos <= query_pos)


def attend_kernel(block, info, starts, q, k, v, ko, vo, out, lse, kn, vn):
    fill(info, k, ko, kn, block)
    fill(info, v, vo, vn, block)

    def run(index, count):
        at = pl.ds(pl.multiple_of(index * block, block), block)
        keys, vals = kn[: count * block, :], vn[: count * block, :]
        query = q[at, :] * jnp.asarray(DH**-0.5, bf16)
        keep = keep_mask(starts, index, info[index] * block, count * block, block)
        sides = []
        for h in range(2):
            scores = jnp.where(keep, by_rows(keys, head_part(query, h)), masked_value)
            top = jnp.max(scores, axis=0, keepdims=True)
            expo = jnp.exp(scores - top)
            total = jnp.sum(expo, axis=0, keepdims=True)
            lse[0, pl.ds(2 * h + index, 1), :] = top + jnp.log(total)
            side = by_columns(vals, expo.astype(bf16)) / total
            sides.append(side[h * DH : (h + 1) * DH])
        out[at, :] = jnp.concatenate(sides, axis=0).T.astype(bf16)

    low = info[4]
    for index, counts in ((low, (1, 2)), (1 - low, (3, 4))):
        for count in counts:
            pl.when(info[index] == count - 1)(functools.partial(run, index, count))


def attend_back_kernel(
    block, info, starts, q, k, v, ko, vo, out, lse, grad, dq, dkv, dkvo, kn, vn, dkn, dvn
):
    fill(info, k, ko, kn, block)
    fill(info, v, vo, vn, block)
    dkn[...] = jnp.zeros_like(dkn)
    dvn[...] = jnp.zeros_like(dvn)

    def run(index, count):
        at = pl.ds(pl.multiple_of(index * block, block), block)
        keys, vals = kn[: count * block, :], vn[: count * block, :]
        query = q[at, :] * jnp.asarray(DH**-0.5, bf16)
        up = grad[at, :]
        product = (up.astype(f32) * out[at, :].astype(f32)).T
        keep = keep_mask(starts, index, info[index] * block, count * block, block)
        sides = []
        for h in range(2):
            query_h, up_h = head_part(query, h), head_part(up, h)
            inner = jnp.sum(product[h * DH : (h + 1) * DH], axis=0, keepdims=True)
            scores = jnp.where(keep, by_rows(keys, query_h), masked_value)
            probs = jnp.exp(scores - lse[0, pl.ds(2 * h + index, 1), :])
            grad_scores = (probs * (by_rows(vals, up_h) - inner)).astype(bf16)
            dvn[: count * block, :] += jnp.dot(
                probs.astype(bf16), up_h, preferred_element_type=f32
            )
            dkn[: count * block, :] += jnp.dot(grad_scores, query_h, preferred_element_type=f32)
            side = by_columns(keys, grad_scores) * DH**-0.5
            sides.append(side[h * DH : (h + 1) * DH])
        dq[at, :] = jnp.concatenate(sides, axis=0).T.astype(bf16)

    low = info[4]
    for index, counts in ((low, (1, 2)), (1 - low, (3, 4))):
        for count in counts:
            pl.when(info[index] == count - 1)(functools.partial(run, index, count))
    for j in range(2):
        rows = slice(j * block, (j + 1) * block)
        own = pl.ds(pl.multiple_of(info[j] * block, block), block)
        other = pl.ds(pl.multiple_of(info[2 + j] * block, block), block)
        for i, whole in enumerate((dkn, dvn)):
            dkv[i, rows, :] = whole[own, :]
            dkvo[i, rows, :] = whole[other, :].astype(bf16)


def attend_specs(count, width, at):
    pairs = width // PAIR
    return [
        pl.BlockSpec((2, count // 2), lambda h, info: (0, 0)),
        pl.BlockSpec((count, PAIR), lambda h, info: (0, at + h)),
        pl.BlockSpec((count, PAIR), lambda h, info: (0, pairs + at + h)),
        pl.BlockSpec((count, PAIR), lambda h, info: (0, 2 * pairs + at + h)),
        pl.BlockSpec((count, PAIR), lambda h, info: (0, at + h)),
        pl.BlockSpec((count, PAIR), lambda h, info: (0, pairs + at + h)),
    ]


def attend(info, starts, mixed, other, part, parts):
    count, width = mixed.shape[0], mixed.shape[1] // 3
    pairs, block = width // PAIR // parts, count // 2
    column = pl.BlockSpec((count, PAIR), lambda h, info: (0, h))
    return pl.pallas_call(
        functools.partial(attend_kernel, block),
        out_shape=(
            jax.ShapeDtypeStruct((count, width // parts), bf16),
            jax.ShapeDtypeStruct((pairs, 4, block), f32),
        ),
        grid_spec=pltpu.PrefetchScalarGridSpec(
            num_scalar_prefetch=1,
            grid=(pairs,),
            in_specs=attend_specs(count, width, part * pairs),
            out_specs=[column, pl.BlockSpec((1, 4, block), lambda h, info: (h, 0, 0))],
            scratch_shapes=[pltpu.VMEM((2 * count, PAIR), bf16)] * 2,
        ),
        compiler_params=pltpu.CompilerParams(vmem_limit_bytes=32 * 2**20),
        cost_estimate=pl.CostEstimate(
            flops=8 * count * count * width // parts, bytes_accessed=12 * count * width // parts,
            transcendentals=20 * count * count // parts,
        ),
        name="attend",
    )(info, starts, mixed, mixed, mixed, other, other)


def attend_back(info, starts, mixed, other, attended, lse, grad, part, parts):
    count, width = grad.shape
    pairs, block = width // PAIR // parts, count // 2
    column = pl.BlockSpec((count, PAIR), lambda h, info: (0, h))
    return pl.pallas_call(
        functools.partial(attend_back_kernel, block),
        out_shape=(
            jax.ShapeDtypeStruct((count, width // parts), bf16),
            jax.ShapeDtypeStruct((2, count, width // parts), f32),
            jax.ShapeDtypeStruct((2, count, width // parts), bf16),
        ),
        grid_spec=pltpu.PrefetchScalarGridSpec(
            num_scalar_prefetch=1,
            grid=(pairs,),
            in_specs=attend_specs(count, width, part * pairs)
            + [
                column,
                pl.BlockSpec((1, 4, block), lambda h, info: (h, 0, 0)),
                pl.BlockSpec((count, PAIR), lambda h, info: (0, part * pairs + h)),
            ],
            out_specs=[column] + [pl.BlockSpec((2, count, PAIR), lambda h, info: (0, 0, h))] * 2,
            scratch_shapes=[pltpu.VMEM((2 * count, PAIR), bf16)] * 2
            + [pltpu.VMEM((2 * count, PAIR), f32)] * 2,
        ),
        compiler_params=pltpu.CompilerParams(vmem_limit_bytes=32 * 2**20),
        cost_estimate=pl.CostEstimate(
            flops=20 * count * count * width // parts, bytes_accessed=28 * count * width // parts,
            transcendentals=20 * count * count // parts,
        ),
        name="attend_back",
    )(info, starts, mixed, mixed, mixed, other, other, attended, lse, grad)


def local(
    n_fsdp,
    n_tok,
    tokens,
    cotangent,
    doc_lengths,
    norm1_gain,
    norm1_shift,
    w_qkv,
    bias_query,
    bias_value,
    w_out,
    bias_out,
    norm2_gain,
    norm2_shift,
    w_fc1,
    bias_fc1,
    w_fc2,
    bias_fc2,
):
    grid = Grid(n_fsdp, n_tok)
    y, t = grid.y, grid.t
    block, width = tokens.shape[2:]
    hidden_width = w_fc1.shape[1]

    def swap(values):
        mine, theirs = pick(values, y, 0)[0], pick(values, 1 - y, 0)[0]
        return jnp.concatenate([mine, grid.over_yc(theirs)], axis=0)

    def swap_back(values):
        mine, back = values[:block], grid.over_yc(values[block:])
        first, second = jnp.where(y == 0, mine, back), jnp.where(y == 0, back, mine)
        return jnp.stack([first, second])[:, None]

    live = {}
    kinds = (Gather, Scatter, GatherVectors, SumVectors)

    def step(*names):
        moving = [live[n].state if isinstance(live[n], kinds) else live[n] for n in names]
        for name, value in zip(names, lax.optimization_barrier(moving)):
            if isinstance(live[name], kinds):
                live[name].state = value
            else:
                live[name] = value

    vectors = (
        norm1_gain, norm1_shift, bias_query, bias_value, bias_out, norm2_gain, norm2_shift, bias_fc2
    )
    part = norm1_gain.shape[0]
    packed = jnp.concatenate([v[None] for v in vectors] + [bias_fc1.reshape(-1, part)], axis=0)
    w1, w2, w3, small = (
        Gather(grid, w_qkv), Gather(grid, w_out, w_fc1), Gather(grid, w_fc2), GatherVectors(grid, packed)
    )
    live.update(w1=w1, w2=w2, w3=w3, small=small)

    mine, across = jnp.stack([t, 3 - t]), jnp.stack([t ^ 1, 3 - (t ^ 1)])
    info = jnp.concatenate([mine, across, y[None]]).astype(jnp.int32)
    lengths = pick(doc_lengths, y, 0)[0]
    ends = jnp.cumsum(lengths)
    place = mine[:, None] * block + jnp.arange(block, dtype=jnp.int32)[None]
    starts = jnp.max(
        jnp.where(place[..., None] >= ends, ends, 0), axis=-1
    ).astype(jnp.int32)

    w1.along_z()
    live["rows"] = swap(tokens)
    small.over_x()
    step("w1", "rows", "small", "w2")
    w1.first()
    w2.near_z()
    small.over_z(1)
    step("w1", "w2", "small")
    w1.second()
    w2.far_z()
    small.over_z(2)
    step("w1", "small", "w3")
    w1.last()
    w3.near_z()
    live["up"] = swap(cotangent)
    packed = small.state
    gain1, shift1, b_query, b_value, b_out, gain2, shift2, b_fc2 = (
        packed[:, i].reshape(width).astype(f32) for i in range(8)
    )
    b_fc1 = packed[:, 8:].reshape(hidden_width).astype(f32)
    inputs = live["rows"].astype(f32)
    live["normed"] = layer_norm(inputs, gain1, shift1).astype(bf16)
    step("w1", "w2", "w3", "normed", "up")
    w2.first()
    (full_qkv,) = w1.place()
    b_qkv = jnp.concatenate([b_query, jnp.zeros_like(b_query), b_value])
    normed = live["normed"]
    live["mixed"] = (jnp.dot(normed, full_qkv, preferred_element_type=f32) + b_qkv).astype(bf16)
    step("mixed", "w3")
    w3.far_z()
    live["other"] = grid.over_core(live["mixed"][:, width:])
    step("mixed", "other")
    low, low_lse = attend(info, starts, live["mixed"], live["other"], 0, 2)
    live["low"] = low
    step("low", "other", "mixed", "w2")
    w2.second()
    high, high_lse = attend(info, starts, live["mixed"], live["other"], 1, 2)
    live["high"] = high
    step("high", "w2", "w3")
    w2.last()
    w3.first()
    attended = jnp.concatenate([live["low"], live["high"]], axis=1)
    live["attended"] = attended
    step("w2", "attended")
    attended = live["attended"]
    full_out, full_fc1 = w2.place()
    middle = inputs + jnp.dot(attended, full_out, preferred_element_type=f32) + b_out
    live["middle"] = middle
    live["normed2"] = layer_norm(middle, gain2, shift2).astype(bf16)
    live["hidden"] = jnp.dot(live["normed2"], full_fc1, preferred_element_type=f32) + b_fc1
    step("hidden", "normed2", "middle", "w3")
    w3.second()
    normed2, middle, upstream = live["normed2"], live["middle"], live["up"]
    live["active"] = smooth_gate(live["hidden"]).astype(bf16)
    live["fc2"] = Scatter(grid, live["active"], upstream)
    step("fc2", "active", "hidden", "w3")

    w3.last()
    live["fc2"].core()
    step("w3", "fc2", "hidden")
    live["fc2"].first()
    (full_fc2,) = w3.place()
    grad_out = upstream.astype(f32)
    grad_bias_fc2 = jnp.sum(grad_out, axis=0)
    unused, gate_pull = jax.vjp(smooth_gate, live["hidden"])
    grad_hidden = gate_pull(by_rows(upstream, full_fc2))[0].astype(bf16)
    live["grad_hidden"] = grad_hidden
    grad_bias_fc1 = jnp.sum(grad_hidden.astype(f32), axis=0)
    step("grad_hidden")
    grad_hidden = live["grad_hidden"]
    live["fc1"] = Scatter(grid, normed2, grad_hidden)
    step("fc1", "grad_hidden", "fc2")
    live["fc2"].second()
    live["fc1"].core()
    live["up2"] = by_rows(live["grad_hidden"], full_fc1)
    step("fc1", "up2")
    grad_mid_norm, grad_gain2, grad_shift2 = norm_back(middle, gain2, shift2, live["up2"])
    grad_middle = grad_out + grad_mid_norm
    grad_branch = grad_middle.astype(bf16)
    grad_bias_out = jnp.sum(grad_branch.astype(f32), axis=0)
    live["grad_attended"] = by_rows(grad_branch, full_out).astype(bf16)
    live["out"] = Scatter(grid, attended, grad_branch)
    step("grad_attended", "out", "fc1", "fc2")
    live["fc2"].far_z()
    live["fc1"].first()
    live["out"].core()
    parts = [
        attend_back(
            info, starts, live["mixed"], live["other"], live["low"], low_lse,
            live["grad_attended"], 0, 2,
        )
    ]
    live["part"] = parts[0]
    step("part", "grad_attended", "out", "fc1", "fc2")
    parts[0] = live["part"]
    live["fc2"].near_z()
    live["fc1"].second()
    live["back"] = grid.over_core(parts[0][2])
    parts.append(
        attend_back(
            info, starts, live["mixed"], live["other"], live["high"], high_lse,
            live["grad_attended"], 1, 2,
        )
    )
    live["part"] = parts[1]
    step("part", "back", "fc1", "fc2", "out", "active")
    parts[1] = live["part"]
    live["fc1"].far_z()
    live["out"].first()
    live["back2"] = grid.over_core(parts[1][2])
    result = middle + jnp.dot(live["active"], full_fc2, preferred_element_type=f32) + b_fc2
    live["output"] = result.astype(bf16)
    step("back", "back2", "output", "out")
    live["out"].second()
    output = swap_back(live["output"])
    dkv = [both(p[1], live[n]) for p, n in zip(parts, ("back", "back2"))]
    grad_mixed = jnp.concatenate(
        [p[0] for p in parts] + [d[0] for d in dkv] + [d[1] for d in dkv], axis=1
    )
    live["grad_mixed"] = grad_mixed
    live["qkv"] = Scatter(grid, normed, grad_mixed)
    step("qkv", "grad_mixed", "fc1", "out")
    live["qkv"].core()
    live["fc1"].near_z()
    live["out"].far_z()
    grad_mixed = live["grad_mixed"]
    live["up1"] = by_rows(grad_mixed, full_qkv)
    step("qkv", "up1", "grad_mixed", "out")
    live["qkv"].first()
    live["out"].near_z()
    grad_mixed = live["grad_mixed"]
    grad_bias_query = jnp.sum(grad_mixed[:, :width].astype(f32), axis=0)
    grad_bias_value = jnp.sum(grad_mixed[:, 2 * width :].astype(f32), axis=0)
    grad_in_norm, grad_gain1, grad_shift1 = norm_back(inputs, gain1, shift1, live["up1"])
    live["grad_tokens"] = (grad_middle + grad_in_norm).astype(bf16)
    sums = SumVectors(
        grid,
        jnp.concatenate(
            [
                v.reshape(-1, width)
                for v in (
                    grad_gain1, grad_shift1, grad_bias_query, grad_bias_value, grad_bias_out,
                    grad_gain2, grad_shift2, grad_bias_fc2, grad_bias_fc1,
                )
            ],
            axis=0,
        ),
    )
    live["sums"] = sums
    step("sums", "grad_tokens", "out")
    grad_tokens = swap_back(live["grad_tokens"])
    sums.add(grid.over_core)
    sums.add(grid.over_x)
    step("sums", "qkv")
    live["qkv"].second()
    sums.add(grid.over_y)
    step("sums", "qkv")
    live["qkv"].along_z()
    sums.add(lambda v: grid.flip_z(v, 1))
    sums.add(lambda v: grid.flip_z(v, 2))
    sums = sums.state
    grad_qkv, grad_w_out, grad_fc1, grad_fc2 = (
        live[n].result() for n in ("qkv", "out", "fc1", "fc2")
    )

    device, devices = grid.f * n_tok + t, n_fsdp * n_tok

    def owned(vector):
        count = vector.shape[0] // devices
        return lax.dynamic_slice_in_dim(vector, device * count, count, 0)

    return (
        output,
        grad_tokens,
        owned(sums[0]),
        owned(sums[1]),
        grad_qkv,
        owned(sums[2]),
        owned(sums[3]),
        grad_w_out,
        owned(sums[4]),
        owned(sums[5]),
        owned(sums[6]),
        grad_fc1,
        owned(sums[8:].reshape(hidden_width)),
        grad_fc2,
        owned(sums[7]),
    )


def solution(mesh):
    vector, matrix = P("fsdp"), P("fsdp", None)
    rows = P(None, "fsdp", "tok", None)
    own_vector, own_matrix = P(("fsdp", "tok")), P(("fsdp", "tok"), None)
    return jax.shard_map(
        functools.partial(local, mesh.shape["fsdp"], mesh.shape["tok"]),
        mesh=mesh,
        in_specs=(
            rows, rows, P(None, "fsdp", None), vector, vector, matrix, vector, vector,
            matrix, vector, vector, vector, matrix, vector, matrix, vector,
        ),
        out_specs=(
            rows, rows, own_vector, own_vector, own_matrix, own_vector, own_vector,
            own_matrix, own_vector, own_vector, own_vector, own_matrix, own_vector,
            own_matrix, own_vector,
        ),
        check_vma=False,
    )
```

time: 629 us -> 516 us (0.82)
  waiting for transfers between devices: 241 us -> 148 us
  matrix products: 84.1 us -> 37.2 us
  starting transfers between devices: 110 us -> 75.8 us
  other arithmetic: 47 us -> 80.3 us
  Pallas kernels: 70.8 us -> 104 us
    ppermute x120 -> x72, waiting for transfers between devices: 241 us -> 148 us  [send(): return lax.ppermute(value, AXES, pairs)]
    dot_general x10 -> x6, matrix products: 76.3 us -> 32.2 us  [the longest x4 22 us: by_rows(): lax.dot_general(a, b, (((1,), (1,)), ((), ())), preferred_element_type=f32)]
    ppermute x120 -> x72, starting transfers between devices: 110 us -> 75.8 us  [send(): return lax.ppermute(value, AXES, pairs)]
    pallas_call x5 -> x9, Pallas kernels: 47.5 us -> 79.5 us  [the longest x4 36.8 us: __init__(): pl.pallas_call(functools.partial(split_kernel, rows), out_shape=(part, pa...]
    dynamic_slice x16 -> x4, local copies, waits for them, and re-layouts: 21.2 us -> 2.86 us  [own(): lax.dynamic_slice_in_dim(w, self.grid.t * self.rows, self.rows, 0)]
    convert_element_type x24 -> x23, other arithmetic: 13.4 us -> 28.6 us  [both(): return (a.astype(f32) + b.astype(f32)).astype(bf16)]
    concatenate x0 -> x10, other arithmetic: none -> 10.2 us  [the longest x3 3.42 us: second(): state['cxy'] = grid.over_core(jnp.concatenate([state['x'], state['y']]))]
    unnamed x268 -> x245, local copies, waits for them, and re-layouts: 21.7 us -> 31.8 us
  transfers between devices with their start and end apart: 120 -> 72, of which waited for: 42 -> 23; matrix products, arithmetic and copies ran while one was open for 20% -> 24% of each run, Pallas kernels for 11% -> 19%
where the time goes in v2:
time: 516 us; the launch traced here: 510 us
  waiting for transfers between devices  148 us (29%)
  Pallas kernels  104 us (20%)
  other arithmetic  80.3 us (16%)
  starting transfers between devices  75.8 us (15%)
  local copies, waits for them, and re-layouts  61.3 us (12%)
  matrix products  37.2 us (7%)
    ppermute x72, waiting for transfers between devices, send(): return lax.ppermute(value, AXES, pairs)  148 us
    ppermute x72, starting transfers between devices, send(): return lax.ppermute(value, AXES, pairs)  75.8 us
    pallas_call x4, Pallas kernels, __init__(): pl.pallas_call(functools.partial(split_kernel, rows), out_shape=(part, pa...  36.8 us
    unnamed x245, local copies, waits for them, and re-layouts  31.8 us
    convert_element_type x23, other arithmetic, both(): return (a.astype(f32) + b.astype(f32)).astype(bf16)  28.6 us
    pallas_call x2, Pallas kernels, attend_back(): pl.pallas_call(functools.partial(attend_back_kernel, block), out_shape=(j...  27.8 us
    pallas_call x2, Pallas kernels, attend(): pl.pallas_call(functools.partial(attend_kernel, block), out_shape=(jax.Sh...  24.9 us
    dot_general x4, matrix products, by_rows(): lax.dot_general(a, b, (((1,), (1,)), ((), ())), preferred_element_type=f32)  22 us
  transfers between devices with their start and end apart: 72, of which 23 were waited for; matrix products, arithmetic and copies ran while one was open for 24% of the time, Pallas kernels for 19%

profile of v2, /device:TPU:0, one launch (start us, length us, event | category | flops | bytes accessed | tf_op | source)
XLA Modules:
  0.0 509.5 jit_solution(275360955236047697)
XLA Ops:
  12.8 4.1 collective-permute-done.3
  18.0 6.9 %collective-permute-done.1 = bf16[32,3072]{1,0:T(8,128)(2,1)S(1)} collective-permute-done((bf16[32,3072]{1,0:T(8,128)(2,1)S(1)}, bf16[32,3072]{1,0:T(8,128)(2,1)S(1)}, u32[]{:S(2)}, u32[]{:S(2)}) %collective-permute-start.1) | collective-permute-done | bytes 196640 | tf_op jit(solution)/shard_map/ppermute | solution.py:36
  27.2 4.8 collective-permute-start.8
  32.1 8.4 %collective-permute-done.9 = bf16[8,12,128]{2,1,0:T(8,128)(2,1)S(1)} collective-permute-done((bf16[8,12,128]{2,1,0:T(8,128)(2,1)S(1)}, bf16[8,12,128]{2,1,0:T(8,128)(2,1)S(1)}, u32[]{:S(2)}, u32[]{:S(2)}) %collective-permute-start.9) | collective-permute-done | bytes 24608 | tf_op jit(solution)/shard_map/ppermute | solution.py:36
  55.1 3.8 collective-permute-start.13
  63.5 6.9 %collective-permute-done.10.refs_3_ = bf16[2,32,3072]{2,1,0:T(8,128)(2,1)S(1)} collective-permute-done((bf16[2,32,3072]{2,1,0:T(8,128)(2,1)S(1)}, bf16[2,32,3072]{2,1,0:T(8,128)(2,1)S(1)}, u32[]{:S(2)}, u32[]{:S(2)}) %collective-permute-start.10) | collective-permute-done | bytes 393248 | tf_op jit(solution)/shard_map/ppermute | solution.py:36
  70.6 3.8 collective-permute-start.15
  78.6 25.2 %collective-permute-done.15 = bf16[2,32,5120]{2,1,0:T(8,128)(2,1)S(1)} collective-permute-done((bf16[2,32,5120]{2,1,0:T(8,128)(2,1)S(1)}, bf16[2,32,5120]{2,1,0:T(8,128)(2,1)S(1)}, u32[]{:S(2)}, u32[]{:S(2)}) %collective-permute-start.15) | collective-permute-done | bytes 655392 | tf_op jit(solution)/shard_map/ppermute | solution.py:36
  104.5 8.0 %place.3 = bf16[1024,3072]{1,0:T(8,128)(2,1)S(1)} custom-call(s32[32]{0:T(128)S(1)} %stack.408.offsets, bf16[4,32,3072]{2,1,0:T(8,128)(2,1)S(1)} %pad_maximum_fusion.8.refs_0_, bf16[4,32,3072]{2,1,0:T(8,128)(2,1)S(1)} %collective-permute-done.6.refs_1_, bf16[4,32,3072]{2,1,0:T(8,128)(2,1)S(1)} %collective-permute-done.7.refs_2_, ...), custom_call_target="tpu_custom_call" | custom-call | bytes 12582912 | tf_op jit(solution)/shard_map/place/pallas_call | solution.py:163
  122.5 12.3 %attend.2 = (bf16[512,512]{1,0:T(8,128)(2,1)S(1)}, f32[4,4,256]{2,1,0:T(4,128)S(1)}) custom-call(s32[5]{0:T(128)S(1)} %concatenate.59.info, s32[2,256]{1,0:T(2,128)S(1)} %select_reduce_fusion.starts, bf16[512,3072]{1,0:T(8,128)(2,1)S(1)} %add_convert_fusion.q.k.v, bf16[512,3072]{1,0:T(8,128)(2,1)S(1)} %add_convert_fusion.q.k.v, ...), custom_call_target="tpu_custom_call" | custom-call | flops 1073741824 | bytes 3145728 | tf_op jit(solution)/shard_map/attend/pallas_call | solution.py:434
  134.9 16.1 %collective-permute-done.20.refs_1_ = bf16[4,32,5120]{2,1,0:T(8,128)(2,1)} collective-permute-done((bf16[4,32,5120]{2,1,0:T(8,128)(2,1)}, bf16[4,32,5120]{2,1,0:T(8,128)(2,1)}, u32[]{:S(2)}, u32[]{:S(2)}) %collective-permute-start.20) | collective-permute-done | bytes 1310752 | tf_op jit(solution)/shard_map/ppermute | solution.py:36
  157.8 12.6 %attend.3 = (bf16[512,512]{1,0:T(8,128)(2,1)S(1)}, f32[4,4,256]{2,1,0:T(4,128)S(1)}) custom-call(s32[5]{0:T(128)S(1)} %concatenate.59.info, s32[2,256]{1,0:T(2,128)S(1)} %select_reduce_fusion.starts, bf16[512,3072]{1,0:T(8,128)(2,1)S(1)} %add_convert_fusion.q.k.v, bf16[512,3072]{1,0:T(8,128)(2,1)S(1)} %add_convert_fusion.q.k.v, ...), custom_call_target="tpu_custom_call" | custom-call | flops 1073741824 | bytes 3145728 | tf_op jit(solution)/shard_map/attend/pallas_call | solution.py:434
  171.2 12.4 %collective-permute-done.25 = bf16[2,128,1024]{2,1,0:T(8,128)(2,1)S(1)} collective-permute-done((bf16[2,128,1024]{2,1,0:T(8,128)(2,1)S(1)}, bf16[2,128,1024]{2,1,0:T(8,128)(2,1)S(1)}, u32[]{:S(2)}, u32[]{:S(2)}) %collective-permute-start.25) | collective-permute-done | bytes 524320 | tf_op jit(solution)/shard_map/ppermute | solution.py:36
  195.7 4.2 place.4
  203.9 4.6 convolution_add_fusion
  209.6 6.9 %collective-permute-done.28.refs_1_ = bf16[4,128,1024]{2,1,0:T(8,128)(2,1)S(1)} collective-permute-done((bf16[4,128,1024]{2,1,0:T(8,128)(2,1)S(1)}, bf16[4,128,1024]{2,1,0:T(8,128)(2,1)S(1)}, u32[]{:S(2)}, u32[]{:S(2)}) %collective-permute-start.28) | collective-permute-done | bytes 1048608 | tf_op jit(solution)/shard_map/ppermute | solution.py:36
  223.6 12.8 %grad_split.4 = (bf16[2,2,2,2,128,1024]{5,4,3,2,1,0:T(8,128)(2,1)S(1)}, bf16[2,2,2,2,128,1024]{5,4,3,2,1,0:T(8,128)(2,1)}) custom-call(s32[1]{0:T(128)} %bitcast.65.core, bf16[512,4096]{1,0:T(8,128)(2,1)S(1)} %fusion.14.left, bf16[512,1024]{1,0:T(8,128)(2,1)S(1)} %copy-done.2), custom_call_target="tpu_custom_call" | custom-call | flops 4294967296 | bytes 13631488 | tf_op jit(solution)/shard_map/grad_split/pallas_call | solution.py:228
  243.0 5.7 %collective-permute-done.33.refs_7_ = bf16[4,128,1024]{2,1,0:T(8,128)(2,1)} collective-permute-done((bf16[4,128,1024]{2,1,0:T(8,128)(2,1)}, bf16[4,128,1024]{2,1,0:T(8,128)(2,1)}, u32[]{:S(2)}, u32[]{:S(2)}) %collective-permute-start.33) | collective-permute-done | bytes 1048608 | tf_op jit(solution)/shard_map/ppermute | solution.py:36
  248.7 4.4 fusion.98
  262.0 6.8 %fusion.106 = f32[512,4096]{1,0:T(8,128)} fusion(bf16[512,1024]{1,0:T(8,128)(2,1)S(1)} %copy-done.3, bf16[4096,1024]{1,0:T(8,128)(2,1)S(1)} %place.5), kind=kOutput, calls=%fused_computation.267 | convolution fusion | flops 4294967296 | bytes 17825792 | tf_op jit(solution)/shard_map/dot_general | solution.py:323
  268.8 9.5 %convert_reduce_fusion = (f32[4096]{0:T(1024)S(1)}, bf16[512,4096]{1,0:T(8,128)(2,1)S(1)}) fusion(f32[512,4096]{1,0:T(8,128)} %copy-done.65, f32[512,4096]{1,0:T(8,128)} %fusion.106), kind=kLoop, calls=%fused_computation.18 | loop fusion | flops 46133248 | bytes 20987904 | tf_op jit(solution)/shard_map/reduce_sum | solution.py:620
  278.3 11.8 %grad_split.5 = (bf16[2,2,2,2,32,4096]{5,4,3,2,1,0:T(8,128)(2,1)S(1)}, bf16[2,2,2,2,32,4096]{5,4,3,2,1,0:T(8,128)(2,1)}) custom-call(s32[1]{0:T(128)} %bitcast.65.core, bf16[512,1024]{1,0:T(8,128)(2,1)S(1)} %copy-done.50, bf16[512,4096]{1,0:T(8,128)(2,1)S(1)} %get-tuple-element.321.right), custom_call_target="tpu_custom_call" | custom-call | flops 4294967296 | bytes 13631488 | tf_op jit(solution)/shard_map/grad_split/pallas_call | solution.py:228
  303.0 7.1 %fusion.107 = f32[512,1024]{1,0:T(8,128)S(1)} fusion(bf16[512,4096]{1,0:T(8,128)(2,1)S(1)} %copy-done.20, bf16[1024,4096]{1,0:T(8,128)(2,1)} %copy-done.56), kind=kOutput, calls=%fused_computation.268 | convolution fusion | flops 4294967296 | bytes 14680064 | tf_op jit(solution)/shard_map/dot_general | solution.py:323
  332.8 14.1 %attend_back.2 = (bf16[512,512]{1,0:T(8,128)(2,1)S(1)}, f32[2,512,512]{2,1,0:T(8,128)S(1)}, bf16[2,512,512]{2,1,0:T(8,128)(2,1)}) custom-call(s32[5]{0:T(128)S(1)} %concatenate.59.info, s32[2,256]{1,0:T(2,128)S(1)} %select_reduce_fusion.starts, bf16[512,3072]{1,0:T(8,128)(2,1)S(1)} %add_convert_fusion.q.k.v, bf16[512,3072]{1,0:T(8,128)(2,1)S(1)} %add_convert_fusion.q.k.v, ...), custom_call_target="tpu_custom_call" | custom-call | flops 2684354560 | bytes 7340032 | tf_op jit(solution)/shard_map/attend_back/pallas_call | solution.py:460
  346.9 10.9 %collective-permute-done.43 = bf16[2,128,1024]{2,1,0:T(8,128)(2,1)S(1)} collective-permute-done((bf16[2,128,1024]{2,1,0:T(8,128)(2,1)S(1)}, bf16[2,128,1024]{2,1,0:T(8,128)(2,1)S(1)}, u32[]{:S(2)}, u32[]{:S(2)}) %collective-permute-start.43) | collective-permute-done | bytes 524320 | tf_op jit(solution)/shard_map/ppermute | solution.py:36
  370.6 13.8 %attend_back.3 = (bf16[512,512]{1,0:T(8,128)(2,1)S(1)}, f32[2,512,512]{2,1,0:T(8,128)S(1)}, bf16[2,512,512]{2,1,0:T(8,128)(2,1)S(1)}) custom-call(s32[5]{0:T(128)S(1)} %concatenate.59.info, s32[2,256]{1,0:T(2,128)S(1)} %select_reduce_fusion.starts, bf16[512,3072]{1,0:T(8,128)(2,1)S(1)} %add_convert_fusion.q.k.v, ...), custom_call_target="tpu_custom_call" | custom-call | flops 2684354560 | bytes 7340032 | tf_op jit(solution)/shard_map/attend_back/pallas_call | solution.py:460
  394.0 5.6 %add_convert_fusion.4 = bf16[512,1024]{1,0:T(8,128)(2,1)} fusion(f32[512,1024]{1,0:T(8,128)S(1)} %copy-done.61, bf16[512,4096]{1,0:T(8,128)(2,1)S(1)} %copy-done.13, bf16[4096,1024]{1,0:T(8,128)(2,1)S(1)} %bitcast.311, f32[1024]{0:T(1024)S(1)} %bitcast.341), kind=kOutput, calls=%fused_computation.49 | convolution fusion | flops 4296540160 | bytes 15732736 | tf_op jit(solution)/shard_map/dot_general | solution.py:663
  407.2 8.9 %grad_split.7 = (bf16[2,2,2,2,32,3072]{5,4,3,2,1,0:T(8,128)(2,1)S(1)}, bf16[2,2,2,2,32,3072]{5,4,3,2,1,0:T(8,128)(2,1)}) custom-call(s32[1]{0:T(128)} %bitcast.65.core, bf16[512,1024]{1,0:T(8,128)(2,1)S(1)} %copy-done.46, bf16[512,3072]{1,0:T(8,128)(2,1)S(1)} %fusion.48.right), custom_call_target="tpu_custom_call" | custom-call | flops 3221225472 | bytes 10485760 | tf_op jit(solution)/shard_map/grad_split/pallas_call | solution.py:228
  429.9 5.9 %fusion.108 = f32[512,1024]{1,0:T(8,128)S(1)} fusion(bf16[512,3072]{1,0:T(8,128)(2,1)S(1)} %copy-done.30, bf16[1024,3072]{1,0:T(8,128)(2,1)} %copy-done.11), kind=kOutput, calls=%fused_computation.269 | convolution fusion | flops 3221225472 | bytes 11534336 | tf_op jit(solution)/shard_map/dot_general | solution.py:323
  455.1 12.8 %collective-permute-done.60 = f32[12,1024]{1,0:T(8,128)S(1)} collective-permute-done((f32[12,1024]{1,0:T(8,128)S(1)}, f32[12,1024]{1,0:T(8,128)S(1)}, u32[]{:S(2)}, u32[]{:S(2)}) %collective-permute-start.60) | collective-permute-done | bytes 49184 | tf_op jit(solution)/shard_map/ppermute | solution.py:36
  477.3 7.4 %collective-permute-done.63 = f32[12,1024]{1,0:T(8,128)S(1)} collective-permute-done((f32[12,1024]{1,0:T(8,128)S(1)}, f32[12,1024]{1,0:T(8,128)S(1)}, u32[]{:S(2)}, u32[]{:S(2)}) %collective-permute-start.63) | collective-permute-done | bytes 49184 | tf_op jit(solution)/shard_map/ppermute | solution.py:36
  495.6 6.6 %collective-permute-done.67 = f32[12,1024]{1,0:T(8,128)S(1)} collective-permute-done((f32[12,1024]{1,0:T(8,128)S(1)}, f32[12,1024]{1,0:T(8,128)S(1)}, u32[]{:S(2)}, u32[]{:S(2)}) %collective-permute-start.67) | collective-permute-done | bytes 49184 | tf_op jit(solution)/shard_map/ppermute | solution.py:36
  (513 shorter events, 221.5 us)
Async XLA Ops:
  25.1 20.0 %collective-permute-start.6 = (bf16[4,32,3072]{2,1,0:T(8,128)(2,1)S(1)}, bf16[4,32,3072]{2,1,0:T(8,128)(2,1)S(1)}, u32[]{:S(2)}, u32[]{:S(2)}) collective-permute-start(bf16[4,32,3072]{2,1,0:T(8,128)(2,1)S(1)} %pad_maximum_fusion.8.refs_0_), channel_id=1, source_target_pairs={{0,4},{1,5},{2,6},{3,7},{4,0},{5,1},{6,2},{7,3},{8,12},{9,13},{10,... | collective-permute-start | bytes 2359304 | tf_op jit(solution)/shard_map/ppermute | solution.py:36
  25.7 19.6 %collective-permute-start.7 = (bf16[4,32,3072]{2,1,0:T(8,128)(2,1)S(1)}, bf16[4,32,3072]{2,1,0:T(8,128)(2,1)S(1)}, u32[]{:S(2)}, u32[]{:S(2)}) collective-permute-start(bf16[4,32,3072]{2,1,0:T(8,128)(2,1)S(1)} %pad_maximum_fusion.8.refs_0_), channel_id=1, source_target_pairs={{0,2},{1,3},{2,0},{3,1},{4,6},{5,7},{6,4},{7,5},{8,10},{9,11},{10,... | collective-permute-start | bytes 2359304 | tf_op jit(solution)/shard_map/ppermute | solution.py:36
  46.6 23.7 %collective-permute-start.12 = (bf16[8,32,3072]{2,1,0:T(8,128)(2,1)}, bf16[8,32,3072]{2,1,0:T(8,128)(2,1)}, u32[]{:S(2)}, u32[]{:S(2)}) collective-permute-start(bf16[8,32,3072]{2,1,0:T(8,128)(2,1)} %pad_maximum_fusion.2), channel_id=1, source_target_pairs={{0,1},{1,0},{2,3},{3,2},{4,5},{5,4},{6,7},{7,6},{8,9},{9,8},{10,11... | collective-permute-start | bytes 4718600 | tf_op jit(solution)/shard_map/ppermute | solution.py:36
  49.8 20.6 %collective-permute-start.10 = (bf16[2,32,3072]{2,1,0:T(8,128)(2,1)S(1)}, bf16[2,32,3072]{2,1,0:T(8,128)(2,1)S(1)}, u32[]{:S(2)}, u32[]{:S(2)}) collective-permute-start(bf16[2,32,3072]{2,1,0:T(8,128)(2,1)S(1)} %slice.153), channel_id=1, source_target_pairs={{0,2},{1,3},{2,0},{3,1},{4,6},{5,7},{6,4},{7,5},{8,10},{9,11},{10,... | collective-permute-start | bytes 1179656 | tf_op jit(solution)/shard_map/ppermute | solution.py:36
  70.4 33.4 %collective-permute-start.14 = (bf16[4,32,3072]{2,1,0:T(8,128)(2,1)S(1)}, bf16[4,32,3072]{2,1,0:T(8,128)(2,1)S(1)}, u32[]{:S(2)}, u32[]{:S(2)}) collective-permute-start(bf16[4,32,3072]{2,1,0:T(8,128)(2,1)S(1)} %pad_maximum_fusion.9), channel_id=1, source_target_pairs={{0,1},{1,0},{2,3},{3,2},{4,5},{5,4},{6,7},{7,6},{8,9},{9,8},{10,11... | collective-permute-start | bytes 2359304 | tf_op jit(solution)/shard_map/ppermute | solution.py:36
  70.6 33.2 %collective-permute-start.15 = (bf16[2,32,5120]{2,1,0:T(8,128)(2,1)S(1)}, bf16[2,32,5120]{2,1,0:T(8,128)(2,1)S(1)}, u32[]{:S(2)}, u32[]{:S(2)}) collective-permute-start(bf16[2,32,5120]{2,1,0:T(8,128)(2,1)S(1)} %pad_maximum_fusion.10), channel_id=1, source_target_pairs={{0,16},{1,17},{2,18},{3,19},{4,20},{5,21},{6,22},{7,23},{8,24},{9,... | collective-permute-start | bytes 1966088 | tf_op jit(solution)/shard_map/ppermute | solution.py:36
  75.3 28.4 %collective-permute-start.16 = (bf16[128,1024]{1,0:T(8,128)(2,1)S(1)}, bf16[128,1024]{1,0:T(8,128)(2,1)S(1)}, u32[]{:S(2)}, u32[]{:S(2)}) collective-permute-start(bf16[128,1024]{1,0:T(8,128)(2,1)S(1)} %constant_dynamic-slice_fusion.8), channel_id=1, source_target_pairs={{0,8},{1,9},{2,10},{3,11},{4,12},{5,13},{6,14},{7,15},{8,0},{9,1},... | collective-permute-start | bytes 786440 | tf_op jit(solution)/shard_map/ppermute | solution.py:36
  120.0 31.0 %collective-permute-start.20 = (bf16[4,32,5120]{2,1,0:T(8,128)(2,1)}, bf16[4,32,5120]{2,1,0:T(8,128)(2,1)}, u32[]{:S(2)}, u32[]{:S(2)}) collective-permute-start(bf16[4,32,5120]{2,1,0:T(8,128)(2,1)} %constant_dynamic-update-slice_fusion.2.refs_0_), channel_id=1, source_target_pairs={{0,4},{1,5},{2,6},{3,7},{4,0},{5,1},{6,2},{7,3},{8,12},{9,13},{10,... | collective-permute-start | bytes 3932168 | tf_op jit(solution)/shard_map/ppermute | solution.py:36
  121.5 30.7 %collective-permute-start.21 = (bf16[4,32,5120]{2,1,0:T(8,128)(2,1)}, bf16[4,32,5120]{2,1,0:T(8,128)(2,1)}, u32[]{:S(2)}, u32[]{:S(2)}) collective-permute-start(bf16[4,32,5120]{2,1,0:T(8,128)(2,1)} %constant_dynamic-update-slice_fusion.2.refs_0_), channel_id=1, source_target_pairs={{0,2},{1,3},{2,0},{3,1},{4,6},{5,7},{6,4},{7,5},{8,10},{9,11},{10,... | collective-permute-start | bytes 3932168 | tf_op jit(solution)/shard_map/ppermute | solution.py:36
  154.2 29.5 %collective-permute-start.24 = (bf16[8,32,5120]{2,1,0:T(8,128)(2,1)S(1)}, bf16[8,32,5120]{2,1,0:T(8,128)(2,1)S(1)}, u32[]{:S(2)}, u32[]{:S(2)}) collective-permute-start(bf16[8,32,5120]{2,1,0:T(8,128)(2,1)S(1)} %pad_maximum_fusion), channel_id=1, source_target_pairs={{0,1},{1,0},{2,3},{3,2},{4,5},{5,4},{6,7},{7,6},{8,9},{9,8},{10,11... | collective-permute-start | bytes 7864328 | tf_op jit(solution)/shard_map/ppermute | solution.py:36
  156.6 27.1 %collective-permute-start.22 = (bf16[2,32,5120]{2,1,0:T(8,128)(2,1)S(1)}, bf16[2,32,5120]{2,1,0:T(8,128)(2,1)S(1)}, u32[]{:S(2)}, u32[]{:S(2)}) collective-permute-start(bf16[2,32,5120]{2,1,0:T(8,128)(2,1)S(1)} %slice.160), channel_id=1, source_target_pairs={{0,2},{1,3},{2,0},{3,1},{4,6},{5,7},{6,4},{7,5},{8,10},{9,11},{10,... | collective-permute-start | bytes 1966088 | tf_op jit(solution)/shard_map/ppermute | solution.py:36
  157.1 26.5 %collective-permute-start.23 = (bf16[2,32,5120]{2,1,0:T(8,128)(2,1)S(1)}, bf16[2,32,5120]{2,1,0:T(8,128)(2,1)S(1)}, u32[]{:S(2)}, u32[]{:S(2)}) collective-permute-start(bf16[2,32,5120]{2,1,0:T(8,128)(2,1)S(1)} %slice.161), channel_id=1, source_target_pairs={{0,4},{1,5},{2,6},{3,7},{4,0},{5,1},{6,2},{7,3},{8,12},{9,13},{10,... | collective-permute-start | bytes 1966088 | tf_op jit(solution)/shard_map/ppermute | solution.py:36
  157.7 25.9 %collective-permute-start.25 = (bf16[2,128,1024]{2,1,0:T(8,128)(2,1)S(1)}, bf16[2,128,1024]{2,1,0:T(8,128)(2,1)S(1)}, u32[]{:S(2)}, u32[]{:S(2)}) collective-permute-start(bf16[2,128,1024]{2,1,0:T(8,128)(2,1)S(1)} %pad_maximum_fusion.11), channel_id=1, source_target_pairs={{0,16},{1,17},{2,18},{3,19},{4,20},{5,21},{6,22},{7,23},{8,24},{9,... | collective-permute-start | bytes 1572872 | tf_op jit(solution)/shard_map/ppermute | solution.py:36
  191.3 25.1 %collective-permute-start.28 = (bf16[4,128,1024]{2,1,0:T(8,128)(2,1)S(1)}, bf16[4,128,1024]{2,1,0:T(8,128)(2,1)S(1)}, u32[]{:S(2)}, u32[]{:S(2)}) collective-permute-start(bf16[4,128,1024]{2,1,0:T(8,128)(2,1)S(1)} %constant_dynamic-update-slice_fusion.4.refs_0_), channel_id=1, source_target_pairs={{0,4},{1,5},{2,6},{3,7},{4,0},{5,1},{6,2},{7,3},{8,12},{9,13},{10,... | collective-permute-start | bytes 3145736 | tf_op jit(solution)/shard_map/ppermute | solution.py:36
  192.8 24.9 %collective-permute-start.29 = (bf16[4,128,1024]{2,1,0:T(8,128)(2,1)S(1)}, bf16[4,128,1024]{2,1,0:T(8,128)(2,1)S(1)}, u32[]{:S(2)}, u32[]{:S(2)}) collective-permute-start(bf16[4,128,1024]{2,1,0:T(8,128)(2,1)S(1)} %constant_dynamic-update-slice_fusion.4.refs_0_), channel_id=1, source_target_pairs={{0,2},{1,3},{2,0},{3,1},{4,6},{5,7},{6,4},{7,5},{8,10},{9,11},{10,... | collective-permute-start | bytes 3145736 | tf_op jit(solution)/shard_map/ppermute | solution.py:36
  217.9 20.5 %collective-permute-start.32 = (bf16[8,128,1024]{2,1,0:T(8,128)(2,1)S(1)}, bf16[8,128,1024]{2,1,0:T(8,128)(2,1)S(1)}, u32[]{:S(2)}, u32[]{:S(2)}) collective-permute-start(bf16[8,128,1024]{2,1,0:T(8,128)(2,1)S(1)} %pad_maximum_fusion.1), channel_id=1, source_target_pairs={{0,1},{1,0},{2,3},{3,2},{4,5},{5,4},{6,7},{7,6},{8,9},{9,8},{10,11... | collective-permute-start | bytes 6291464 | tf_op jit(solution)/shard_map/ppermute | solution.py:36
  218.7 19.6 %collective-permute-start.30 = (bf16[2,128,1024]{2,1,0:T(8,128)(2,1)S(1)}, bf16[2,128,1024]{2,1,0:T(8,128)(2,1)S(1)}, u32[]{:S(2)}, u32[]{:S(2)}) collective-permute-start(bf16[2,128,1024]{2,1,0:T(8,128)(2,1)S(1)} %slice.166), channel_id=1, source_target_pairs={{0,2},{1,3},{2,0},{3,1},{4,6},{5,7},{6,4},{7,5},{8,10},{9,11},{10,... | collective-permute-start | bytes 1572872 | tf_op jit(solution)/shard_map/ppermute | solution.py:36
  255.4 36.7 %collective-permute-start.36 = (bf16[2,2,128,1024]{3,2,1,0:T(8,128)(2,1)}, bf16[2,2,128,1024]{3,2,1,0:T(8,128)(2,1)S(1)}, u32[]{:S(2)}, u32[]{:S(2)}) collective-permute-start(bf16[2,2,128,1024]{3,2,1,0:T(8,128)(2,1)} %get-tuple-element.463), channel_id=1, source_target_pairs={{0,2},{1,3},{2,0},{3,1},{4,6},{5,7},{6,4},{7,5},{8,10},{9,11},{10,... | collective-permute-start | bytes 3145736 | tf_op jit(solution)/shard_map/ppermute | solution.py:36
  258.0 35.2 %collective-permute-start.35 = (bf16[2,2,128,1024]{3,2,1,0:T(8,128)(2,1)S(1)}, bf16[2,2,128,1024]{3,2,1,0:T(8,128)(2,1)S(1)}, u32[]{:S(2)}, u32[]{:S(2)}) collective-permute-start(bf16[2,2,128,1024]{3,2,1,0:T(8,128)(2,1)S(1)} %get-tuple-element.469), channel_id=1, source_target_pairs={{0,4},{1,5},{2,6},{3,7},{4,0},{5,1},{6,2},{7,3},{8,12},{9,13},{10,... | collective-permute-start | bytes 3145736 | tf_op jit(solution)/shard_map/ppermute | solution.py:36
  299.3 20.9 %collective-permute-start.39 = (bf16[2,128,1024]{2,1,0:T(8,128)(2,1)S(1)}, bf16[2,128,1024]{2,1,0:T(8,128)(2,1)S(1)}, u32[]{:S(2)}, u32[]{:S(2)}) collective-permute-start(bf16[2,128,1024]{2,1,0:T(8,128)(2,1)S(1)} %get-tuple-element.487), channel_id=1, source_target_pairs={{0,4},{1,5},{2,6},{3,7},{4,0},{5,1},{6,2},{7,3},{8,12},{9,13},{10,... | collective-permute-start | bytes 1572872 | tf_op jit(solution)/shard_map/ppermute | solution.py:36
  326.2 31.7 %collective-permute-start.42 = (bf16[2,2,32,4096]{3,2,1,0:T(8,128)(2,1)}, bf16[2,2,32,4096]{3,2,1,0:T(8,128)(2,1)}, u32[]{:S(2)}, u32[]{:S(2)}) collective-permute-start(bf16[2,2,32,4096]{3,2,1,0:T(8,128)(2,1)} %get-tuple-element.455), channel_id=1, source_target_pairs={{0,2},{1,3},{2,0},{3,1},{4,6},{5,7},{6,4},{7,5},{8,10},{9,11},{10,... | collective-permute-start | bytes 3145736 | tf_op jit(solution)/shard_map/ppermute | solution.py:36
  329.0 28.9 %collective-permute-start.41 = (bf16[2,2,32,4096]{3,2,1,0:T(8,128)(2,1)}, bf16[2,2,32,4096]{3,2,1,0:T(8,128)(2,1)}, u32[]{:S(2)}, u32[]{:S(2)}) collective-permute-start(bf16[2,2,32,4096]{3,2,1,0:T(8,128)(2,1)} %get-tuple-element.461), channel_id=1, source_target_pairs={{0,4},{1,5},{2,6},{3,7},{4,0},{5,1},{6,2},{7,3},{8,12},{9,13},{10,... | collective-permute-start | bytes 3145736 | tf_op jit(solution)/shard_map/ppermute | solution.py:36
  329.9 27.9 %collective-permute-start.40 = (bf16[2,2,2,2,32,1024]{5,4,3,2,1,0:T(8,128)(2,1)}, bf16[2,2,2,2,32,1024]{5,4,3,2,1,0:T(8,128)(2,1)}, u32[]{:S(2)}, u32[]{:S(2)}) collective-permute-start(bf16[2,2,2,2,32,1024]{5,4,3,2,1,0:T(8,128)(2,1)} %get-tuple-element.337), channel_id=1, source_target_pairs={{0,1},{1,0},{2,3},{3,2},{4,5},{5,4},{6,7},{7,6},{8,9},{9,8},{10,11... | collective-permute-start | bytes 3145736 | tf_op jit(solution)/shard_map/ppermute | solution.py:36
  332.8 25.0 %collective-permute-start.43 = (bf16[2,128,1024]{2,1,0:T(8,128)(2,1)S(1)}, bf16[2,128,1024]{2,1,0:T(8,128)(2,1)S(1)}, u32[]{:S(2)}, u32[]{:S(2)}) collective-permute-start(bf16[2,128,1024]{2,1,0:T(8,128)(2,1)S(1)} %get-tuple-element.485), channel_id=1, source_target_pairs={{0,16},{1,17},{2,18},{3,19},{4,20},{5,21},{6,22},{7,23},{8,24},{9,... | collective-permute-start | bytes 1572872 | tf_op jit(solution)/shard_map/ppermute | solution.py:36
  357.9 26.6 %collective-permute-start.44 = (bf16[2,512,512]{2,1,0:T(8,128)(2,1)}, bf16[2,512,512]{2,1,0:T(8,128)(2,1)}, u32[]{:S(2)}, u32[]{:S(2)}) collective-permute-start(bf16[2,512,512]{2,1,0:T(8,128)(2,1)} %get-tuple-element.348), channel_id=1, source_target_pairs={{0,1},{1,0},{2,3},{3,2},{4,5},{5,4},{6,7},{7,6},{8,9},{9,8},{10,11... | collective-permute-start | bytes 3145736 | tf_op jit(solution)/shard_map/ppermute | solution.py:36
  360.5 24.0 %collective-permute-start.46 = (bf16[2,32,4096]{2,1,0:T(8,128)(2,1)}, bf16[2,32,4096]{2,1,0:T(8,128)(2,1)}, u32[]{:S(2)}, u32[]{:S(2)}) collective-permute-start(bf16[2,32,4096]{2,1,0:T(8,128)(2,1)} %get-tuple-element.481), channel_id=1, source_target_pairs={{0,4},{1,5},{2,6},{3,7},{4,0},{5,1},{6,2},{7,3},{8,12},{9,13},{10,... | collective-permute-start | bytes 1572872 | tf_op jit(solution)/shard_map/ppermute | solution.py:36
  364.0 20.4 %collective-permute-start.45 = (bf16[2,32,4096]{2,1,0:T(8,128)(2,1)}, bf16[2,32,4096]{2,1,0:T(8,128)(2,1)}, u32[]{:S(2)}, u32[]{:S(2)}) collective-permute-start(bf16[2,32,4096]{2,1,0:T(8,128)(2,1)} %get-tuple-element.483), channel_id=1, source_target_pairs={{0,2},{1,3},{2,0},{3,1},{4,6},{5,7},{6,4},{7,5},{8,10},{9,11},{10,... | collective-permute-start | bytes 1572872 | tf_op jit(solution)/shard_map/ppermute | solution.py:36
  390.8 26.9 %collective-permute-start.52 = (bf16[2,32,4096]{2,1,0:T(8,128)(2,1)S(1)}, bf16[2,32,4096]{2,1,0:T(8,128)(2,1)S(1)}, u32[]{:S(2)}, u32[]{:S(2)}) collective-permute-start(bf16[2,32,4096]{2,1,0:T(8,128)(2,1)S(1)} %get-tuple-element.479), channel_id=1, source_target_pairs={{0,16},{1,17},{2,18},{3,19},{4,20},{5,21},{6,22},{7,23},{8,24},{9,... | collective-permute-start | bytes 1572872 | tf_op jit(solution)/shard_map/ppermute | solution.py:36
  419.7 19.2 %collective-permute-start.55 = (bf16[2,2,2,2,32,3072]{5,4,3,2,1,0:T(8,128)(2,1)}, bf16[2,2,2,2,32,3072]{5,4,3,2,1,0:T(8,128)(2,1)}, u32[]{:S(2)}, u32[]{:S(2)}) collective-permute-start(bf16[2,2,2,2,32,3072]{5,4,3,2,1,0:T(8,128)(2,1)} %get-tuple-element.381), channel_id=1, source_target_pairs={{0,1},{1,0},{2,3},{3,2},{4,5},{5,4},{6,7},{7,6},{8,9},{9,8},{10,11... | collective-permute-start | bytes 9437192 | tf_op jit(solution)/shard_map/ppermute | solution.py:36
  444.7 23.1 %collective-permute-start.62 = (bf16[2,2,32,3072]{3,2,1,0:T(8,128)(2,1)}, bf16[2,2,32,3072]{3,2,1,0:T(8,128)(2,1)}, u32[]{:S(2)}, u32[]{:S(2)}) collective-permute-start(bf16[2,2,32,3072]{3,2,1,0:T(8,128)(2,1)} %get-tuple-element.471), channel_id=1, source_target_pairs={{0,2},{1,3},{2,0},{3,1},{4,6},{5,7},{6,4},{7,5},{8,10},{9,11},{10,... | collective-permute-start | bytes 2359304 | tf_op jit(solution)/shard_map/ppermute | solution.py:36
  446.6 21.3 %collective-permute-start.61 = (bf16[2,2,32,3072]{3,2,1,0:T(8,128)(2,1)}, bf16[2,2,32,3072]{3,2,1,0:T(8,128)(2,1)}, u32[]{:S(2)}, u32[]{:S(2)}) collective-permute-start(bf16[2,2,32,3072]{3,2,1,0:T(8,128)(2,1)} %get-tuple-element.477), channel_id=1, source_target_pairs={{0,4},{1,5},{2,6},{3,7},{4,0},{5,1},{6,2},{7,3},{8,12},{9,13},{10,... | collective-permute-start | bytes 2359304 | tf_op jit(solution)/shard_map/ppermute | solution.py:36
  452.1 22.4 %collective-permute-start.58 = (bf16[256,1024]{1,0:T(8,128)(2,1)S(1)}, bf16[256,1024]{1,0:T(8,128)(2,1)S(1)}, u32[]{:S(2)}, u32[]{:S(2)}) collective-permute-start(bf16[256,1024]{1,0:T(8,128)(2,1)S(1)} %slice.190), channel_id=1, source_target_pairs={{0,3},{1,2},{2,1},{3,0},{4,7},{5,6},{6,5},{7,4},{8,11},{9,10},{10,... | collective-permute-start | bytes 1572872 | tf_op jit(solution)/shard_map/ppermute | solution.py:36
  (158 other events, 1328.8 us)

commit v3 on v2

--- a/solution.py
+++ b/solution.py
@@ -62,9 +62,13 @@
     return (a.astype(f32) + b.astype(f32)).astype(bf16)
 
 
-def halves(a, b, index):
-    keep, send = index, 1 - index
-    return both(pick(a, keep, 0), pick(b, keep, 0)), both(pick(a, send, 0), pick(b, send, 0))
+def halves(a, b, index, lead=()):
+    def part(values, i):
+        rest = values.shape[len(lead) + 1 :]
+        start = lead + (i,) + (0,) * len(rest)
+        return lax.dynamic_slice(values, start, (1,) * (len(lead) + 1) + rest).reshape(rest)
+
+    return both(part(a, index), part(b, index)), both(part(a, 1 - index), part(b, 1 - index))
 
 
 def place_kernel(rows, widths, offsets, *refs):
@@ -112,6 +116,19 @@
             self.flip = False
             self.state = {"steps": [own] + [self.grid.over_z(own, k) for k in (1, 2, 3)]}
 
+    def beside_z(self):
+        if self.staged:
+            own = self.own()
+            self.flip = False
+            self.state = {"own": own, "z1": self.grid.over_z(own, 1), "z3": self.grid.over_z(own, 3)}
+
+    def across_z(self):
+        if self.staged:
+            state = self.state
+            self.state = {
+                "steps": [state["own"], state["z1"], self.grid.over_z(state["own"], 2), state["z3"]]
+            }
+
     def near_z(self):
         if self.staged:
             own = self.own()
@@ -126,15 +143,27 @@
         if self.staged:
             grid, steps = self.grid, self.state["steps"]
             q = jnp.concatenate(steps) if self.flip else jnp.stack(steps)
-            self.state = {
-                "q": q, "x": grid.over_x(q), "y": grid.over_y(q), "cq": grid.over_core(q)
-            }
+            self.state = {"q": q, "x": [grid.over_x(q[:2])], "y": [grid.over_y(q[2:])]}
+
+    def first_whole(self):
+        if self.staged:
+            grid, q = self.grid, jnp.stack(self.state["steps"])
+            self.state = {"q": q, "x": [grid.over_x(q)], "y": [grid.over_y(q)]}
+
+    def first_rest(self):
+        if self.staged:
+            grid, state = self.grid, self.state
+            state["x"] = state["x"] + [grid.over_x(state["q"][2:])]
+            state["y"] = [grid.over_y(state["q"][:2])] + state["y"]
 
     def second(self):
         if self.staged:
             state, grid = self.state, self.grid
-            state["a"], state["b"] = grid.over_y(state["x"][:2]), grid.over_x(state["y"][2:])
-            state["cxy"] = grid.over_core(jnp.concatenate([state["x"], state["y"]]))
+            state["a"] = grid.over_y(state["x"][0][:2])
+            state["b"] = grid.over_x(state["y"][-1][-2:])
+            state["near"] = grid.over_core(
+                jnp.concatenate([state["q"]] + state["x"] + state["y"])
+            )
 
     def last(self):
         if self.staged:
@@ -151,10 +180,12 @@
         ab = at(1, 1)
         order = (
             ("q", at(0, 0), 0), ("x", at(1, 0), 0), ("y", at(0, 1), 0), ("a", ab[:2], 0),
-            ("b", ab[2:], 0), ("cq", at(0, 0), 1), ("cxy", at(1, 0) + at(0, 1), 1), ("cab", ab, 1),
+            ("b", ab[2:], 0), ("near", at(0, 0) + at(1, 0) + at(0, 1), 1), ("cab", ab, 1),
         )
-        offsets = []
+        offsets, pieces = [], []
         for name, places, dc in order:
+            have = self.state[name]
+            pieces += have if isinstance(have, (list, tuple)) else [have]
             for k, dx, dy in places:
                 z = grid.z ^ k if self.flip else (grid.z + 4 - k) % 4
                 x, y, c = grid.x ^ dx, grid.y ^ dy, grid.c ^ dc
@@ -164,7 +195,7 @@
             functools.partial(place_kernel, rows, widths),
             out_shape=[jax.ShapeDtypeStruct((total, width), kind) for width in widths],
             in_specs=[pl.BlockSpec(memory_space=pltpu.SMEM)]
-            + [pl.BlockSpec(memory_space=pl.ANY)] * len(order),
+            + [pl.BlockSpec(memory_space=pl.ANY)] * len(pieces),
             out_specs=[pl.BlockSpec(memory_space=pltpu.VMEM)] * len(widths),
             scratch_shapes=[pltpu.SemaphoreType.DMA((len(offsets) * len(widths),))],
             compiler_params=pltpu.CompilerParams(vmem_limit_bytes=24 * 2**20),
@@ -172,7 +203,7 @@
                 flops=0, bytes_accessed=4 * total * sum(widths), transcendentals=0
             ),
             name="place",
-        )(jnp.stack(offsets).astype(jnp.int32), *(self.state[name] for name, *_ in order))
+        )(jnp.stack(offsets).astype(jnp.int32), *pieces)
 
 
 class GatherVectors:
@@ -193,8 +224,12 @@
             self.state = self.state + self.grid.flip_z(self.state, bit)
 
 
-def split_kernel(rows, core, left, right, own, other):
-    total = by_columns(left[...], right[...]).astype(bf16)
+def split_kernel(rows, core, left, right, own, other, turned):
+    @pl.when(pl.program_id(1) == 0)
+    def turn():
+        turned[...] = left[...].T
+
+    total = jnp.dot(turned[...], right[...], preferred_element_type=f32).astype(bf16)
     first = core[0] == 0
 
     def put(order):
@@ -206,7 +241,7 @@
                 own[0, i, j, 0] = jnp.where(first, low, high)
                 other[0, i, j, 0] = jnp.where(first, high, low)
 
-    z = pl.program_id(1)
+    z = pl.program_id(0)
     pl.when(z < 2)(lambda: put(True))
     pl.when(z >= 2)(lambda: put(False))
 
@@ -220,22 +255,23 @@
         if not self.staged:
             self.state = by_columns(left, right)
             return
-        tile = min(width, 2**18 // (8 * rows))
+        tile = min(width, 1024 if rows <= 32 else 512)
         part = jax.ShapeDtypeStruct((2, 2, 2, 2, rows, width), bf16)
         block = pl.BlockSpec(
-            (1, 2, 2, 1, rows, tile), lambda n, z, core: (z // 2, 0, 0, z % 2, 0, n)
+            (1, 2, 2, 1, rows, tile), lambda z, n, core: (z // 2, 0, 0, z % 2, 0, n)
         )
         self.state = pl.pallas_call(
             functools.partial(split_kernel, rows),
             out_shape=(part, part),
             grid_spec=pltpu.PrefetchScalarGridSpec(
                 num_scalar_prefetch=1,
-                grid=(width // tile, 4),
+                grid=(4, width // tile),
                 in_specs=[
-                    pl.BlockSpec((count, 8 * rows), lambda n, z, core: (0, z)),
-                    pl.BlockSpec((count, tile), lambda n, z, core: (0, n)),
+                    pl.BlockSpec((count, 8 * rows), lambda z, n, core: (0, z)),
+                    pl.BlockSpec((count, tile), lambda z, n, core: (0, n)),
                 ],
                 out_specs=[block, block],
+                scratch_shapes=[pltpu.VMEM((8 * rows, count), bf16)],
             ),
             compiler_params=pltpu.CompilerParams(vmem_limit_bytes=32 * 2**20),
             cost_estimate=pl.CostEstimate(
@@ -254,8 +290,8 @@
     def first(self):
         if self.staged:
             grid, (own, more) = self.grid, self.state
-            ka, sa = halves(own[0], more[0], grid.x)
-            kb, sb = halves(own[1], more[1], grid.y)
+            ka, sa = halves(own, more, grid.x, (0,))
+            kb, sb = halves(own, more, grid.y, (1,))
             self.state = (ka, grid.over_x(sa), kb, grid.over_y(sb))
 
     def second(self):
@@ -551,20 +587,19 @@
     ).astype(jnp.int32)
 
     w1.along_z()
-    live["rows"] = swap(tokens)
+    live["rows"], live["up"] = swap(tokens), swap(cotangent)
+    step("w1", "rows", "up", "small", "w2")
+    w1.first_whole()
+    w2.beside_z()
     small.over_x()
-    step("w1", "rows", "small", "w2")
-    w1.first()
-    w2.near_z()
-    small.over_z(1)
     step("w1", "w2", "small")
     w1.second()
-    w2.far_z()
+    w2.across_z()
+    small.over_z(1)
+    step("w1", "w2", "small", "w3")
+    w1.last()
+    w2.first()
     small.over_z(2)
-    step("w1", "small", "w3")
-    w1.last()
-    w3.near_z()
-    live["up"] = swap(cotangent)
     packed = small.state
     gain1, shift1, b_query, b_value, b_out, gain2, shift2, b_fc2 = (
         packed[:, i].reshape(width).astype(f32) for i in range(8)
@@ -572,16 +607,17 @@
     b_fc1 = packed[:, 8:].reshape(hidden_width).astype(f32)
     inputs = live["rows"].astype(f32)
     live["normed"] = layer_norm(inputs, gain1, shift1).astype(bf16)
-    step("w1", "w2", "w3", "normed", "up")
-    w2.first()
+    step("w1", "normed", "w3")
+    w3.near_z()
     (full_qkv,) = w1.place()
     b_qkv = jnp.concatenate([b_query, jnp.zeros_like(b_query), b_value])
     normed = live["normed"]
     live["mixed"] = (jnp.dot(normed, full_qkv, preferred_element_type=f32) + b_qkv).astype(bf16)
-    step("mixed", "w3")
-    w3.far_z()
+    step("mixed", "w3", "w2")
+    w2.first_rest()
     live["other"] = grid.over_core(live["mixed"][:, width:])
     step("mixed", "other")
+    w3.far_z()
     low, low_lse = attend(info, starts, live["mixed"], live["other"], 0, 2)
     live["low"] = low
     step("low", "other", "mixed", "w2")
@@ -601,15 +637,17 @@
     live["normed2"] = layer_norm(middle, gain2, shift2).astype(bf16)
     live["hidden"] = jnp.dot(live["normed2"], full_fc1, preferred_element_type=f32) + b_fc1
     step("hidden", "normed2", "middle", "w3")
-    w3.second()
+    w3.first_rest()
     normed2, middle, upstream = live["normed2"], live["middle"], live["up"]
     live["active"] = smooth_gate(live["hidden"]).astype(bf16)
     live["fc2"] = Scatter(grid, live["active"], upstream)
     step("fc2", "active", "hidden", "w3")
+    w3.second()
+    live["fc2"].core()
+    step("fc2", "hidden", "w3")
 
     w3.last()
-    live["fc2"].core()
-    step("w3", "fc2", "hidden")
+    step("w3", "hidden")
     live["fc2"].first()
     (full_fc2,) = w3.place()
     grad_out = upstream.astype(f32)
@@ -618,14 +656,13 @@
     grad_hidden = gate_pull(by_rows(upstream, full_fc2))[0].astype(bf16)
     live["grad_hidden"] = grad_hidden
     grad_bias_fc1 = jnp.sum(grad_hidden.astype(f32), axis=0)
-    step("grad_hidden")
+    step("grad_hidden", "fc2")
+    live["fc2"].second()
     grad_hidden = live["grad_hidden"]
     live["fc1"] = Scatter(grid, normed2, grad_hidden)
-    step("fc1", "grad_hidden", "fc2")
-    live["fc2"].second()
+    live["up2"] = by_rows(grad_hidden, full_fc1)
+    step("fc1", "up2", "fc2")
     live["fc1"].core()
-    live["up2"] = by_rows(live["grad_hidden"], full_fc1)
-    step("fc1", "up2")
     grad_mid_norm, grad_gain2, grad_shift2 = norm_back(middle, gain2, shift2, live["up2"])
     grad_middle = grad_out + grad_mid_norm
     grad_branch = grad_middle.astype(bf16)
@@ -636,50 +673,32 @@
     live["fc2"].far_z()
     live["fc1"].first()
     live["out"].core()
-    parts = [
-        attend_back(
-            info, starts, live["mixed"], live["other"], live["low"], low_lse,
-            live["grad_attended"], 0, 2,
-        )
-    ]
-    live["part"] = parts[0]
-    step("part", "grad_attended", "out", "fc1", "fc2")
-    parts[0] = live["part"]
+    live["part"] = attend_back(
+        info, starts, live["mixed"], live["other"], attended,
+        jnp.concatenate([low_lse, high_lse]), live["grad_attended"], 0, 1,
+    )
+    step("part", "out", "fc1", "fc2", "active")
+    dq, dkv, dkv_other = live["part"]
     live["fc2"].near_z()
-    live["fc1"].second()
-    live["back"] = grid.over_core(parts[0][2])
-    parts.append(
-        attend_back(
-            info, starts, live["mixed"], live["other"], live["high"], high_lse,
-            live["grad_attended"], 1, 2,
-        )
-    )
-    live["part"] = parts[1]
-    step("part", "back", "fc1", "fc2", "out", "active")
-    parts[1] = live["part"]
-    live["fc1"].far_z()
     live["out"].first()
-    live["back2"] = grid.over_core(parts[1][2])
+    live["back"] = grid.over_core(dkv_other)
     result = middle + jnp.dot(live["active"], full_fc2, preferred_element_type=f32) + b_fc2
     live["output"] = result.astype(bf16)
-    step("back", "back2", "output", "out")
+    step("back", "output", "out", "fc2", "fc1")
+    live["fc1"].second()
+    dk, dv = both(dkv, live["back"])
+    grad_mixed = jnp.concatenate([dq, dk, dv], axis=1)
+    live["grad_mixed"] = grad_mixed
+    live["qkv"] = Scatter(grid, normed, grad_mixed)
+    step("qkv", "grad_mixed", "fc1", "out", "output")
+    live["qkv"].core()
     live["out"].second()
     output = swap_back(live["output"])
-    dkv = [both(p[1], live[n]) for p, n in zip(parts, ("back", "back2"))]
-    grad_mixed = jnp.concatenate(
-        [p[0] for p in parts] + [d[0] for d in dkv] + [d[1] for d in dkv], axis=1
-    )
-    live["grad_mixed"] = grad_mixed
-    live["qkv"] = Scatter(grid, normed, grad_mixed)
-    step("qkv", "grad_mixed", "fc1", "out")
-    live["qkv"].core()
-    live["fc1"].near_z()
-    live["out"].far_z()
-    grad_mixed = live["grad_mixed"]
-    live["up1"] = by_rows(grad_mixed, full_qkv)
+    live["up1"] = by_rows(live["grad_mixed"], full_qkv)
     step("qkv", "up1", "grad_mixed", "out")
     live["qkv"].first()
-    live["out"].near_z()
+    live["fc1"].far_z()
+    live["out"].far_z()
     grad_mixed = live["grad_mixed"]
     grad_bias_query = jnp.sum(grad_mixed[:, :width].astype(f32), axis=0)
     grad_bias_value = jnp.sum(grad_mixed[:, 2 * width :].astype(f32), axis=0)
@@ -699,16 +718,18 @@
         ),
     )
     live["sums"] = sums
-    step("sums", "grad_tokens", "out")
-    grad_tokens = swap_back(live["grad_tokens"])
+    step("sums", "grad_tokens")
     sums.add(grid.over_core)
     sums.add(grid.over_x)
-    step("sums", "qkv")
+    step("sums", "qkv", "grad_tokens", "fc1", "out")
     live["qkv"].second()
+    live["fc1"].near_z()
+    live["out"].near_z()
     sums.add(grid.over_y)
-    step("sums", "qkv")
+    sums.add(lambda v: grid.flip_z(v, 1))
+    step("sums", "qkv", "grad_tokens", "fc1", "out")
     live["qkv"].along_z()
-    sums.add(lambda v: grid.flip_z(v, 1))
+    grad_tokens = swap_back(live["grad_tokens"])
     sums.add(lambda v: grid.flip_z(v, 2))
     sums = sums.state
     grad_qkv, grad_w_out, grad_fc1, grad_fc2 = (

time: 516 us -> 466 us (0.903)
  waiting for transfers between devices: 148 us -> 112 us
  local copies, waits for them, and re-layouts: 61.3 us -> 41.7 us
  matrix products: 37.2 us -> 44.9 us
  Pallas kernels: 104 us -> 97.1 us
  other arithmetic: 80.3 us -> 86.5 us
    ppermute x72 -> x73, waiting for transfers between devices: 148 us -> 112 us  [send(): return lax.ppermute(value, AXES, pairs)]
    slice x13 -> x4, local copies, waits for them, and re-layouts: 13.9 us -> 2.59 us  [the longest x2 2.53 us: first_rest(): state['y'] = [grid.over_y(state['q'][:2])] + state['y']]
    convert_element_type x23 -> x18, other arithmetic: 28.6 us -> 35.7 us  [both(): return (a.astype(f32) + b.astype(f32)).astype(bf16)]
    unnamed x245 -> x218, local copies, waits for them, and re-layouts: 31.8 us -> 24.7 us
    pallas_call x2 -> x1, Pallas kernels: 27.8 us -> 25.9 us  [attend_back(): pl.pallas_call(functools.partial(attend_back_kernel, block), out_shape=(j...]
    ppermute x72 -> x73, starting transfers between devices: 75.8 us -> 75.6 us  [send(): return lax.ppermute(value, AXES, pairs)]
  transfers between devices with their start and end apart: 72 -> 73, of which waited for: 23 -> 21; matrix products, arithmetic and copies ran while one was open for 24% -> 28% of each run, Pallas kernels for 19% -> 21%
where the time goes in v3:
time: 466 us; the launch traced here: 461 us
  waiting for transfers between devices  112 us (24%)
  Pallas kernels  97.1 us (21%)
  other arithmetic  86.5 us (19%)
  starting transfers between devices  75.6 us (16%)
  matrix products  44.9 us (10%)
  local copies, waits for them, and re-layouts  41.7 us (9%)
    ppermute x73, waiting for transfers between devices, send(): return lax.ppermute(value, AXES, pairs)  112 us
    ppermute x73, starting transfers between devices, send(): return lax.ppermute(value, AXES, pairs)  75.6 us
    convert_element_type x18, other arithmetic, both(): return (a.astype(f32) + b.astype(f32)).astype(bf16)  35.7 us
    pallas_call x4, Pallas kernels, __init__(): pl.pallas_call(functools.partial(split_kernel, rows), out_shape=(part, pa...  33.9 us
    pallas_call x1, Pallas kernels, attend_back(): pl.pallas_call(functools.partial(attend_back_kernel, block), out_shape=(j...  25.9 us
    unnamed x218, local copies, waits for them, and re-layouts  24.7 us
    pallas_call x2, Pallas kernels, attend(): pl.pallas_call(functools.partial(attend_kernel, block), out_shape=(jax.Sh...  24.7 us
    dot_general x4, matrix products, by_rows(): lax.dot_general(a, b, (((1,), (1,)), ((), ())), preferred_element_type=f32)  23.4 us
  transfers between devices with their start and end apart: 73, of which 21 were waited for; matrix products, arithmetic and copies ran while one was open for 28% of the time, Pallas kernels for 21%

profile of v3, /device:TPU:0, one launch (start us, length us, event | category | flops | bytes accessed | tf_op | source)
XLA Modules:
  0.0 460.9 jit_solution(9282442063900651756)
XLA Ops:
  13.7 4.3 collective-permute-done.4
  20.1 9.1 %collective-permute-done.3 = bf16[256,1024]{1,0:T(8,128)(2,1)S(1)} collective-permute-done((bf16[256,1024]{1,0:T(8,128)(2,1)}, bf16[256,1024]{1,0:T(8,128)(2,1)S(1)}, u32[]{:S(2)}, u32[]{:S(2)}) %collective-permute-start.3) | collective-permute-done | bytes 524320 | tf_op jit(solution)/shard_map/ppermute | solution.py:36
  39.7 11.5 %collective-permute-done.9 = bf16[8,12,128]{2,1,0:T(8,128)(2,1)S(1)} collective-permute-done((bf16[8,12,128]{2,1,0:T(8,128)(2,1)S(1)}, bf16[8,12,128]{2,1,0:T(8,128)(2,1)S(1)}, u32[]{:S(2)}, u32[]{:S(2)}) %collective-permute-start.9) | collective-permute-done | bytes 24608 | tf_op jit(solution)/shard_map/ppermute | solution.py:36
  62.3 5.8 %collective-permute-done.14 = bf16[8,12,128]{2,1,0:T(8,128)(2,1)S(1)} collective-permute-done((bf16[8,12,128]{2,1,0:T(8,128)(2,1)S(1)}, bf16[8,12,128]{2,1,0:T(8,128)(2,1)S(1)}, u32[]{:S(2)}, u32[]{:S(2)}) %collective-permute-start.14) | collective-permute-done | bytes 24608 | tf_op jit(solution)/shard_map/ppermute | solution.py:36
  68.1 7.1 %collective-permute-done.13 = bf16[32,5120]{1,0:T(8,128)(2,1)S(1)} collective-permute-done((bf16[32,5120]{1,0:T(8,128)(2,1)S(1)}, bf16[32,5120]{1,0:T(8,128)(2,1)S(1)}, u32[]{:S(2)}, u32[]{:S(2)}) %collective-permute-start.13) | collective-permute-done | bytes 327712 | tf_op jit(solution)/shard_map/ppermute | solution.py:36
  83.8 7.0 %place.3 = bf16[1024,3072]{1,0:T(8,128)(2,1)S(1)} custom-call(s32[32]{0:T(128)S(1)} %stack.349.offsets, bf16[4,32,3072]{2,1,0:T(8,128)(2,1)S(1)} %pad_maximum_fusion.9.refs_0_, bf16[4,32,3072]{2,1,0:T(8,128)(2,1)S(1)} %collective-permute-done.5.refs_1_, bf16[4,32,3072]{2,1,0:T(8,128)(2,1)S(1)} %collective-permute-done.6.refs_2_, ...), custom_call_target="tpu_custom_call" | custom-call | bytes 12582912 | tf_op jit(solution)/shard_map/place/pallas_call | solution.py:194
  90.9 3.7 add_convert_fusion.q.k.v
  102.4 12.3 %attend.2 = (bf16[512,512]{1,0:T(8,128)(2,1)S(1)}, f32[4,4,256]{2,1,0:T(4,128)S(1)}) custom-call(s32[5]{0:T(128)S(1)} %concatenate.67.info, s32[2,256]{1,0:T(2,128)S(1)} %select_reduce_fusion.starts, bf16[512,3072]{1,0:T(8,128)(2,1)S(1)} %add_convert_fusion.q.k.v, bf16[512,3072]{1,0:T(8,128)(2,1)S(1)} %add_convert_fusion.q.k.v, ...), custom_call_target="tpu_custom_call" | custom-call | flops 1073741824 | bytes 3145728 | tf_op jit(solution)/shard_map/attend/pallas_call | solution.py:470
  124.9 12.4 %attend.3 = (bf16[512,512]{1,0:T(8,128)(2,1)S(1)}, f32[4,4,256]{2,1,0:T(4,128)S(1)}) custom-call(s32[5]{0:T(128)S(1)} %concatenate.67.info, s32[2,256]{1,0:T(2,128)S(1)} %select_reduce_fusion.starts, bf16[512,3072]{1,0:T(8,128)(2,1)S(1)} %add_convert_fusion.q.k.v, bf16[512,3072]{1,0:T(8,128)(2,1)S(1)} %add_convert_fusion.q.k.v, ...), custom_call_target="tpu_custom_call" | custom-call | flops 1073741824 | bytes 3145728 | tf_op jit(solution)/shard_map/attend/pallas_call | solution.py:470
  137.3 11.0 %collective-permute-done.26 = bf16[2,128,1024]{2,1,0:T(8,128)(2,1)S(1)} collective-permute-done((bf16[2,128,1024]{2,1,0:T(8,128)(2,1)S(1)}, bf16[2,128,1024]{2,1,0:T(8,128)(2,1)S(1)}, u32[]{:S(2)}, u32[]{:S(2)}) %collective-permute-start.26) | collective-permute-done | bytes 524320 | tf_op jit(solution)/shard_map/ppermute | solution.py:36
  159.1 6.8 %broadcast_add_fusion = f32[512,4096]{1,0:T(8,128)} fusion(f32[4096]{0:T(1024)S(1)} %convert.10, bf16[512,1024]{1,0:T(8,128)(2,1)S(1)} %add_convert_fusion.12.left, bf16[1024,4096]{1,0:T(8,128)(2,1)S(1)} %get-tuple-element.306), kind=kOutput, calls=%fused_computation.21 | convolution fusion | flops 4297064448 | bytes 17842176 | tf_op jit(solution)/shard_map/dot_general | solution.py:638
  168.0 4.8 %fusion.14.left = bf16[512,4096]{1,0:T(8,128)(2,1)S(1)} fusion(f32[512,4096]{1,0:T(8,128)} %broadcast_add_fusion), kind=kLoop, calls=%fused_computation.17 | loop fusion | flops 18874368 | bytes 12582912 | tf_op jit(solution)/shard_map/convert_element_type | solution.py:642
  172.8 9.3 %grad_split.4 = (bf16[2,2,2,2,128,1024]{5,4,3,2,1,0:T(8,128)(2,1)S(1)}, bf16[2,2,2,2,128,1024]{5,4,3,2,1,0:T(8,128)(2,1)S(1)}) custom-call(s32[1]{0:T(128)} %bitcast.core, bf16[512,4096]{1,0:T(8,128)(2,1)S(1)} %fusion.14.left, bf16[512,1024]{1,0:T(8,128)(2,1)S(1)} %copy-done.5), custom_call_target="tpu_custom_call" | custom-call | flops 4294967296 | bytes 13631488 | tf_op jit(solution)/shard_map/grad_split/pallas_call | solution.py:263
  186.8 12.2 %collective-permute-done.33.refs_5_ = bf16[2,128,1024]{2,1,0:T(8,128)(2,1)S(1)} collective-permute-done((bf16[2,128,1024]{2,1,0:T(8,128)(2,1)S(1)}, bf16[2,128,1024]{2,1,0:T(8,128)(2,1)S(1)}, u32[]{:S(2)}, u32[]{:S(2)}) %collective-permute-start.33) | collective-permute-done | bytes 524320 | tf_op jit(solution)/shard_map/ppermute | solution.py:36
  206.2 6.7 %fusion.31 = (bf16[2,2,128,1024]{3,2,1,0:T(8,128)(2,1)S(1)}, bf16[2,2,128,1024]{3,2,1,0:T(8,128)(2,1)S(1)}, bf16[2,2,128,1024]{3,2,1,0:T(8,128)(2,1)}, bf16[2,2,128,1024]{3,2,1,0:T(8,128)(2,1)S(1)}) fusion(bf16[2,2,2,2,128,1024]{5,4,3,2,1,0:T(8,128)(2,1)} %copy-done.60, s32[]{:T(128)S(6)} %select_n.366, bf16[2,2,2,2,128,1024]{5,4,3,2,1,0:T(8,128)(2,1)} %copy-done.13, ...), kind=kLoop, calls=%fused_computation.80 | loop fusion | flops 8388608 | bytes 12582928 | tf_op jit(solution)/shard_map/convert_element_type | solution.py:62
  217.1 7.1 %fusion.97 = f32[512,4096]{1,0:T(8,128)} fusion(bf16[512,1024]{1,0:T(8,128)(2,1)S(1)} %copy-done.6, bf16[4096,1024]{1,0:T(8,128)(2,1)S(1)} %place.5), kind=kOutput, calls=%fused_computation.261 | convolution fusion | flops 4294967296 | bytes 17825792 | tf_op jit(solution)/shard_map/dot_general | solution.py:359
  224.2 9.4 %convert_reduce_fusion = (f32[4096]{0:T(1024)S(1)}, bf16[512,4096]{1,0:T(8,128)(2,1)S(1)}) fusion(f32[512,4096]{1,0:T(8,128)} %broadcast_add_fusion, f32[512,4096]{1,0:T(8,128)} %fusion.97), kind=kLoop, calls=%fused_computation.18 | loop fusion | flops 46133248 | bytes 20987904 | tf_op jit(solution)/shard_map/reduce_sum | solution.py:658
  233.7 5.1 %collective-permute-done.37 = bf16[2,2,128,1024]{3,2,1,0:T(8,128)(2,1)S(1)} collective-permute-done((bf16[2,2,128,1024]{3,2,1,0:T(8,128)(2,1)}, bf16[2,2,128,1024]{3,2,1,0:T(8,128)(2,1)S(1)}, u32[]{:S(2)}, u32[]{:S(2)}) %collective-permute-start.37) | collective-permute-done | bytes 1048608 | tf_op jit(solution)/shard_map/ppermute | solution.py:36
  243.2 8.3 %fusion.98 = f32[512,1024]{1,0:T(8,128)} fusion(bf16[512,4096]{1,0:T(8,128)(2,1)S(1)} %get-tuple-element.345.right, bf16[1024,4096]{1,0:T(8,128)(2,1)} %copy-done.48), kind=kOutput, calls=%fused_computation.262 | convolution fusion | flops 4294967296 | bytes 14680064 | tf_op jit(solution)/shard_map/dot_general | solution.py:359
  251.4 11.8 %grad_split.5 = (bf16[2,2,2,2,32,4096]{5,4,3,2,1,0:T(8,128)(2,1)S(1)}, bf16[2,2,2,2,32,4096]{5,4,3,2,1,0:T(8,128)(2,1)}) custom-call(s32[1]{0:T(128)} %bitcast.core, bf16[512,1024]{1,0:T(8,128)(2,1)S(1)} %copy-done.44, bf16[512,4096]{1,0:T(8,128)(2,1)S(1)} %get-tuple-element.345.right), custom_call_target="tpu_custom_call" | custom-call | flops 4294967296 | bytes 13631488 | tf_op jit(solution)/shard_map/grad_split/pallas_call | solution.py:263
  269.3 3.1 multiply_reduce_fusion
  275.1 3.4 grad_split.6
  281.5 5.3 %fusion.35 = (bf16[2,2,32,4096]{3,2,1,0:T(8,128)(2,1)}, bf16[2,2,32,4096]{3,2,1,0:T(8,128)(2,1)}, bf16[2,2,32,4096]{3,2,1,0:T(8,128)(2,1)}, bf16[2,2,32,4096]{3,2,1,0:T(8,128)(2,1)}) fusion(bf16[2,2,2,2,32,4096]{5,4,3,2,1,0:T(8,128)(2,1)} %collective-permute-done.41, s32[]{:T(128)S(6)} %select_n.366, bf16[2,2,2,2,32,4096]{5,4,3,2,1,0:T(8,128)(2,1)S(1)} %copy-done.17, ...), kind=kLoop, calls=%fused_computation.84 | loop fusion | flops 8388608 | bytes 12582928 | tf_op jit(solution)/shard_map/convert_element_type | solution.py:62
  291.8 25.9 %attend_back.1 = (bf16[512,1024]{1,0:T(8,128)(2,1)S(1)}, f32[2,512,1024]{2,1,0:T(8,128)S(1)}, bf16[2,512,1024]{2,1,0:T(8,128)(2,1)}) custom-call(s32[5]{0:T(128)S(1)} %concatenate.67.info, s32[2,256]{1,0:T(2,128)S(1)} %select_reduce_fusion.starts, bf16[512,3072]{1,0:T(8,128)(2,1)S(1)} %add_convert_fusion.q.k.v, bf16[512,3072]{1,0:T(8,128)(2,1)S(1)} %add_convert_fusion.q.k.v, ...), custom_call_target="tpu_custom_call" | custom-call | flops 5368709120 | bytes 14680064 | tf_op jit(solution)/shard_map/attend_back/pallas_call | solution.py:496
  323.0 4.0 collective-permute-start.49
  331.4 9.7 %add_convert_fusion.3 = bf16[512,1024]{1,0:T(8,128)(2,1)} fusion(f32[512,1024]{1,0:T(8,128)} %copy-done.52, f32[1024]{0:T(1024)S(1)} %bitcast.300, bf16[512,4096]{1,0:T(8,128)(2,1)S(1)} %copy-done.12, bf16[4096,1024]{1,0:T(8,128)(2,1)} %copy-done.9), kind=kOutput, calls=%fused_computation.48 | convolution fusion | flops 4296540160 | bytes 15732736 | tf_op jit(solution)/shard_map/dot_general | solution.py:685
  351.8 9.3 %grad_split.7 = (bf16[2,2,2,2,32,3072]{5,4,3,2,1,0:T(8,128)(2,1)S(1)}, bf16[2,2,2,2,32,3072]{5,4,3,2,1,0:T(8,128)(2,1)}) custom-call(s32[1]{0:T(128)} %bitcast.core, bf16[512,1024]{1,0:T(8,128)(2,1)S(1)} %copy-done.39, bf16[512,3072]{1,0:T(8,128)(2,1)S(1)} %pad_maximum_fusion.right), custom_call_target="tpu_custom_call" | custom-call | flops 3221225472 | bytes 10485760 | tf_op jit(solution)/shard_map/grad_split/pallas_call | solution.py:263
  370.9 5.7 %fusion.99 = f32[512,1024]{1,0:T(8,128)S(1)} fusion(bf16[512,3072]{1,0:T(8,128)(2,1)S(1)} %pad_maximum_fusion.right, bf16[1024,3072]{1,0:T(8,128)(2,1)} %copy-done.10), kind=kOutput, calls=%fused_computation.263 | convolution fusion | flops 3221225472 | bytes 11534336 | tf_op jit(solution)/shard_map/dot_general | solution.py:359
  377.0 4.5 fusion.39
  395.1 7.1 %collective-permute-done.57 = f32[12,1024]{1,0:T(8,128)S(1)} collective-permute-done((f32[12,1024]{1,0:T(8,128)S(1)}, f32[12,1024]{1,0:T(8,128)S(1)}, u32[]{:S(2)}, u32[]{:S(2)}) %collective-permute-start.57) | collective-permute-done | bytes 49184 | tf_op jit(solution)/shard_map/ppermute | solution.py:36
  418.6 7.2 %collective-permute-done.62 = f32[12,1024]{1,0:T(8,128)S(1)} collective-permute-done((f32[12,1024]{1,0:T(8,128)S(1)}, f32[12,1024]{1,0:T(8,128)S(1)}, u32[]{:S(2)}, u32[]{:S(2)}) %collective-permute-start.62) | collective-permute-done | bytes 49184 | tf_op jit(solution)/shard_map/ppermute | solution.py:36
  438.2 15.0 %collective-permute-done.69 = f32[12,1024]{1,0:T(8,128)S(1)} collective-permute-done((f32[12,1024]{1,0:T(8,128)S(1)}, f32[12,1024]{1,0:T(8,128)S(1)}, u32[]{:S(2)}, u32[]{:S(2)}) %collective-permute-start.69) | collective-permute-done | bytes 49184 | tf_op jit(solution)/shard_map/ppermute | solution.py:36
  (473 shorter events, 192.1 us)
Async XLA Ops:
  6.3 23.0 %collective-permute-start.3 = (bf16[256,1024]{1,0:T(8,128)(2,1)}, bf16[256,1024]{1,0:T(8,128)(2,1)S(1)}, u32[]{:S(2)}, u32[]{:S(2)}) collective-permute-start(bf16[256,1024]{1,0:T(8,128)(2,1)} %get-tuple-element.540), channel_id=1, source_target_pairs={{0,3},{1,2},{2,1},{3,0},{4,7},{5,6},{6,5},{7,4},{8,11},{9,10},{10,... | collective-permute-start | bytes 1572872 | tf_op jit(solution)/shard_map/ppermute | solution.py:36
  7.2 23.1 %collective-permute-start = (bf16[32,3072]{1,0:T(8,128)(2,1)S(1)}, bf16[32,3072]{1,0:T(8,128)(2,1)S(1)}, u32[]{:S(2)}, u32[]{:S(2)}) collective-permute-start(bf16[32,3072]{1,0:T(8,128)(2,1)S(1)} %constant_dynamic-slice_fusion.13), channel_id=1, source_target_pairs={{0,8},{1,9},{2,10},{3,11},{4,12},{5,13},{6,14},{7,15},{8,16},{9,17... | collective-permute-start | bytes 589832 | tf_op jit(solution)/shard_map/ppermute | solution.py:36
  9.6 20.7 %collective-permute-start.1 = (bf16[32,3072]{1,0:T(8,128)(2,1)S(1)}, bf16[32,3072]{1,0:T(8,128)(2,1)S(1)}, u32[]{:S(2)}, u32[]{:S(2)}) collective-permute-start(bf16[32,3072]{1,0:T(8,128)(2,1)S(1)} %constant_dynamic-slice_fusion.13), channel_id=1, source_target_pairs={{0,16},{1,17},{2,18},{3,19},{4,20},{5,21},{6,22},{7,23},{8,24},{9,... | collective-permute-start | bytes 589832 | tf_op jit(solution)/shard_map/ppermute | solution.py:36
  30.4 22.4 %collective-permute-start.5 = (bf16[4,32,3072]{2,1,0:T(8,128)(2,1)S(1)}, bf16[4,32,3072]{2,1,0:T(8,128)(2,1)S(1)}, u32[]{:S(2)}, u32[]{:S(2)}) collective-permute-start(bf16[4,32,3072]{2,1,0:T(8,128)(2,1)S(1)} %pad_maximum_fusion.9.refs_0_), channel_id=1, source_target_pairs={{0,4},{1,5},{2,6},{3,7},{4,0},{5,1},{6,2},{7,3},{8,12},{9,13},{10,... | collective-permute-start | bytes 2359304 | tf_op jit(solution)/shard_map/ppermute | solution.py:36
  32.8 20.8 %collective-permute-start.6 = (bf16[4,32,3072]{2,1,0:T(8,128)(2,1)S(1)}, bf16[4,32,3072]{2,1,0:T(8,128)(2,1)S(1)}, u32[]{:S(2)}, u32[]{:S(2)}) collective-permute-start(bf16[4,32,3072]{2,1,0:T(8,128)(2,1)S(1)} %pad_maximum_fusion.9.refs_0_), channel_id=1, source_target_pairs={{0,2},{1,3},{2,0},{3,1},{4,6},{5,7},{6,4},{7,5},{8,10},{9,11},{10,... | collective-permute-start | bytes 2359304 | tf_op jit(solution)/shard_map/ppermute | solution.py:36
  55.2 19.9 %collective-permute-start.12 = (bf16[12,32,3072]{2,1,0:T(8,128)(2,1)}, bf16[12,32,3072]{2,1,0:T(8,128)(2,1)}, u32[]{:S(2)}, u32[]{:S(2)}) collective-permute-start(bf16[12,32,3072]{2,1,0:T(8,128)(2,1)} %pad_maximum_fusion.1), channel_id=1, source_target_pairs={{0,1},{1,0},{2,3},{3,2},{4,5},{5,4},{6,7},{7,6},{8,9},{9,8},{10,11... | collective-permute-start | bytes 7077896 | tf_op jit(solution)/shard_map/ppermute | solution.py:36
  55.7 19.5 %collective-permute-start.10 = (bf16[2,32,3072]{2,1,0:T(8,128)(2,1)S(1)}, bf16[2,32,3072]{2,1,0:T(8,128)(2,1)S(1)}, u32[]{:S(2)}, u32[]{:S(2)}) collective-permute-start(bf16[2,32,3072]{2,1,0:T(8,128)(2,1)S(1)} %slice.97), channel_id=1, source_target_pairs={{0,2},{1,3},{2,0},{3,1},{4,6},{5,7},{6,4},{7,5},{8,10},{9,11},{10,... | collective-permute-start | bytes 1179656 | tf_op jit(solution)/shard_map/ppermute | solution.py:36
  56.2 19.0 %collective-permute-start.11 = (bf16[2,32,3072]{2,1,0:T(8,128)(2,1)S(1)}, bf16[2,32,3072]{2,1,0:T(8,128)(2,1)S(1)}, u32[]{:S(2)}, u32[]{:S(2)}) collective-permute-start(bf16[2,32,3072]{2,1,0:T(8,128)(2,1)S(1)} %slice.98), channel_id=1, source_target_pairs={{0,4},{1,5},{2,6},{3,7},{4,0},{5,1},{6,2},{7,3},{8,12},{9,13},{10,... | collective-permute-start | bytes 1179656 | tf_op jit(solution)/shard_map/ppermute | solution.py:36
  120.0 28.2 %collective-permute-start.25 = (bf16[12,32,5120]{2,1,0:T(8,128)(2,1)S(1)}, bf16[12,32,5120]{2,1,0:T(8,128)(2,1)S(1)}, u32[]{:S(2)}, u32[]{:S(2)}) collective-permute-start(bf16[12,32,5120]{2,1,0:T(8,128)(2,1)S(1)} %constant_dynamic-update-slice_fusion.2), channel_id=1, source_target_pairs={{0,1},{1,0},{2,3},{3,2},{4,5},{5,4},{6,7},{7,6},{8,9},{9,8},{10,11... | collective-permute-start | bytes 11796488 | tf_op jit(solution)/shard_map/ppermute | solution.py:36
  120.1 28.2 %collective-permute-start.23 = (bf16[2,32,5120]{2,1,0:T(8,128)(2,1)S(1)}, bf16[2,32,5120]{2,1,0:T(8,128)(2,1)S(1)}, u32[]{:S(2)}, u32[]{:S(2)}) collective-permute-start(bf16[2,32,5120]{2,1,0:T(8,128)(2,1)S(1)} %copy-done.25), channel_id=1, source_target_pairs={{0,2},{1,3},{2,0},{3,1},{4,6},{5,7},{6,4},{7,5},{8,10},{9,11},{10,... | collective-permute-start | bytes 1966088 | tf_op jit(solution)/shard_map/ppermute | solution.py:36
  121.8 26.5 %collective-permute-start.24 = (bf16[2,32,5120]{2,1,0:T(8,128)(2,1)S(1)}, bf16[2,32,5120]{2,1,0:T(8,128)(2,1)S(1)}, u32[]{:S(2)}, u32[]{:S(2)}) collective-permute-start(bf16[2,32,5120]{2,1,0:T(8,128)(2,1)S(1)} %copy-done.23), channel_id=1, source_target_pairs={{0,4},{1,5},{2,6},{3,7},{4,0},{5,1},{6,2},{7,3},{8,12},{9,13},{10,... | collective-permute-start | bytes 1966088 | tf_op jit(solution)/shard_map/ppermute | solution.py:36
  122.3 25.9 %collective-permute-start.26 = (bf16[2,128,1024]{2,1,0:T(8,128)(2,1)S(1)}, bf16[2,128,1024]{2,1,0:T(8,128)(2,1)S(1)}, u32[]{:S(2)}, u32[]{:S(2)}) collective-permute-start(bf16[2,128,1024]{2,1,0:T(8,128)(2,1)S(1)} %pad_maximum_fusion.13), channel_id=1, source_target_pairs={{0,16},{1,17},{2,18},{3,19},{4,20},{5,21},{6,22},{7,23},{8,24},{9,... | collective-permute-start | bytes 1572872 | tf_op jit(solution)/shard_map/ppermute | solution.py:36
  182.2 19.8 %collective-permute-start.32 = (bf16[2,2,2,2,128,1024]{5,4,3,2,1,0:T(8,128)(2,1)S(1)}, bf16[2,2,2,2,128,1024]{5,4,3,2,1,0:T(8,128)(2,1)S(1)}, u32[]{:S(2)}, u32[]{:S(2)}) collective-permute-start(bf16[2,2,2,2,128,1024]{5,4,3,2,1,0:T(8,128)(2,1)S(1)} %get-tuple-element.317), channel_id=1, source_target_pairs={{0,1},{1,0},{2,3},{3,2},{4,5},{5,4},{6,7},{7,6},{8,9},{9,8},{10,11... | collective-permute-start | bytes 12582920 | tf_op jit(solution)/shard_map/ppermute | solution.py:36
  213.0 25.8 %collective-permute-start.37 = (bf16[2,2,128,1024]{3,2,1,0:T(8,128)(2,1)}, bf16[2,2,128,1024]{3,2,1,0:T(8,128)(2,1)S(1)}, u32[]{:S(2)}, u32[]{:S(2)}) collective-permute-start(bf16[2,2,128,1024]{3,2,1,0:T(8,128)(2,1)} %get-tuple-element.495), channel_id=1, source_target_pairs={{0,4},{1,5},{2,6},{3,7},{4,0},{5,1},{6,2},{7,3},{8,12},{9,13},{10,... | collective-permute-start | bytes 3145736 | tf_op jit(solution)/shard_map/ppermute | solution.py:36
  213.5 25.3 %collective-permute-start.38 = (bf16[2,2,128,1024]{3,2,1,0:T(8,128)(2,1)S(1)}, bf16[2,2,128,1024]{3,2,1,0:T(8,128)(2,1)S(1)}, u32[]{:S(2)}, u32[]{:S(2)}) collective-permute-start(bf16[2,2,128,1024]{3,2,1,0:T(8,128)(2,1)S(1)} %get-tuple-element.493), channel_id=1, source_target_pairs={{0,2},{1,3},{2,0},{3,1},{4,6},{5,7},{6,4},{7,5},{8,10},{9,11},{10,... | collective-permute-start | bytes 3145736 | tf_op jit(solution)/shard_map/ppermute | solution.py:36
  240.0 25.3 %collective-permute-start.40 = (bf16[2,128,1024]{2,1,0:T(8,128)(2,1)S(1)}, bf16[2,128,1024]{2,1,0:T(8,128)(2,1)}, u32[]{:S(2)}, u32[]{:S(2)}) collective-permute-start(bf16[2,128,1024]{2,1,0:T(8,128)(2,1)S(1)} %get-tuple-element.515), channel_id=1, source_target_pairs={{0,4},{1,5},{2,6},{3,7},{4,0},{5,1},{6,2},{7,3},{8,12},{9,13},{10,... | collective-permute-start | bytes 1572872 | tf_op jit(solution)/shard_map/ppermute | solution.py:36
  242.7 22.6 %collective-permute-start.39 = (bf16[2,128,1024]{2,1,0:T(8,128)(2,1)S(1)}, bf16[2,128,1024]{2,1,0:T(8,128)(2,1)}, u32[]{:S(2)}, u32[]{:S(2)}) collective-permute-start(bf16[2,128,1024]{2,1,0:T(8,128)(2,1)S(1)} %get-tuple-element.517), channel_id=1, source_target_pairs={{0,2},{1,3},{2,0},{3,1},{4,6},{5,7},{6,4},{7,5},{8,10},{9,11},{10,... | collective-permute-start | bytes 1572872 | tf_op jit(solution)/shard_map/ppermute | solution.py:36
  286.8 33.9 %collective-permute-start.43 = (bf16[2,2,32,4096]{3,2,1,0:T(8,128)(2,1)}, bf16[2,2,32,4096]{3,2,1,0:T(8,128)(2,1)}, u32[]{:S(2)}, u32[]{:S(2)}) collective-permute-start(bf16[2,2,32,4096]{3,2,1,0:T(8,128)(2,1)} %get-tuple-element.491), channel_id=1, source_target_pairs={{0,4},{1,5},{2,6},{3,7},{4,0},{5,1},{6,2},{7,3},{8,12},{9,13},{10,... | collective-permute-start | bytes 3145736 | tf_op jit(solution)/shard_map/ppermute | solution.py:36
  287.7 33.0 %collective-permute-start.44 = (bf16[2,2,32,4096]{3,2,1,0:T(8,128)(2,1)}, bf16[2,2,32,4096]{3,2,1,0:T(8,128)(2,1)}, u32[]{:S(2)}, u32[]{:S(2)}) collective-permute-start(bf16[2,2,32,4096]{3,2,1,0:T(8,128)(2,1)} %get-tuple-element.489), channel_id=1, source_target_pairs={{0,2},{1,3},{2,0},{3,1},{4,6},{5,7},{6,4},{7,5},{8,10},{9,11},{10,... | collective-permute-start | bytes 3145736 | tf_op jit(solution)/shard_map/ppermute | solution.py:36
  288.9 31.9 %collective-permute-start.42 = (bf16[2,2,2,2,32,1024]{5,4,3,2,1,0:T(8,128)(2,1)}, bf16[2,2,2,2,32,1024]{5,4,3,2,1,0:T(8,128)(2,1)}, u32[]{:S(2)}, u32[]{:S(2)}) collective-permute-start(bf16[2,2,2,2,32,1024]{5,4,3,2,1,0:T(8,128)(2,1)} %get-tuple-element.367), channel_id=1, source_target_pairs={{0,1},{1,0},{2,3},{3,2},{4,5},{5,4},{6,7},{7,6},{8,9},{9,8},{10,11... | collective-permute-start | bytes 3145736 | tf_op jit(solution)/shard_map/ppermute | solution.py:36
  291.8 28.9 %collective-permute-start.45 = (bf16[2,128,1024]{2,1,0:T(8,128)(2,1)S(1)}, bf16[2,128,1024]{2,1,0:T(8,128)(2,1)S(1)}, u32[]{:S(2)}, u32[]{:S(2)}) collective-permute-start(bf16[2,128,1024]{2,1,0:T(8,128)(2,1)S(1)} %get-tuple-element.513), channel_id=1, source_target_pairs={{0,16},{1,17},{2,18},{3,19},{4,20},{5,21},{6,22},{7,23},{8,24},{9,... | collective-permute-start | bytes 1572872 | tf_op jit(solution)/shard_map/ppermute | solution.py:36
  321.5 19.6 %collective-permute-start.46 = (bf16[2,512,1024]{2,1,0:T(8,128)(2,1)}, bf16[2,512,1024]{2,1,0:T(8,128)(2,1)S(1)}, u32[]{:S(2)}, u32[]{:S(2)}) collective-permute-start(bf16[2,512,1024]{2,1,0:T(8,128)(2,1)} %get-tuple-element.377), channel_id=1, source_target_pairs={{0,1},{1,0},{2,3},{3,2},{4,5},{5,4},{6,7},{7,6},{8,9},{9,8},{10,11... | collective-permute-start | bytes 6291464 | tf_op jit(solution)/shard_map/ppermute | solution.py:36
  343.7 19.0 %collective-permute-start.51 = (bf16[2,32,4096]{2,1,0:T(8,128)(2,1)S(1)}, bf16[2,32,4096]{2,1,0:T(8,128)(2,1)}, u32[]{:S(2)}, u32[]{:S(2)}) collective-permute-start(bf16[2,32,4096]{2,1,0:T(8,128)(2,1)S(1)} %get-tuple-element.503), channel_id=1, source_target_pairs={{0,4},{1,5},{2,6},{3,7},{4,0},{5,1},{6,2},{7,3},{8,12},{9,13},{10,... | collective-permute-start | bytes 1572872 | tf_op jit(solution)/shard_map/ppermute | solution.py:36
  376.6 28.6 %collective-permute-start.60 = (bf16[2,32,4096]{2,1,0:T(8,128)(2,1)}, bf16[2,32,4096]{2,1,0:T(8,128)(2,1)}, u32[]{:S(2)}, u32[]{:S(2)}) collective-permute-start(bf16[2,32,4096]{2,1,0:T(8,128)(2,1)} %get-tuple-element.501), channel_id=1, source_target_pairs={{0,16},{1,17},{2,18},{3,19},{4,20},{5,21},{6,22},{7,23},{8,24},{9,... | collective-permute-start | bytes 1572872 | tf_op jit(solution)/shard_map/ppermute | solution.py:36
  381.5 26.3 %collective-permute-start.58 = (bf16[2,2,32,3072]{3,2,1,0:T(8,128)(2,1)}, bf16[2,2,32,3072]{3,2,1,0:T(8,128)(2,1)}, u32[]{:S(2)}, u32[]{:S(2)}) collective-permute-start(bf16[2,2,32,3072]{3,2,1,0:T(8,128)(2,1)} %get-tuple-element.499), channel_id=1, source_target_pairs={{0,4},{1,5},{2,6},{3,7},{4,0},{5,1},{6,2},{7,3},{8,12},{9,13},{10,... | collective-permute-start | bytes 2359304 | tf_op jit(solution)/shard_map/ppermute | solution.py:36
  382.6 25.2 %collective-permute-start.59 = (bf16[2,2,32,3072]{3,2,1,0:T(8,128)(2,1)}, bf16[2,2,32,3072]{3,2,1,0:T(8,128)(2,1)}, u32[]{:S(2)}, u32[]{:S(2)}) collective-permute-start(bf16[2,2,32,3072]{3,2,1,0:T(8,128)(2,1)} %get-tuple-element.497), channel_id=1, source_target_pairs={{0,2},{1,3},{2,0},{3,1},{4,6},{5,7},{6,4},{7,5},{8,10},{9,11},{10,... | collective-permute-start | bytes 2359304 | tf_op jit(solution)/shard_map/ppermute | solution.py:36
  409.0 21.1 %collective-permute-start.66 = (bf16[32,4096]{1,0:T(8,128)(2,1)S(1)}, bf16[32,4096]{1,0:T(8,128)(2,1)S(1)}, u32[]{:S(2)}, u32[]{:S(2)}) collective-permute-start(bf16[32,4096]{1,0:T(8,128)(2,1)S(1)} %get-tuple-element.529), channel_id=1, source_target_pairs={{0,8},{1,9},{2,10},{3,11},{4,12},{5,13},{6,14},{7,15},{8,0},{9,1},... | collective-permute-start | bytes 786440 | tf_op jit(solution)/shard_map/ppermute | solution.py:36
  410.4 19.8 %collective-permute-start.65 = (bf16[2,32,3072]{2,1,0:T(8,128)(2,1)S(1)}, bf16[2,32,3072]{2,1,0:T(8,128)(2,1)S(1)}, u32[]{:S(2)}, u32[]{:S(2)}) collective-permute-start(bf16[2,32,3072]{2,1,0:T(8,128)(2,1)S(1)} %get-tuple-element.521), channel_id=1, source_target_pairs={{0,4},{1,5},{2,6},{3,7},{4,0},{5,1},{6,2},{7,3},{8,12},{9,13},{10,... | collective-permute-start | bytes 1179656 | tf_op jit(solution)/shard_map/ppermute | solution.py:36
  430.6 27.8 %collective-permute-start.70 = (bf16[32,3072]{1,0:T(8,128)(2,1)S(1)}, bf16[32,3072]{1,0:T(8,128)(2,1)S(1)}, u32[]{:S(2)}, u32[]{:S(2)}) collective-permute-start(bf16[32,3072]{1,0:T(8,128)(2,1)S(1)} %get-tuple-element.541), channel_id=1, source_target_pairs={{0,8},{1,9},{2,10},{3,11},{4,12},{5,13},{6,14},{7,15},{8,16},{9,17... | collective-permute-start | bytes 589832 | tf_op jit(solution)/shard_map/ppermute | solution.py:36
  432.4 26.1 %collective-permute-start.71 = (bf16[32,3072]{1,0:T(8,128)(2,1)S(1)}, bf16[32,3072]{1,0:T(8,128)(2,1)S(1)}, u32[]{:S(2)}, u32[]{:S(2)}) collective-permute-start(bf16[32,3072]{1,0:T(8,128)(2,1)S(1)} %get-tuple-element.542), channel_id=1, source_target_pairs={{0,16},{1,17},{2,18},{3,19},{4,20},{5,21},{6,22},{7,23},{8,24},{9,... | collective-permute-start | bytes 589832 | tf_op jit(solution)/shard_map/ppermute | solution.py:36
  433.4 25.1 %collective-permute-start.72 = (bf16[32,3072]{1,0:T(8,128)(2,1)S(1)}, bf16[32,3072]{1,0:T(8,128)(2,1)S(1)}, u32[]{:S(2)}, u32[]{:S(2)}) collective-permute-start(bf16[32,3072]{1,0:T(8,128)(2,1)S(1)} %get-tuple-element.543), channel_id=1, source_target_pairs={{0,24},{1,25},{2,26},{3,27},{4,28},{5,29},{6,30},{7,31},{8,0},{9,1... | collective-permute-start | bytes 589832 | tf_op jit(solution)/shard_map/ppermute | solution.py:36
  436.6 22.8 %collective-permute-start.68 = (bf16[256,1024]{1,0:T(8,128)(2,1)S(1)}, bf16[256,1024]{1,0:T(8,128)(2,1)S(1)}, u32[]{:S(2)}, u32[]{:S(2)}) collective-permute-start(bf16[256,1024]{1,0:T(8,128)(2,1)S(1)} %slice.118), channel_id=1, source_target_pairs={{0,3},{1,2},{2,1},{3,0},{4,7},{5,6},{6,5},{7,4},{8,11},{9,10},{10,... | collective-permute-start | bytes 1572872 | tf_op jit(solution)/shard_map/ppermute | solution.py:36
  (145 other events, 1212.0 us)

commit v4 on v3

--- a/solution.py
+++ b/solution.py
@@ -229,7 +229,9 @@
     def turn():
         turned[...] = left[...].T
 
-    total = jnp.dot(turned[...], right[...], preferred_element_type=f32).astype(bf16)
+    tile = own.shape[-1]
+    columns = pl.ds(pl.multiple_of(pl.program_id(1) * tile, tile), tile)
+    total = jnp.dot(turned[...], right[:, columns], preferred_element_type=f32).astype(bf16)
     first = core[0] == 0
 
     def put(order):
@@ -268,7 +270,7 @@
                 grid=(4, width // tile),
                 in_specs=[
                     pl.BlockSpec((count, 8 * rows), lambda z, n, core: (0, z)),
-                    pl.BlockSpec((count, tile), lambda z, n, core: (0, n)),
+                    pl.BlockSpec((count, width), lambda z, n, core: (0, 0)),
                 ],
                 out_specs=[block, block],
                 scratch_shapes=[pltpu.VMEM((8 * rows, count), bf16)],
@@ -551,8 +553,9 @@
         mine, theirs = pick(values, y, 0)[0], pick(values, 1 - y, 0)[0]
         return jnp.concatenate([mine, grid.over_yc(theirs)], axis=0)
 
-    def swap_back(values):
-        mine, back = values[:block], grid.over_yc(values[block:])
+    def swap_back(values, back=None):
+        mine = values[:block]
+        back = grid.over_yc(values[block:]) if back is None else back
         first, second = jnp.where(y == 0, mine, back), jnp.where(y == 0, back, mine)
         return jnp.stack([first, second])[:, None]
 
@@ -608,7 +611,7 @@
     inputs = live["rows"].astype(f32)
     live["normed"] = layer_norm(inputs, gain1, shift1).astype(bf16)
     step("w1", "normed", "w3")
-    w3.near_z()
+    w3.beside_z()
     (full_qkv,) = w1.place()
     b_qkv = jnp.concatenate([b_query, jnp.zeros_like(b_query), b_value])
     normed = live["normed"]
@@ -617,10 +620,10 @@
     w2.first_rest()
     live["other"] = grid.over_core(live["mixed"][:, width:])
     step("mixed", "other")
-    w3.far_z()
+    w3.across_z()
     low, low_lse = attend(info, starts, live["mixed"], live["other"], 0, 2)
     live["low"] = low
-    step("low", "other", "mixed", "w2")
+    step("low", "other", "mixed", "w2", "w3")
     w2.second()
     high, high_lse = attend(info, starts, live["mixed"], live["other"], 1, 2)
     live["high"] = high
@@ -693,9 +696,10 @@
     step("qkv", "grad_mixed", "fc1", "out", "output")
     live["qkv"].core()
     live["out"].second()
-    output = swap_back(live["output"])
+    live["back"] = grid.over_yc(live["output"][block:])
     live["up1"] = by_rows(live["grad_mixed"], full_qkv)
-    step("qkv", "up1", "grad_mixed", "out")
+    step("qkv", "up1", "grad_mixed", "out", "back")
+    output = swap_back(live["output"], live["back"])
     live["qkv"].first()
     live["fc1"].far_z()
     live["out"].far_z()
@@ -727,10 +731,10 @@
     live["out"].near_z()
     sums.add(grid.over_y)
     sums.add(lambda v: grid.flip_z(v, 1))
+    sums.add(lambda v: grid.flip_z(v, 2))
     step("sums", "qkv", "grad_tokens", "fc1", "out")
     live["qkv"].along_z()
     grad_tokens = swap_back(live["grad_tokens"])
-    sums.add(lambda v: grid.flip_z(v, 2))
     sums = sums.state
     grad_qkv, grad_w_out, grad_fc1, grad_fc2 = (
         live[n].result() for n in ("qkv", "out", "fc1", "fc2")

time: 466 us -> 456 us (0.979)
  waiting for transfers between devices: 112 us -> 102 us
    ppermute x73 -> x74, waiting for transfers between devices: 112 us -> 102 us  [send(): return lax.ppermute(value, AXES, pairs)]
    ppermute x73 -> x74, starting transfers between devices: 75.6 us -> 74 us  [send(): return lax.ppermute(value, AXES, pairs)]
    unnamed x218 -> x228, local copies, waits for them, and re-layouts: 24.7 us -> 24.9 us
  transfers between devices with their start and end apart: 73 -> 74, of which waited for: 21 -> 23; matrix products, arithmetic and copies ran while one was open for 28% -> 30% of each run, Pallas kernels for 21% -> 21%
where the time goes in v4:
time: 456 us; the launch traced here: 452 us
  waiting for transfers between devices  102 us (22%)
  Pallas kernels  95.8 us (21%)
  other arithmetic  88.4 us (19%)
  starting transfers between devices  74 us (16%)
  matrix products  44.9 us (10%)
  local copies, waits for them, and re-layouts  43.6 us (10%)
    ppermute x74, waiting for transfers between devices, send(): return lax.ppermute(value, AXES, pairs)  102 us
    ppermute x74, starting transfers between devices, send(): return lax.ppermute(value, AXES, pairs)  74 us
    convert_element_type x18, other arithmetic, both(): return (a.astype(f32) + b.astype(f32)).astype(bf16)  36 us
    pallas_call x4, Pallas kernels, __init__(): pl.pallas_call(functools.partial(split_kernel, rows), out_shape=(part, pa...  32.4 us
    pallas_call x1, Pallas kernels, attend_back(): pl.pallas_call(functools.partial(attend_back_kernel, block), out_shape=(j...  25.9 us
    unnamed x228, local copies, waits for them, and re-layouts  24.9 us
    pallas_call x2, Pallas kernels, attend(): pl.pallas_call(functools.partial(attend_kernel, block), out_shape=(jax.Sh...  24.7 us
    dot_general x4, matrix products, by_rows(): lax.dot_general(a, b, (((1,), (1,)), ((), ())), preferred_element_type=f32)  23.3 us
  transfers between devices with their start and end apart: 74, of which 23 were waited for; matrix products, arithmetic and copies ran while one was open for 30% of the time, Pallas kernels for 21%

profile of v4, /device:TPU:0, one launch (start us, length us, event | category | flops | bytes accessed | tf_op | source)
XLA Modules:
  0.0 451.5 jit_solution(8133766875776921296)
XLA Ops:
  13.7 4.3 collective-permute-done.4
  20.1 9.2 %collective-permute-done.3 = bf16[256,1024]{1,0:T(8,128)(2,1)S(1)} collective-permute-done((bf16[256,1024]{1,0:T(8,128)(2,1)}, bf16[256,1024]{1,0:T(8,128)(2,1)S(1)}, u32[]{:S(2)}, u32[]{:S(2)}) %collective-permute-start.3) | collective-permute-done | bytes 524320 | tf_op jit(solution)/shard_map/ppermute | solution.py:36
  39.7 11.5 %collective-permute-done.9 = bf16[8,12,128]{2,1,0:T(8,128)(2,1)S(1)} collective-permute-done((bf16[8,12,128]{2,1,0:T(8,128)(2,1)S(1)}, bf16[8,12,128]{2,1,0:T(8,128)(2,1)S(1)}, u32[]{:S(2)}, u32[]{:S(2)}) %collective-permute-start.9) | collective-permute-done | bytes 24608 | tf_op jit(solution)/shard_map/ppermute | solution.py:36
  62.3 5.8 %collective-permute-done.14 = bf16[8,12,128]{2,1,0:T(8,128)(2,1)S(1)} collective-permute-done((bf16[8,12,128]{2,1,0:T(8,128)(2,1)S(1)}, bf16[8,12,128]{2,1,0:T(8,128)(2,1)S(1)}, u32[]{:S(2)}, u32[]{:S(2)}) %collective-permute-start.14) | collective-permute-done | bytes 24608 | tf_op jit(solution)/shard_map/ppermute | solution.py:36
  68.1 7.1 %collective-permute-done.13 = bf16[32,5120]{1,0:T(8,128)(2,1)S(1)} collective-permute-done((bf16[32,5120]{1,0:T(8,128)(2,1)S(1)}, bf16[32,5120]{1,0:T(8,128)(2,1)S(1)}, u32[]{:S(2)}, u32[]{:S(2)}) %collective-permute-start.13) | collective-permute-done | bytes 327712 | tf_op jit(solution)/shard_map/ppermute | solution.py:36
  86.9 7.0 %place.3 = bf16[1024,3072]{1,0:T(8,128)(2,1)S(1)} custom-call(s32[32]{0:T(128)S(1)} %stack.359.offsets, bf16[4,32,3072]{2,1,0:T(8,128)(2,1)S(1)} %pad_maximum_fusion.9.refs_0_, bf16[4,32,3072]{2,1,0:T(8,128)(2,1)S(1)} %collective-permute-done.5.refs_1_, bf16[4,32,3072]{2,1,0:T(8,128)(2,1)S(1)} %collective-permute-done.6.refs_2_, ...), custom_call_target="tpu_custom_call" | custom-call | bytes 12582912 | tf_op jit(solution)/shard_map/place/pallas_call | solution.py:194
  94.0 3.7 add_convert_fusion.q.k.v
  104.5 12.3 %attend.2 = (bf16[512,512]{1,0:T(8,128)(2,1)S(1)}, f32[4,4,256]{2,1,0:T(4,128)S(1)}) custom-call(s32[5]{0:T(128)S(1)} %concatenate.66.info, s32[2,256]{1,0:T(2,128)S(1)} %select_reduce_fusion.starts, bf16[512,3072]{1,0:T(8,128)(2,1)S(1)} %add_convert_fusion.q.k.v, bf16[512,3072]{1,0:T(8,128)(2,1)S(1)} %add_convert_fusion.q.k.v, ...), custom_call_target="tpu_custom_call" | custom-call | flops 1073741824 | bytes 3145728 | tf_op jit(solution)/shard_map/attend/pallas_call | solution.py:472
  124.4 12.4 %attend.3 = (bf16[512,512]{1,0:T(8,128)(2,1)S(1)}, f32[4,4,256]{2,1,0:T(4,128)S(1)}) custom-call(s32[5]{0:T(128)S(1)} %concatenate.66.info, s32[2,256]{1,0:T(2,128)S(1)} %select_reduce_fusion.starts, bf16[512,3072]{1,0:T(8,128)(2,1)S(1)} %add_convert_fusion.q.k.v, bf16[512,3072]{1,0:T(8,128)(2,1)S(1)} %add_convert_fusion.q.k.v, ...), custom_call_target="tpu_custom_call" | custom-call | flops 1073741824 | bytes 3145728 | tf_op jit(solution)/shard_map/attend/pallas_call | solution.py:472
  146.5 3.1 place.4
  154.2 6.8 %broadcast_add_fusion = f32[512,4096]{1,0:T(8,128)} fusion(f32[4096]{0:T(1024)S(1)} %convert.10, bf16[512,1024]{1,0:T(8,128)(2,1)S(1)} %add_convert_fusion.12.left, bf16[1024,4096]{1,0:T(8,128)(2,1)S(1)} %get-tuple-element.319), kind=kOutput, calls=%fused_computation.21 | convolution fusion | flops 4297064448 | bytes 17842176 | tf_op jit(solution)/shard_map/dot_general | solution.py:641
  162.8 4.8 %fusion.14.left = bf16[512,4096]{1,0:T(8,128)(2,1)S(1)} fusion(f32[512,4096]{1,0:T(8,128)} %broadcast_add_fusion), kind=kLoop, calls=%fused_computation.17 | loop fusion | flops 18874368 | bytes 12582912 | tf_op jit(solution)/shard_map/convert_element_type | solution.py:645
  167.6 9.1 %grad_split.4 = (bf16[2,2,2,2,128,1024]{5,4,3,2,1,0:T(8,128)(2,1)S(1)}, bf16[2,2,2,2,128,1024]{5,4,3,2,1,0:T(8,128)(2,1)S(1)}) custom-call(s32[1]{0:T(128)} %bitcast.core, bf16[512,4096]{1,0:T(8,128)(2,1)S(1)} %fusion.14.left, bf16[512,1024]{1,0:T(8,128)(2,1)S(1)} %copy-done.5), custom_call_target="tpu_custom_call" | custom-call | flops 4294967296 | bytes 13631488 | tf_op jit(solution)/shard_map/grad_split/pallas_call | solution.py:265
  181.8 11.7 %collective-permute-done.34.refs_5_ = bf16[2,128,1024]{2,1,0:T(8,128)(2,1)S(1)} collective-permute-done((bf16[2,128,1024]{2,1,0:T(8,128)(2,1)S(1)}, bf16[2,128,1024]{2,1,0:T(8,128)(2,1)S(1)}, u32[]{:S(2)}, u32[]{:S(2)}) %collective-permute-start.34) | collective-permute-done | bytes 524320 | tf_op jit(solution)/shard_map/ppermute | solution.py:36
  200.3 6.7 %fusion.31 = (bf16[2,2,128,1024]{3,2,1,0:T(8,128)(2,1)S(1)}, bf16[2,2,128,1024]{3,2,1,0:T(8,128)(2,1)S(1)}, bf16[2,2,128,1024]{3,2,1,0:T(8,128)(2,1)}, bf16[2,2,128,1024]{3,2,1,0:T(8,128)(2,1)S(1)}) fusion(bf16[2,2,2,2,128,1024]{5,4,3,2,1,0:T(8,128)(2,1)} %copy-done.60, s32[]{:T(128)S(6)} %select_n.430, bf16[2,2,2,2,128,1024]{5,4,3,2,1,0:T(8,128)(2,1)} %copy-done.13, ...), kind=kLoop, calls=%fused_computation.80 | loop fusion | flops 8388608 | bytes 12582928 | tf_op jit(solution)/shard_map/convert_element_type | solution.py:62
  211.7 7.0 %fusion.97 = f32[512,4096]{1,0:T(8,128)} fusion(bf16[512,1024]{1,0:T(8,128)(2,1)S(1)} %copy-done.6, bf16[4096,1024]{1,0:T(8,128)(2,1)S(1)} %place.5), kind=kOutput, calls=%fused_computation.262 | convolution fusion | flops 4294967296 | bytes 17825792 | tf_op jit(solution)/shard_map/dot_general | solution.py:361
  218.8 9.4 %convert_reduce_fusion = (f32[4096]{0:T(1024)S(1)}, bf16[512,4096]{1,0:T(8,128)(2,1)S(1)}) fusion(f32[512,4096]{1,0:T(8,128)} %broadcast_add_fusion, f32[512,4096]{1,0:T(8,128)} %fusion.97), kind=kLoop, calls=%fused_computation.18 | loop fusion | flops 46133248 | bytes 20987904 | tf_op jit(solution)/shard_map/reduce_sum | solution.py:661
  228.2 4.6 %collective-permute-done.38 = bf16[2,2,128,1024]{3,2,1,0:T(8,128)(2,1)S(1)} collective-permute-done((bf16[2,2,128,1024]{3,2,1,0:T(8,128)(2,1)}, bf16[2,2,128,1024]{3,2,1,0:T(8,128)(2,1)S(1)}, u32[]{:S(2)}, u32[]{:S(2)}) %collective-permute-start.38) | collective-permute-done | bytes 1048608 | tf_op jit(solution)/shard_map/ppermute | solution.py:36
  237.7 8.3 %fusion.98 = f32[512,1024]{1,0:T(8,128)} fusion(bf16[512,4096]{1,0:T(8,128)(2,1)S(1)} %get-tuple-element.360.right, bf16[1024,4096]{1,0:T(8,128)(2,1)} %copy-done.48), kind=kOutput, calls=%fused_computation.263 | convolution fusion | flops 4294967296 | bytes 14680064 | tf_op jit(solution)/shard_map/dot_general | solution.py:361
  246.0 11.2 %grad_split.5 = (bf16[2,2,2,2,32,4096]{5,4,3,2,1,0:T(8,128)(2,1)S(1)}, bf16[2,2,2,2,32,4096]{5,4,3,2,1,0:T(8,128)(2,1)}) custom-call(s32[1]{0:T(128)} %bitcast.core, bf16[512,1024]{1,0:T(8,128)(2,1)S(1)} %copy-done.44, bf16[512,4096]{1,0:T(8,128)(2,1)S(1)} %get-tuple-element.360.right), custom_call_target="tpu_custom_call" | custom-call | flops 4294967296 | bytes 13631488 | tf_op jit(solution)/shard_map/grad_split/pallas_call | solution.py:265
  263.3 3.1 multiply_reduce_fusion
  269.1 3.4 grad_split.6
  275.5 5.2 %fusion.35 = (bf16[2,2,32,4096]{3,2,1,0:T(8,128)(2,1)}, bf16[2,2,32,4096]{3,2,1,0:T(8,128)(2,1)}, bf16[2,2,32,4096]{3,2,1,0:T(8,128)(2,1)}, bf16[2,2,32,4096]{3,2,1,0:T(8,128)(2,1)}) fusion(bf16[2,2,2,2,32,4096]{5,4,3,2,1,0:T(8,128)(2,1)} %collective-permute-done.42, s32[]{:T(128)S(6)} %select_n.430, bf16[2,2,2,2,32,4096]{5,4,3,2,1,0:T(8,128)(2,1)S(1)} %copy-done.17, ...), kind=kLoop, calls=%fused_computation.84 | loop fusion | flops 8388608 | bytes 12582928 | tf_op jit(solution)/shard_map/convert_element_type | solution.py:62
  286.2 25.9 %attend_back.1 = (bf16[512,1024]{1,0:T(8,128)(2,1)S(1)}, f32[2,512,1024]{2,1,0:T(8,128)S(1)}, bf16[2,512,1024]{2,1,0:T(8,128)(2,1)}) custom-call(s32[5]{0:T(128)S(1)} %concatenate.66.info, s32[2,256]{1,0:T(2,128)S(1)} %select_reduce_fusion.starts, bf16[512,3072]{1,0:T(8,128)(2,1)S(1)} %add_convert_fusion.q.k.v, bf16[512,3072]{1,0:T(8,128)(2,1)S(1)} %add_convert_fusion.q.k.v, ...), custom_call_target="tpu_custom_call" | custom-call | flops 5368709120 | bytes 14680064 | tf_op jit(solution)/shard_map/attend_back/pallas_call | solution.py:498
  326.2 9.7 %add_convert_fusion.3 = bf16[512,1024]{1,0:T(8,128)(2,1)} fusion(f32[512,1024]{1,0:T(8,128)} %copy-done.52, f32[1024]{0:T(1024)S(1)} %bitcast.304, bf16[512,4096]{1,0:T(8,128)(2,1)S(1)} %copy-done.12, bf16[4096,1024]{1,0:T(8,128)(2,1)} %copy-done.9), kind=kOutput, calls=%fused_computation.48 | convolution fusion | flops 4296540160 | bytes 15732736 | tf_op jit(solution)/shard_map/dot_general | solution.py:688
  345.1 8.7 %grad_split.7 = (bf16[2,2,2,2,32,3072]{5,4,3,2,1,0:T(8,128)(2,1)S(1)}, bf16[2,2,2,2,32,3072]{5,4,3,2,1,0:T(8,128)(2,1)}) custom-call(s32[1]{0:T(128)} %bitcast.core, bf16[512,1024]{1,0:T(8,128)(2,1)S(1)} %copy-done.39, bf16[512,3072]{1,0:T(8,128)(2,1)S(1)} %pad_maximum_fusion.right), custom_call_target="tpu_custom_call" | custom-call | flops 3221225472 | bytes 10485760 | tf_op jit(solution)/shard_map/grad_split/pallas_call | solution.py:265
  366.0 5.7 %fusion.99 = f32[512,1024]{1,0:T(8,128)S(1)} fusion(bf16[512,3072]{1,0:T(8,128)(2,1)S(1)} %pad_maximum_fusion.right, bf16[1024,3072]{1,0:T(8,128)(2,1)} %copy-done.10), kind=kOutput, calls=%fused_computation.264 | convolution fusion | flops 3221225472 | bytes 11534336 | tf_op jit(solution)/shard_map/dot_general | solution.py:361
  372.7 4.9 %collective-permute-done.56 = bf16[256,1024]{1,0:T(8,128)(2,1)S(1)} collective-permute-done((bf16[256,1024]{1,0:T(8,128)(2,1)S(1)}, bf16[256,1024]{1,0:T(8,128)(2,1)S(1)}, u32[]{:S(2)}, u32[]{:S(2)}) %collective-permute-start.56) | collective-permute-done | bytes 524320 | tf_op jit(solution)/shard_map/ppermute | solution.py:36
  377.7 4.6 %fusion.39 = (bf16[2,2,32,3072]{3,2,1,0:T(8,128)(2,1)}, bf16[2,2,32,3072]{3,2,1,0:T(8,128)(2,1)}, bf16[2,2,32,3072]{3,2,1,0:T(8,128)(2,1)}, bf16[2,2,32,3072]{3,2,1,0:T(8,128)(2,1)}) fusion(bf16[2,2,2,2,32,3072]{5,4,3,2,1,0:T(8,128)(2,1)} %collective-permute-done.53, s32[]{:T(128)S(6)} %select_n.430, bf16[2,2,2,2,32,3072]{5,4,3,2,1,0:T(8,128)(2,1)S(1)} %copy-done.21, ...), kind=kLoop, calls=%fused_computation.109 | loop fusion | flops 6291456 | bytes 9437200 | tf_op jit(solution)/shard_map/convert_element_type | solution.py:62
  392.9 10.8 %collective-permute-done.58 = f32[12,1024]{1,0:T(8,128)S(1)} collective-permute-done((f32[12,1024]{1,0:T(8,128)S(1)}, f32[12,1024]{1,0:T(8,128)S(1)}, u32[]{:S(2)}, u32[]{:S(2)}) %collective-permute-start.58) | collective-permute-done | bytes 49184 | tf_op jit(solution)/shard_map/ppermute | solution.py:36
  410.5 9.9 %collective-permute-done.63 = f32[12,1024]{1,0:T(8,128)S(1)} collective-permute-done((f32[12,1024]{1,0:T(8,128)S(1)}, f32[12,1024]{1,0:T(8,128)S(1)}, u32[]{:S(2)}, u32[]{:S(2)}) %collective-permute-start.63) | collective-permute-done | bytes 49184 | tf_op jit(solution)/shard_map/ppermute | solution.py:36
  445.8 4.1 collective-permute-done.70
  (486 shorter events, 196.3 us)
Async XLA Ops:
  6.3 23.0 %collective-permute-start.3 = (bf16[256,1024]{1,0:T(8,128)(2,1)}, bf16[256,1024]{1,0:T(8,128)(2,1)S(1)}, u32[]{:S(2)}, u32[]{:S(2)}) collective-permute-start(bf16[256,1024]{1,0:T(8,128)(2,1)} %get-tuple-element.556), channel_id=1, source_target_pairs={{0,3},{1,2},{2,1},{3,0},{4,7},{5,6},{6,5},{7,4},{8,11},{9,10},{10,... | collective-permute-start | bytes 1572872 | tf_op jit(solution)/shard_map/ppermute | solution.py:36
  7.2 23.1 %collective-permute-start = (bf16[32,3072]{1,0:T(8,128)(2,1)S(1)}, bf16[32,3072]{1,0:T(8,128)(2,1)S(1)}, u32[]{:S(2)}, u32[]{:S(2)}) collective-permute-start(bf16[32,3072]{1,0:T(8,128)(2,1)S(1)} %constant_dynamic-slice_fusion.13), channel_id=1, source_target_pairs={{0,8},{1,9},{2,10},{3,11},{4,12},{5,13},{6,14},{7,15},{8,16},{9,17... | collective-permute-start | bytes 589832 | tf_op jit(solution)/shard_map/ppermute | solution.py:36
  9.6 20.7 %collective-permute-start.1 = (bf16[32,3072]{1,0:T(8,128)(2,1)S(1)}, bf16[32,3072]{1,0:T(8,128)(2,1)S(1)}, u32[]{:S(2)}, u32[]{:S(2)}) collective-permute-start(bf16[32,3072]{1,0:T(8,128)(2,1)S(1)} %constant_dynamic-slice_fusion.13), channel_id=1, source_target_pairs={{0,16},{1,17},{2,18},{3,19},{4,20},{5,21},{6,22},{7,23},{8,24},{9,... | collective-permute-start | bytes 589832 | tf_op jit(solution)/shard_map/ppermute | solution.py:36
  12.2 18.1 %collective-permute-start.2 = (bf16[32,3072]{1,0:T(8,128)(2,1)S(1)}, bf16[32,3072]{1,0:T(8,128)(2,1)S(1)}, u32[]{:S(2)}, u32[]{:S(2)}) collective-permute-start(bf16[32,3072]{1,0:T(8,128)(2,1)S(1)} %constant_dynamic-slice_fusion.13), channel_id=1, source_target_pairs={{0,24},{1,25},{2,26},{3,27},{4,28},{5,29},{6,30},{7,31},{8,0},{9,1... | collective-permute-start | bytes 589832 | tf_op jit(solution)/shard_map/ppermute | solution.py:36
  30.4 22.4 %collective-permute-start.5 = (bf16[4,32,3072]{2,1,0:T(8,128)(2,1)S(1)}, bf16[4,32,3072]{2,1,0:T(8,128)(2,1)S(1)}, u32[]{:S(2)}, u32[]{:S(2)}) collective-permute-start(bf16[4,32,3072]{2,1,0:T(8,128)(2,1)S(1)} %pad_maximum_fusion.9.refs_0_), channel_id=1, source_target_pairs={{0,4},{1,5},{2,6},{3,7},{4,0},{5,1},{6,2},{7,3},{8,12},{9,13},{10,... | collective-permute-start | bytes 2359304 | tf_op jit(solution)/shard_map/ppermute | solution.py:36
  32.7 20.8 %collective-permute-start.6 = (bf16[4,32,3072]{2,1,0:T(8,128)(2,1)S(1)}, bf16[4,32,3072]{2,1,0:T(8,128)(2,1)S(1)}, u32[]{:S(2)}, u32[]{:S(2)}) collective-permute-start(bf16[4,32,3072]{2,1,0:T(8,128)(2,1)S(1)} %pad_maximum_fusion.9.refs_0_), channel_id=1, source_target_pairs={{0,2},{1,3},{2,0},{3,1},{4,6},{5,7},{6,4},{7,5},{8,10},{9,11},{10,... | collective-permute-start | bytes 2359304 | tf_op jit(solution)/shard_map/ppermute | solution.py:36
  55.2 19.9 %collective-permute-start.12 = (bf16[12,32,3072]{2,1,0:T(8,128)(2,1)}, bf16[12,32,3072]{2,1,0:T(8,128)(2,1)}, u32[]{:S(2)}, u32[]{:S(2)}) collective-permute-start(bf16[12,32,3072]{2,1,0:T(8,128)(2,1)} %pad_maximum_fusion.1), channel_id=1, source_target_pairs={{0,1},{1,0},{2,3},{3,2},{4,5},{5,4},{6,7},{7,6},{8,9},{9,8},{10,11... | collective-permute-start | bytes 7077896 | tf_op jit(solution)/shard_map/ppermute | solution.py:36
  55.7 19.5 %collective-permute-start.10 = (bf16[2,32,3072]{2,1,0:T(8,128)(2,1)S(1)}, bf16[2,32,3072]{2,1,0:T(8,128)(2,1)S(1)}, u32[]{:S(2)}, u32[]{:S(2)}) collective-permute-start(bf16[2,32,3072]{2,1,0:T(8,128)(2,1)S(1)} %slice.101), channel_id=1, source_target_pairs={{0,2},{1,3},{2,0},{3,1},{4,6},{5,7},{6,4},{7,5},{8,10},{9,11},{10,... | collective-permute-start | bytes 1179656 | tf_op jit(solution)/shard_map/ppermute | solution.py:36
  56.2 19.0 %collective-permute-start.11 = (bf16[2,32,3072]{2,1,0:T(8,128)(2,1)S(1)}, bf16[2,32,3072]{2,1,0:T(8,128)(2,1)S(1)}, u32[]{:S(2)}, u32[]{:S(2)}) collective-permute-start(bf16[2,32,3072]{2,1,0:T(8,128)(2,1)S(1)} %slice.102), channel_id=1, source_target_pairs={{0,4},{1,5},{2,6},{3,7},{4,0},{5,1},{6,2},{7,3},{8,12},{9,13},{10,... | collective-permute-start | bytes 1179656 | tf_op jit(solution)/shard_map/ppermute | solution.py:36
  76.8 20.9 %collective-permute-start.20 = (bf16[2,32,5120]{2,1,0:T(8,128)(2,1)S(1)}, bf16[2,32,5120]{2,1,0:T(8,128)(2,1)S(1)}, u32[]{:S(2)}, u32[]{:S(2)}) collective-permute-start(bf16[2,32,5120]{2,1,0:T(8,128)(2,1)S(1)} %pad_maximum_fusion.12), channel_id=1, source_target_pairs={{0,2},{1,3},{2,0},{3,1},{4,6},{5,7},{6,4},{7,5},{8,10},{9,11},{10,... | collective-permute-start | bytes 1966088 | tf_op jit(solution)/shard_map/ppermute | solution.py:36
  77.5 20.2 %collective-permute-start.19 = (bf16[2,32,5120]{2,1,0:T(8,128)(2,1)S(1)}, bf16[2,32,5120]{2,1,0:T(8,128)(2,1)S(1)}, u32[]{:S(2)}, u32[]{:S(2)}) collective-permute-start(bf16[2,32,5120]{2,1,0:T(8,128)(2,1)S(1)} %pad_maximum_fusion.11), channel_id=1, source_target_pairs={{0,4},{1,5},{2,6},{3,7},{4,0},{5,1},{6,2},{7,3},{8,12},{9,13},{10,... | collective-permute-start | bytes 1966088 | tf_op jit(solution)/shard_map/ppermute | solution.py:36
  122.3 17.9 %collective-permute-start.27 = (bf16[12,32,5120]{2,1,0:T(8,128)(2,1)S(1)}, bf16[12,32,5120]{2,1,0:T(8,128)(2,1)S(1)}, u32[]{:S(2)}, u32[]{:S(2)}) collective-permute-start(bf16[12,32,5120]{2,1,0:T(8,128)(2,1)S(1)} %constant_dynamic-update-slice_fusion.2), channel_id=1, source_target_pairs={{0,1},{1,0},{2,3},{3,2},{4,5},{5,4},{6,7},{7,6},{8,9},{9,8},{10,11... | collective-permute-start | bytes 11796488 | tf_op jit(solution)/shard_map/ppermute | solution.py:36
  141.5 19.6 %collective-permute-start.30 = (bf16[2,128,1024]{2,1,0:T(8,128)(2,1)S(1)}, bf16[2,128,1024]{2,1,0:T(8,128)(2,1)S(1)}, u32[]{:S(2)}, u32[]{:S(2)}) collective-permute-start(bf16[2,128,1024]{2,1,0:T(8,128)(2,1)S(1)} %pad_maximum_fusion.14), channel_id=1, source_target_pairs={{0,2},{1,3},{2,0},{3,1},{4,6},{5,7},{6,4},{7,5},{8,10},{9,11},{10,... | collective-permute-start | bytes 1572872 | tf_op jit(solution)/shard_map/ppermute | solution.py:36
  143.6 17.5 %collective-permute-start.29 = (bf16[2,128,1024]{2,1,0:T(8,128)(2,1)S(1)}, bf16[2,128,1024]{2,1,0:T(8,128)(2,1)S(1)}, u32[]{:S(2)}, u32[]{:S(2)}) collective-permute-start(bf16[2,128,1024]{2,1,0:T(8,128)(2,1)S(1)} %pad_maximum_fusion.13), channel_id=1, source_target_pairs={{0,4},{1,5},{2,6},{3,7},{4,0},{5,1},{6,2},{7,3},{8,12},{9,13},{10,... | collective-permute-start | bytes 1572872 | tf_op jit(solution)/shard_map/ppermute | solution.py:36
  176.8 19.3 %collective-permute-start.33 = (bf16[2,2,2,2,128,1024]{5,4,3,2,1,0:T(8,128)(2,1)S(1)}, bf16[2,2,2,2,128,1024]{5,4,3,2,1,0:T(8,128)(2,1)S(1)}, u32[]{:S(2)}, u32[]{:S(2)}) collective-permute-start(bf16[2,2,2,2,128,1024]{5,4,3,2,1,0:T(8,128)(2,1)S(1)} %get-tuple-element.332), channel_id=1, source_target_pairs={{0,1},{1,0},{2,3},{3,2},{4,5},{5,4},{6,7},{7,6},{8,9},{9,8},{10,11... | collective-permute-start | bytes 12582920 | tf_op jit(solution)/shard_map/ppermute | solution.py:36
  207.0 25.8 %collective-permute-start.38 = (bf16[2,2,128,1024]{3,2,1,0:T(8,128)(2,1)}, bf16[2,2,128,1024]{3,2,1,0:T(8,128)(2,1)S(1)}, u32[]{:S(2)}, u32[]{:S(2)}) collective-permute-start(bf16[2,2,128,1024]{3,2,1,0:T(8,128)(2,1)} %get-tuple-element.511), channel_id=1, source_target_pairs={{0,4},{1,5},{2,6},{3,7},{4,0},{5,1},{6,2},{7,3},{8,12},{9,13},{10,... | collective-permute-start | bytes 3145736 | tf_op jit(solution)/shard_map/ppermute | solution.py:36
  208.5 25.3 %collective-permute-start.39 = (bf16[2,2,128,1024]{3,2,1,0:T(8,128)(2,1)S(1)}, bf16[2,2,128,1024]{3,2,1,0:T(8,128)(2,1)S(1)}, u32[]{:S(2)}, u32[]{:S(2)}) collective-permute-start(bf16[2,2,128,1024]{3,2,1,0:T(8,128)(2,1)S(1)} %get-tuple-element.509), channel_id=1, source_target_pairs={{0,2},{1,3},{2,0},{3,1},{4,6},{5,7},{6,4},{7,5},{8,10},{9,11},{10,... | collective-permute-start | bytes 3145736 | tf_op jit(solution)/shard_map/ppermute | solution.py:36
  235.0 24.2 %collective-permute-start.41 = (bf16[2,128,1024]{2,1,0:T(8,128)(2,1)S(1)}, bf16[2,128,1024]{2,1,0:T(8,128)(2,1)}, u32[]{:S(2)}, u32[]{:S(2)}) collective-permute-start(bf16[2,128,1024]{2,1,0:T(8,128)(2,1)S(1)} %get-tuple-element.531), channel_id=1, source_target_pairs={{0,4},{1,5},{2,6},{3,7},{4,0},{5,1},{6,2},{7,3},{8,12},{9,13},{10,... | collective-permute-start | bytes 1572872 | tf_op jit(solution)/shard_map/ppermute | solution.py:36
  236.7 22.5 %collective-permute-start.40 = (bf16[2,128,1024]{2,1,0:T(8,128)(2,1)S(1)}, bf16[2,128,1024]{2,1,0:T(8,128)(2,1)}, u32[]{:S(2)}, u32[]{:S(2)}) collective-permute-start(bf16[2,128,1024]{2,1,0:T(8,128)(2,1)S(1)} %get-tuple-element.533), channel_id=1, source_target_pairs={{0,2},{1,3},{2,0},{3,1},{4,6},{5,7},{6,4},{7,5},{8,10},{9,11},{10,... | collective-permute-start | bytes 1572872 | tf_op jit(solution)/shard_map/ppermute | solution.py:36
  280.7 34.5 %collective-permute-start.44 = (bf16[2,2,32,4096]{3,2,1,0:T(8,128)(2,1)}, bf16[2,2,32,4096]{3,2,1,0:T(8,128)(2,1)}, u32[]{:S(2)}, u32[]{:S(2)}) collective-permute-start(bf16[2,2,32,4096]{3,2,1,0:T(8,128)(2,1)} %get-tuple-element.507), channel_id=1, source_target_pairs={{0,4},{1,5},{2,6},{3,7},{4,0},{5,1},{6,2},{7,3},{8,12},{9,13},{10,... | collective-permute-start | bytes 3145736 | tf_op jit(solution)/shard_map/ppermute | solution.py:36
  281.7 33.5 %collective-permute-start.45 = (bf16[2,2,32,4096]{3,2,1,0:T(8,128)(2,1)}, bf16[2,2,32,4096]{3,2,1,0:T(8,128)(2,1)}, u32[]{:S(2)}, u32[]{:S(2)}) collective-permute-start(bf16[2,2,32,4096]{3,2,1,0:T(8,128)(2,1)} %get-tuple-element.505), channel_id=1, source_target_pairs={{0,2},{1,3},{2,0},{3,1},{4,6},{5,7},{6,4},{7,5},{8,10},{9,11},{10,... | collective-permute-start | bytes 3145736 | tf_op jit(solution)/shard_map/ppermute | solution.py:36
  283.3 31.9 %collective-permute-start.43 = (bf16[2,2,2,2,32,1024]{5,4,3,2,1,0:T(8,128)(2,1)}, bf16[2,2,2,2,32,1024]{5,4,3,2,1,0:T(8,128)(2,1)}, u32[]{:S(2)}, u32[]{:S(2)}) collective-permute-start(bf16[2,2,2,2,32,1024]{5,4,3,2,1,0:T(8,128)(2,1)} %get-tuple-element.382), channel_id=1, source_target_pairs={{0,1},{1,0},{2,3},{3,2},{4,5},{5,4},{6,7},{7,6},{8,9},{9,8},{10,11... | collective-permute-start | bytes 3145736 | tf_op jit(solution)/shard_map/ppermute | solution.py:36
  286.2 29.0 %collective-permute-start.46 = (bf16[2,128,1024]{2,1,0:T(8,128)(2,1)S(1)}, bf16[2,128,1024]{2,1,0:T(8,128)(2,1)S(1)}, u32[]{:S(2)}, u32[]{:S(2)}) collective-permute-start(bf16[2,128,1024]{2,1,0:T(8,128)(2,1)S(1)} %get-tuple-element.529), channel_id=1, source_target_pairs={{0,16},{1,17},{2,18},{3,19},{4,20},{5,21},{6,22},{7,23},{8,24},{9,... | collective-permute-start | bytes 1572872 | tf_op jit(solution)/shard_map/ppermute | solution.py:36
  316.0 20.0 %collective-permute-start.47 = (bf16[2,512,1024]{2,1,0:T(8,128)(2,1)}, bf16[2,512,1024]{2,1,0:T(8,128)(2,1)S(1)}, u32[]{:S(2)}, u32[]{:S(2)}) collective-permute-start(bf16[2,512,1024]{2,1,0:T(8,128)(2,1)} %get-tuple-element.392), channel_id=1, source_target_pairs={{0,1},{1,0},{2,3},{3,2},{4,5},{5,4},{6,7},{7,6},{8,9},{9,8},{10,11... | collective-permute-start | bytes 6291464 | tf_op jit(solution)/shard_map/ppermute | solution.py:36
  317.5 18.4 %collective-permute-start.50 = (bf16[128,1024]{1,0:T(8,128)(2,1)S(1)}, bf16[128,1024]{1,0:T(8,128)(2,1)S(1)}, u32[]{:S(2)}, u32[]{:S(2)}) collective-permute-start(bf16[128,1024]{1,0:T(8,128)(2,1)S(1)} %get-tuple-element.549), channel_id=1, source_target_pairs={{0,8},{1,9},{2,10},{3,11},{4,12},{5,13},{6,14},{7,15},{8,0},{9,1},... | collective-permute-start | bytes 786440 | tf_op jit(solution)/shard_map/ppermute | solution.py:36
  355.4 22.2 %collective-permute-start.53 = (bf16[2,2,2,2,32,3072]{5,4,3,2,1,0:T(8,128)(2,1)}, bf16[2,2,2,2,32,3072]{5,4,3,2,1,0:T(8,128)(2,1)}, u32[]{:S(2)}, u32[]{:S(2)}) collective-permute-start(bf16[2,2,2,2,32,3072]{5,4,3,2,1,0:T(8,128)(2,1)} %get-tuple-element.416), channel_id=1, source_target_pairs={{0,1},{1,0},{2,3},{3,2},{4,5},{5,4},{6,7},{7,6},{8,9},{9,8},{10,11... | collective-permute-start | bytes 9437192 | tf_op jit(solution)/shard_map/ppermute | solution.py:36
  371.8 32.0 %collective-permute-start.61 = (bf16[2,32,4096]{2,1,0:T(8,128)(2,1)}, bf16[2,32,4096]{2,1,0:T(8,128)(2,1)}, u32[]{:S(2)}, u32[]{:S(2)}) collective-permute-start(bf16[2,32,4096]{2,1,0:T(8,128)(2,1)} %get-tuple-element.517), channel_id=1, source_target_pairs={{0,16},{1,17},{2,18},{3,19},{4,20},{5,21},{6,22},{7,23},{8,24},{9,... | collective-permute-start | bytes 1572872 | tf_op jit(solution)/shard_map/ppermute | solution.py:36
  382.3 21.5 %collective-permute-start.59 = (bf16[2,2,32,3072]{3,2,1,0:T(8,128)(2,1)}, bf16[2,2,32,3072]{3,2,1,0:T(8,128)(2,1)}, u32[]{:S(2)}, u32[]{:S(2)}) collective-permute-start(bf16[2,2,32,3072]{3,2,1,0:T(8,128)(2,1)} %get-tuple-element.515), channel_id=1, source_target_pairs={{0,4},{1,5},{2,6},{3,7},{4,0},{5,1},{6,2},{7,3},{8,12},{9,13},{10,... | collective-permute-start | bytes 2359304 | tf_op jit(solution)/shard_map/ppermute | solution.py:36
  382.9 20.9 %collective-permute-start.60 = (bf16[2,2,32,3072]{3,2,1,0:T(8,128)(2,1)}, bf16[2,2,32,3072]{3,2,1,0:T(8,128)(2,1)}, u32[]{:S(2)}, u32[]{:S(2)}) collective-permute-start(bf16[2,2,32,3072]{3,2,1,0:T(8,128)(2,1)} %get-tuple-element.513), channel_id=1, source_target_pairs={{0,2},{1,3},{2,0},{3,1},{4,6},{5,7},{6,4},{7,5},{8,10},{9,11},{10,... | collective-permute-start | bytes 2359304 | tf_op jit(solution)/shard_map/ppermute | solution.py:36
  405.0 25.1 %collective-permute-start.68 = (bf16[32,4096]{1,0:T(8,128)(2,1)S(1)}, bf16[32,4096]{1,0:T(8,128)(2,1)S(1)}, u32[]{:S(2)}, u32[]{:S(2)}) collective-permute-start(bf16[32,4096]{1,0:T(8,128)(2,1)S(1)} %get-tuple-element.545), channel_id=1, source_target_pairs={{0,8},{1,9},{2,10},{3,11},{4,12},{5,13},{6,14},{7,15},{8,0},{9,1},... | collective-permute-start | bytes 786440 | tf_op jit(solution)/shard_map/ppermute | solution.py:36
  406.5 23.6 %collective-permute-start.67 = (bf16[2,32,3072]{2,1,0:T(8,128)(2,1)S(1)}, bf16[2,32,3072]{2,1,0:T(8,128)(2,1)S(1)}, u32[]{:S(2)}, u32[]{:S(2)}) collective-permute-start(bf16[2,32,3072]{2,1,0:T(8,128)(2,1)S(1)} %get-tuple-element.537), channel_id=1, source_target_pairs={{0,4},{1,5},{2,6},{3,7},{4,0},{5,1},{6,2},{7,3},{8,12},{9,13},{10,... | collective-permute-start | bytes 1179656 | tf_op jit(solution)/shard_map/ppermute | solution.py:36
  408.4 21.7 %collective-permute-start.66 = (bf16[2,32,3072]{2,1,0:T(8,128)(2,1)S(1)}, bf16[2,32,3072]{2,1,0:T(8,128)(2,1)S(1)}, u32[]{:S(2)}, u32[]{:S(2)}) collective-permute-start(bf16[2,32,3072]{2,1,0:T(8,128)(2,1)S(1)} %get-tuple-element.539), channel_id=1, source_target_pairs={{0,2},{1,3},{2,0},{3,1},{4,6},{5,7},{6,4},{7,5},{8,10},{9,11},{10,... | collective-permute-start | bytes 1179656 | tf_op jit(solution)/shard_map/ppermute | solution.py:36
  (151 other events, 1230.3 us)

commit v5 on v4

--- a/solution.py
+++ b/solution.py
@@ -590,16 +590,18 @@
     ).astype(jnp.int32)
 
     w1.along_z()
-    live["rows"], live["up"] = swap(tokens), swap(cotangent)
-    step("w1", "rows", "up", "small", "w2")
+    live["rows"] = swap(tokens)
+    small.over_x()
+    live["later"] = cotangent
+    step("w1", "rows", "small", "w2", "later")
     w1.first_whole()
     w2.beside_z()
-    small.over_x()
-    step("w1", "w2", "small")
+    small.over_z(1)
+    step("w1", "w2", "small", "later")
     w1.second()
     w2.across_z()
-    small.over_z(1)
-    step("w1", "w2", "small", "w3")
+    live["up"] = swap(live["later"])
+    step("w1", "w2", "small", "w3", "up")
     w1.last()
     w2.first()
     small.over_z(2)

time: 456 us -> 455 us (level)
    unnamed x228 -> x226, local copies, waits for them, and re-layouts: 24.9 us -> 24.8 us
  transfers between devices with their start and end apart: 74 -> 74, of which waited for: 23 -> 23; matrix products, arithmetic and copies ran while one was open for 30% -> 29% of each run, Pallas kernels for 21% -> 21%
where the time goes in v5:
time: 455 us; the launch traced here: 450 us
  waiting for transfers between devices  103 us (23%)
  Pallas kernels  95.8 us (21%)
  other arithmetic  87.5 us (19%)
  starting transfers between devices  73.7 us (16%)
  matrix products  44.6 us (10%)
  local copies, waits for them, and re-layouts  42.9 us (9%)
    ppermute x74, waiting for transfers between devices, send(): return lax.ppermute(value, AXES, pairs)  103 us
    ppermute x74, starting transfers between devices, send(): return lax.ppermute(value, AXES, pairs)  73.7 us
    convert_element_type x18, other arithmetic, both(): return (a.astype(f32) + b.astype(f32)).astype(bf16)  36 us
    pallas_call x4, Pallas kernels, __init__(): pl.pallas_call(functools.partial(split_kernel, rows), out_shape=(part, pa...  32.4 us
    pallas_call x1, Pallas kernels, attend_back(): pl.pallas_call(functools.partial(attend_back_kernel, block), out_shape=(j...  25.9 us
    unnamed x226, local copies, waits for them, and re-layouts  24.8 us
    pallas_call x2, Pallas kernels, attend(): pl.pallas_call(functools.partial(attend_kernel, block), out_shape=(jax.Sh...  24.7 us
    dot_general x4, matrix products, by_rows(): lax.dot_general(a, b, (((1,), (1,)), ((), ())), preferred_element_type=f32)  23.2 us
  transfers between devices with their start and end apart: 74, of which 23 were waited for; matrix products, arithmetic and copies ran while one was open for 29% of the time, Pallas kernels for 21%

profile of v5, /device:TPU:0, one launch (start us, length us, event | category | flops | bytes accessed | tf_op | source)
XLA Modules:
  0.0 450.5 jit_solution(6375582676952909311)
XLA Ops:
  12.8 4.1 collective-permute-done.3
  18.0 6.9 %collective-permute-done.1 = bf16[32,3072]{1,0:T(8,128)(2,1)S(1)} collective-permute-done((bf16[32,3072]{1,0:T(8,128)(2,1)S(1)}, bf16[32,3072]{1,0:T(8,128)(2,1)S(1)}, u32[]{:S(2)}, u32[]{:S(2)}) %collective-permute-start.1) | collective-permute-done | bytes 196640 | tf_op jit(solution)/shard_map/ppermute | solution.py:36
  27.1 4.7 %collective-permute-start.7 = (bf16[32,5120]{1,0:T(8,128)(2,1)S(1)}, bf16[32,5120]{1,0:T(8,128)(2,1)S(1)}, u32[]{:S(2)}, u32[]{:S(2)}) collective-permute-start(bf16[32,5120]{1,0:T(8,128)(2,1)S(1)} %pad_maximum_fusion.15), channel_id=1, source_target_pairs={{0,8},{1,9},{2,10},{3,11},{4,12},{5,13},{6,14},{7,15},{8,16},{9,17... | collective-permute-start | bytes 983048 | tf_op jit(solution)/shard_map/ppermute | solution.py:36
  33.8 13.5 %collective-permute-done.9 = bf16[8,12,128]{2,1,0:T(8,128)(2,1)S(1)} collective-permute-done((bf16[8,12,128]{2,1,0:T(8,128)(2,1)S(1)}, bf16[8,12,128]{2,1,0:T(8,128)(2,1)S(1)}, u32[]{:S(2)}, u32[]{:S(2)}) %collective-permute-start.9) | collective-permute-done | bytes 24608 | tf_op jit(solution)/shard_map/ppermute | solution.py:36
  56.5 9.2 %collective-permute-done.14 = bf16[256,1024]{1,0:T(8,128)(2,1)S(1)} collective-permute-done((bf16[256,1024]{1,0:T(8,128)(2,1)S(1)}, bf16[256,1024]{1,0:T(8,128)(2,1)S(1)}, u32[]{:S(2)}, u32[]{:S(2)}) %collective-permute-start.14) | collective-permute-done | bytes 524320 | tf_op jit(solution)/shard_map/ppermute | solution.py:36
  66.8 6.2 %collective-permute-done.13 = bf16[32,5120]{1,0:T(8,128)(2,1)S(1)} collective-permute-done((bf16[32,5120]{1,0:T(8,128)(2,1)S(1)}, bf16[32,5120]{1,0:T(8,128)(2,1)S(1)}, u32[]{:S(2)}, u32[]{:S(2)}) %collective-permute-start.13) | collective-permute-done | bytes 327712 | tf_op jit(solution)/shard_map/ppermute | solution.py:36
  86.0 7.0 %place.3 = bf16[1024,3072]{1,0:T(8,128)(2,1)S(1)} custom-call(s32[32]{0:T(128)S(1)} %stack.359.offsets, bf16[4,32,3072]{2,1,0:T(8,128)(2,1)S(1)} %pad_maximum_fusion.9.refs_0_, bf16[4,32,3072]{2,1,0:T(8,128)(2,1)S(1)} %collective-permute-done.5.refs_1_, bf16[4,32,3072]{2,1,0:T(8,128)(2,1)S(1)} %collective-permute-done.6.refs_2_, ...), custom_call_target="tpu_custom_call" | custom-call | bytes 12582912 | tf_op jit(solution)/shard_map/place/pallas_call | solution.py:194
  93.0 3.7 add_convert_fusion.q.k.v
  104.3 12.3 %attend.2 = (bf16[512,512]{1,0:T(8,128)(2,1)S(1)}, f32[4,4,256]{2,1,0:T(4,128)S(1)}) custom-call(s32[5]{0:T(128)S(1)} %concatenate.66.info, s32[2,256]{1,0:T(2,128)S(1)} %select_reduce_fusion.starts, bf16[512,3072]{1,0:T(8,128)(2,1)S(1)} %add_convert_fusion.q.k.v, bf16[512,3072]{1,0:T(8,128)(2,1)S(1)} %add_convert_fusion.q.k.v, ...), custom_call_target="tpu_custom_call" | custom-call | flops 1073741824 | bytes 3145728 | tf_op jit(solution)/shard_map/attend/pallas_call | solution.py:472
  124.3 12.4 %attend.3 = (bf16[512,512]{1,0:T(8,128)(2,1)S(1)}, f32[4,4,256]{2,1,0:T(4,128)S(1)}) custom-call(s32[5]{0:T(128)S(1)} %concatenate.66.info, s32[2,256]{1,0:T(2,128)S(1)} %select_reduce_fusion.starts, bf16[512,3072]{1,0:T(8,128)(2,1)S(1)} %add_convert_fusion.q.k.v, bf16[512,3072]{1,0:T(8,128)(2,1)S(1)} %add_convert_fusion.q.k.v, ...), custom_call_target="tpu_custom_call" | custom-call | flops 1073741824 | bytes 3145728 | tf_op jit(solution)/shard_map/attend/pallas_call | solution.py:472
  146.5 3.1 place.4
  154.2 6.7 %broadcast_add_fusion = f32[512,4096]{1,0:T(8,128)} fusion(f32[4096]{0:T(1024)S(1)} %convert.10, bf16[512,1024]{1,0:T(8,128)(2,1)S(1)} %add_convert_fusion.12.left, bf16[1024,4096]{1,0:T(8,128)(2,1)S(1)} %get-tuple-element.323), kind=kOutput, calls=%fused_computation.21 | convolution fusion | flops 4297064448 | bytes 17842176 | tf_op jit(solution)/shard_map/dot_general | solution.py:643
  162.8 4.8 %fusion.14.left = bf16[512,4096]{1,0:T(8,128)(2,1)S(1)} fusion(f32[512,4096]{1,0:T(8,128)} %broadcast_add_fusion), kind=kLoop, calls=%fused_computation.17 | loop fusion | flops 18874368 | bytes 12582912 | tf_op jit(solution)/shard_map/convert_element_type | solution.py:647
  167.7 9.1 %grad_split.4 = (bf16[2,2,2,2,128,1024]{5,4,3,2,1,0:T(8,128)(2,1)S(1)}, bf16[2,2,2,2,128,1024]{5,4,3,2,1,0:T(8,128)(2,1)S(1)}) custom-call(s32[1]{0:T(128)} %bitcast.core, bf16[512,4096]{1,0:T(8,128)(2,1)S(1)} %fusion.14.left, bf16[512,1024]{1,0:T(8,128)(2,1)S(1)} %copy-done.5), custom_call_target="tpu_custom_call" | custom-call | flops 4294967296 | bytes 13631488 | tf_op jit(solution)/shard_map/grad_split/pallas_call | solution.py:265
  181.7 11.9 %collective-permute-done.34.refs_5_ = bf16[2,128,1024]{2,1,0:T(8,128)(2,1)S(1)} collective-permute-done((bf16[2,128,1024]{2,1,0:T(8,128)(2,1)S(1)}, bf16[2,128,1024]{2,1,0:T(8,128)(2,1)S(1)}, u32[]{:S(2)}, u32[]{:S(2)}) %collective-permute-start.34) | collective-permute-done | bytes 524320 | tf_op jit(solution)/shard_map/ppermute | solution.py:36
  200.1 6.7 %fusion.31 = (bf16[2,2,128,1024]{3,2,1,0:T(8,128)(2,1)S(1)}, bf16[2,2,128,1024]{3,2,1,0:T(8,128)(2,1)S(1)}, bf16[2,2,128,1024]{3,2,1,0:T(8,128)(2,1)}, bf16[2,2,128,1024]{3,2,1,0:T(8,128)(2,1)S(1)}) fusion(bf16[2,2,2,2,128,1024]{5,4,3,2,1,0:T(8,128)(2,1)} %copy-done.60, s32[]{:T(128)S(6)} %select_n.430, bf16[2,2,2,2,128,1024]{5,4,3,2,1,0:T(8,128)(2,1)} %copy-done.13, ...), kind=kLoop, calls=%fused_computation.80 | loop fusion | flops 8388608 | bytes 12582928 | tf_op jit(solution)/shard_map/convert_element_type | solution.py:62
  211.5 6.9 %fusion.97 = f32[512,4096]{1,0:T(8,128)} fusion(bf16[512,1024]{1,0:T(8,128)(2,1)S(1)} %copy-done.6, bf16[4096,1024]{1,0:T(8,128)(2,1)S(1)} %place.5), kind=kOutput, calls=%fused_computation.262 | convolution fusion | flops 4294967296 | bytes 17825792 | tf_op jit(solution)/shard_map/dot_general | solution.py:361
  218.4 9.4 %convert_reduce_fusion = (f32[4096]{0:T(1024)S(1)}, bf16[512,4096]{1,0:T(8,128)(2,1)S(1)}) fusion(f32[512,4096]{1,0:T(8,128)} %broadcast_add_fusion, f32[512,4096]{1,0:T(8,128)} %fusion.97), kind=kLoop, calls=%fused_computation.18 | loop fusion | flops 46133248 | bytes 20987904 | tf_op jit(solution)/shard_map/reduce_sum | solution.py:663
  227.8 4.8 %collective-permute-done.38 = bf16[2,2,128,1024]{3,2,1,0:T(8,128)(2,1)S(1)} collective-permute-done((bf16[2,2,128,1024]{3,2,1,0:T(8,128)(2,1)}, bf16[2,2,128,1024]{3,2,1,0:T(8,128)(2,1)S(1)}, u32[]{:S(2)}, u32[]{:S(2)}) %collective-permute-start.38) | collective-permute-done | bytes 1048608 | tf_op jit(solution)/shard_map/ppermute | solution.py:36
  237.7 8.3 %fusion.98 = f32[512,1024]{1,0:T(8,128)} fusion(bf16[512,4096]{1,0:T(8,128)(2,1)S(1)} %get-tuple-element.364.right, bf16[1024,4096]{1,0:T(8,128)(2,1)} %copy-done.48), kind=kOutput, calls=%fused_computation.263 | convolution fusion | flops 4294967296 | bytes 14680064 | tf_op jit(solution)/shard_map/dot_general | solution.py:361
  246.0 11.2 %grad_split.5 = (bf16[2,2,2,2,32,4096]{5,4,3,2,1,0:T(8,128)(2,1)S(1)}, bf16[2,2,2,2,32,4096]{5,4,3,2,1,0:T(8,128)(2,1)}) custom-call(s32[1]{0:T(128)} %bitcast.core, bf16[512,1024]{1,0:T(8,128)(2,1)S(1)} %copy-done.44, bf16[512,4096]{1,0:T(8,128)(2,1)S(1)} %get-tuple-element.364.right), custom_call_target="tpu_custom_call" | custom-call | flops 4294967296 | bytes 13631488 | tf_op jit(solution)/shard_map/grad_split/pallas_call | solution.py:265
  269.1 3.4 grad_split.6
  275.4 5.3 %fusion.35 = (bf16[2,2,32,4096]{3,2,1,0:T(8,128)(2,1)}, bf16[2,2,32,4096]{3,2,1,0:T(8,128)(2,1)}, bf16[2,2,32,4096]{3,2,1,0:T(8,128)(2,1)}, bf16[2,2,32,4096]{3,2,1,0:T(8,128)(2,1)}) fusion(bf16[2,2,2,2,32,4096]{5,4,3,2,1,0:T(8,128)(2,1)} %collective-permute-done.42, s32[]{:T(128)S(6)} %select_n.430, bf16[2,2,2,2,32,4096]{5,4,3,2,1,0:T(8,128)(2,1)S(1)} %copy-done.17, ...), kind=kLoop, calls=%fused_computation.84 | loop fusion | flops 8388608 | bytes 12582928 | tf_op jit(solution)/shard_map/convert_element_type | solution.py:62
  286.6 25.9 %attend_back.1 = (bf16[512,1024]{1,0:T(8,128)(2,1)S(1)}, f32[2,512,1024]{2,1,0:T(8,128)S(1)}, bf16[2,512,1024]{2,1,0:T(8,128)(2,1)}) custom-call(s32[5]{0:T(128)S(1)} %concatenate.66.info, s32[2,256]{1,0:T(2,128)S(1)} %select_reduce_fusion.starts, bf16[512,3072]{1,0:T(8,128)(2,1)S(1)} %add_convert_fusion.q.k.v, bf16[512,3072]{1,0:T(8,128)(2,1)S(1)} %add_convert_fusion.q.k.v, ...), custom_call_target="tpu_custom_call" | custom-call | flops 5368709120 | bytes 14680064 | tf_op jit(solution)/shard_map/attend_back/pallas_call | solution.py:498
  324.2 9.7 %add_convert_fusion.3 = bf16[512,1024]{1,0:T(8,128)(2,1)} fusion(f32[512,1024]{1,0:T(8,128)} %copy-done.52, f32[1024]{0:T(1024)S(1)} %bitcast.304, bf16[512,4096]{1,0:T(8,128)(2,1)S(1)} %copy-done.12, bf16[4096,1024]{1,0:T(8,128)(2,1)} %copy-done.9), kind=kOutput, calls=%fused_computation.48 | convolution fusion | flops 4296540160 | bytes 15732736 | tf_op jit(solution)/shard_map/dot_general | solution.py:690
  345.0 8.7 %grad_split.7 = (bf16[2,2,2,2,32,3072]{5,4,3,2,1,0:T(8,128)(2,1)S(1)}, bf16[2,2,2,2,32,3072]{5,4,3,2,1,0:T(8,128)(2,1)}) custom-call(s32[1]{0:T(128)} %bitcast.core, bf16[512,1024]{1,0:T(8,128)(2,1)S(1)} %copy-done.39, bf16[512,3072]{1,0:T(8,128)(2,1)S(1)} %pad_maximum_fusion.right), custom_call_target="tpu_custom_call" | custom-call | flops 3221225472 | bytes 10485760 | tf_op jit(solution)/shard_map/grad_split/pallas_call | solution.py:265
  364.8 5.7 %fusion.99 = f32[512,1024]{1,0:T(8,128)S(1)} fusion(bf16[512,3072]{1,0:T(8,128)(2,1)S(1)} %pad_maximum_fusion.right, bf16[1024,3072]{1,0:T(8,128)(2,1)} %copy-done.10), kind=kOutput, calls=%fused_computation.264 | convolution fusion | flops 3221225472 | bytes 11534336 | tf_op jit(solution)/shard_map/dot_general | solution.py:361
  371.3 4.5 collective-permute-done.56
  375.8 4.6 %fusion.39 = (bf16[2,2,32,3072]{3,2,1,0:T(8,128)(2,1)}, bf16[2,2,32,3072]{3,2,1,0:T(8,128)(2,1)}, bf16[2,2,32,3072]{3,2,1,0:T(8,128)(2,1)}, bf16[2,2,32,3072]{3,2,1,0:T(8,128)(2,1)}) fusion(bf16[2,2,2,2,32,3072]{5,4,3,2,1,0:T(8,128)(2,1)} %collective-permute-done.53, s32[]{:T(128)S(6)} %select_n.430, bf16[2,2,2,2,32,3072]{5,4,3,2,1,0:T(8,128)(2,1)S(1)} %copy-done.21, ...), kind=kLoop, calls=%fused_computation.109 | loop fusion | flops 6291456 | bytes 9437200 | tf_op jit(solution)/shard_map/convert_element_type | solution.py:62
  391.5 10.9 %collective-permute-done.58 = f32[12,1024]{1,0:T(8,128)S(1)} collective-permute-done((f32[12,1024]{1,0:T(8,128)S(1)}, f32[12,1024]{1,0:T(8,128)S(1)}, u32[]{:S(2)}, u32[]{:S(2)}) %collective-permute-start.58) | collective-permute-done | bytes 49184 | tf_op jit(solution)/shard_map/ppermute | solution.py:36
  410.3 10.1 %collective-permute-done.63 = f32[12,1024]{1,0:T(8,128)S(1)} collective-permute-done((f32[12,1024]{1,0:T(8,128)S(1)}, f32[12,1024]{1,0:T(8,128)S(1)}, u32[]{:S(2)}, u32[]{:S(2)}) %collective-permute-start.63) | collective-permute-done | bytes 49184 | tf_op jit(solution)/shard_map/ppermute | solution.py:36
  445.7 3.2 collective-permute-done.70
  (484 shorter events, 192.4 us)
Async XLA Ops:
  25.0 22.4 %collective-permute-start.5 = (bf16[4,32,3072]{2,1,0:T(8,128)(2,1)S(1)}, bf16[4,32,3072]{2,1,0:T(8,128)(2,1)S(1)}, u32[]{:S(2)}, u32[]{:S(2)}) collective-permute-start(bf16[4,32,3072]{2,1,0:T(8,128)(2,1)S(1)} %pad_maximum_fusion.9.refs_0_), channel_id=1, source_target_pairs={{0,4},{1,5},{2,6},{3,7},{4,0},{5,1},{6,2},{7,3},{8,12},{9,13},{10,... | collective-permute-start | bytes 2359304 | tf_op jit(solution)/shard_map/ppermute | solution.py:36
  25.6 22.6 %collective-permute-start.6 = (bf16[4,32,3072]{2,1,0:T(8,128)(2,1)S(1)}, bf16[4,32,3072]{2,1,0:T(8,128)(2,1)S(1)}, u32[]{:S(2)}, u32[]{:S(2)}) collective-permute-start(bf16[4,32,3072]{2,1,0:T(8,128)(2,1)S(1)} %pad_maximum_fusion.9.refs_0_), channel_id=1, source_target_pairs={{0,2},{1,3},{2,0},{3,1},{4,6},{5,7},{6,4},{7,5},{8,10},{9,11},{10,... | collective-permute-start | bytes 2359304 | tf_op jit(solution)/shard_map/ppermute | solution.py:36
  27.1 20.3 %collective-permute-start.7 = (bf16[32,5120]{1,0:T(8,128)(2,1)S(1)}, bf16[32,5120]{1,0:T(8,128)(2,1)S(1)}, u32[]{:S(2)}, u32[]{:S(2)}) collective-permute-start(bf16[32,5120]{1,0:T(8,128)(2,1)S(1)} %pad_maximum_fusion.15), channel_id=1, source_target_pairs={{0,8},{1,9},{2,10},{3,11},{4,12},{5,13},{6,14},{7,15},{8,16},{9,17... | collective-permute-start | bytes 983048 | tf_op jit(solution)/shard_map/ppermute | solution.py:36
  49.9 24.5 %collective-permute-start.12 = (bf16[12,32,3072]{2,1,0:T(8,128)(2,1)}, bf16[12,32,3072]{2,1,0:T(8,128)(2,1)}, u32[]{:S(2)}, u32[]{:S(2)}) collective-permute-start(bf16[12,32,3072]{2,1,0:T(8,128)(2,1)} %pad_maximum_fusion.1), channel_id=1, source_target_pairs={{0,1},{1,0},{2,3},{3,2},{4,5},{5,4},{6,7},{7,6},{8,9},{9,8},{10,11... | collective-permute-start | bytes 7077896 | tf_op jit(solution)/shard_map/ppermute | solution.py:36
  53.5 20.8 %collective-permute-start.10 = (bf16[2,32,3072]{2,1,0:T(8,128)(2,1)S(1)}, bf16[2,32,3072]{2,1,0:T(8,128)(2,1)S(1)}, u32[]{:S(2)}, u32[]{:S(2)}) collective-permute-start(bf16[2,32,3072]{2,1,0:T(8,128)(2,1)S(1)} %slice.101), channel_id=1, source_target_pairs={{0,2},{1,3},{2,0},{3,1},{4,6},{5,7},{6,4},{7,5},{8,10},{9,11},{10,... | collective-permute-start | bytes 1179656 | tf_op jit(solution)/shard_map/ppermute | solution.py:36
  53.9 20.5 %collective-permute-start.11 = (bf16[2,32,3072]{2,1,0:T(8,128)(2,1)S(1)}, bf16[2,32,3072]{2,1,0:T(8,128)(2,1)S(1)}, u32[]{:S(2)}, u32[]{:S(2)}) collective-permute-start(bf16[2,32,3072]{2,1,0:T(8,128)(2,1)S(1)} %slice.102), channel_id=1, source_target_pairs={{0,4},{1,5},{2,6},{3,7},{4,0},{5,1},{6,2},{7,3},{8,12},{9,13},{10,... | collective-permute-start | bytes 1179656 | tf_op jit(solution)/shard_map/ppermute | solution.py:36
  76.5 20.2 %collective-permute-start.20 = (bf16[2,32,5120]{2,1,0:T(8,128)(2,1)S(1)}, bf16[2,32,5120]{2,1,0:T(8,128)(2,1)S(1)}, u32[]{:S(2)}, u32[]{:S(2)}) collective-permute-start(bf16[2,32,5120]{2,1,0:T(8,128)(2,1)S(1)} %pad_maximum_fusion.12), channel_id=1, source_target_pairs={{0,2},{1,3},{2,0},{3,1},{4,6},{5,7},{6,4},{7,5},{8,10},{9,11},{10,... | collective-permute-start | bytes 1966088 | tf_op jit(solution)/shard_map/ppermute | solution.py:36
  78.2 18.5 %collective-permute-start.19 = (bf16[2,32,5120]{2,1,0:T(8,128)(2,1)S(1)}, bf16[2,32,5120]{2,1,0:T(8,128)(2,1)S(1)}, u32[]{:S(2)}, u32[]{:S(2)}) collective-permute-start(bf16[2,32,5120]{2,1,0:T(8,128)(2,1)S(1)} %pad_maximum_fusion.11), channel_id=1, source_target_pairs={{0,4},{1,5},{2,6},{3,7},{4,0},{5,1},{6,2},{7,3},{8,12},{9,13},{10,... | collective-permute-start | bytes 1966088 | tf_op jit(solution)/shard_map/ppermute | solution.py:36
  102.0 17.4 %collective-permute-start.22 = (bf16[2,32,5120]{2,1,0:T(8,128)(2,1)}, bf16[2,32,5120]{2,1,0:T(8,128)(2,1)}, u32[]{:S(2)}, u32[]{:S(2)}) collective-permute-start(bf16[2,32,5120]{2,1,0:T(8,128)(2,1)} %get-tuple-element.548), channel_id=1, source_target_pairs={{0,4},{1,5},{2,6},{3,7},{4,0},{5,1},{6,2},{7,3},{8,12},{9,13},{10,... | collective-permute-start | bytes 1966088 | tf_op jit(solution)/shard_map/ppermute | solution.py:36
  102.6 17.2 %collective-permute-start.23 = (bf16[2,32,5120]{2,1,0:T(8,128)(2,1)}, bf16[2,32,5120]{2,1,0:T(8,128)(2,1)}, u32[]{:S(2)}, u32[]{:S(2)}) collective-permute-start(bf16[2,32,5120]{2,1,0:T(8,128)(2,1)} %get-tuple-element.547), channel_id=1, source_target_pairs={{0,2},{1,3},{2,0},{3,1},{4,6},{5,7},{6,4},{7,5},{8,10},{9,11},{10,... | collective-permute-start | bytes 1966088 | tf_op jit(solution)/shard_map/ppermute | solution.py:36
  122.3 18.1 %collective-permute-start.27 = (bf16[12,32,5120]{2,1,0:T(8,128)(2,1)S(1)}, bf16[12,32,5120]{2,1,0:T(8,128)(2,1)S(1)}, u32[]{:S(2)}, u32[]{:S(2)}) collective-permute-start(bf16[12,32,5120]{2,1,0:T(8,128)(2,1)S(1)} %constant_dynamic-update-slice_fusion.2), channel_id=1, source_target_pairs={{0,1},{1,0},{2,3},{3,2},{4,5},{5,4},{6,7},{7,6},{8,9},{9,8},{10,11... | collective-permute-start | bytes 11796488 | tf_op jit(solution)/shard_map/ppermute | solution.py:36
  122.4 17.1 %collective-permute-start.25 = (bf16[2,32,5120]{2,1,0:T(8,128)(2,1)S(1)}, bf16[2,32,5120]{2,1,0:T(8,128)(2,1)S(1)}, u32[]{:S(2)}, u32[]{:S(2)}) collective-permute-start(bf16[2,32,5120]{2,1,0:T(8,128)(2,1)S(1)} %copy-done.25), channel_id=1, source_target_pairs={{0,2},{1,3},{2,0},{3,1},{4,6},{5,7},{6,4},{7,5},{8,10},{9,11},{10,... | collective-permute-start | bytes 1966088 | tf_op jit(solution)/shard_map/ppermute | solution.py:36
  141.7 19.3 %collective-permute-start.30 = (bf16[2,128,1024]{2,1,0:T(8,128)(2,1)S(1)}, bf16[2,128,1024]{2,1,0:T(8,128)(2,1)S(1)}, u32[]{:S(2)}, u32[]{:S(2)}) collective-permute-start(bf16[2,128,1024]{2,1,0:T(8,128)(2,1)S(1)} %pad_maximum_fusion.14), channel_id=1, source_target_pairs={{0,2},{1,3},{2,0},{3,1},{4,6},{5,7},{6,4},{7,5},{8,10},{9,11},{10,... | collective-permute-start | bytes 1572872 | tf_op jit(solution)/shard_map/ppermute | solution.py:36
  143.6 17.4 %collective-permute-start.29 = (bf16[2,128,1024]{2,1,0:T(8,128)(2,1)S(1)}, bf16[2,128,1024]{2,1,0:T(8,128)(2,1)S(1)}, u32[]{:S(2)}, u32[]{:S(2)}) collective-permute-start(bf16[2,128,1024]{2,1,0:T(8,128)(2,1)S(1)} %pad_maximum_fusion.13), channel_id=1, source_target_pairs={{0,4},{1,5},{2,6},{3,7},{4,0},{5,1},{6,2},{7,3},{8,12},{9,13},{10,... | collective-permute-start | bytes 1572872 | tf_op jit(solution)/shard_map/ppermute | solution.py:36
  176.8 19.1 %collective-permute-start.33 = (bf16[2,2,2,2,128,1024]{5,4,3,2,1,0:T(8,128)(2,1)S(1)}, bf16[2,2,2,2,128,1024]{5,4,3,2,1,0:T(8,128)(2,1)S(1)}, u32[]{:S(2)}, u32[]{:S(2)}) collective-permute-start(bf16[2,2,2,2,128,1024]{5,4,3,2,1,0:T(8,128)(2,1)S(1)} %get-tuple-element.336), channel_id=1, source_target_pairs={{0,1},{1,0},{2,3},{3,2},{4,5},{5,4},{6,7},{7,6},{8,9},{9,8},{10,11... | collective-permute-start | bytes 12582920 | tf_op jit(solution)/shard_map/ppermute | solution.py:36
  206.9 25.8 %collective-permute-start.38 = (bf16[2,2,128,1024]{3,2,1,0:T(8,128)(2,1)}, bf16[2,2,128,1024]{3,2,1,0:T(8,128)(2,1)S(1)}, u32[]{:S(2)}, u32[]{:S(2)}) collective-permute-start(bf16[2,2,128,1024]{3,2,1,0:T(8,128)(2,1)} %get-tuple-element.515), channel_id=1, source_target_pairs={{0,4},{1,5},{2,6},{3,7},{4,0},{5,1},{6,2},{7,3},{8,12},{9,13},{10,... | collective-permute-start | bytes 3145736 | tf_op jit(solution)/shard_map/ppermute | solution.py:36
  208.3 25.3 %collective-permute-start.39 = (bf16[2,2,128,1024]{3,2,1,0:T(8,128)(2,1)S(1)}, bf16[2,2,128,1024]{3,2,1,0:T(8,128)(2,1)S(1)}, u32[]{:S(2)}, u32[]{:S(2)}) collective-permute-start(bf16[2,2,128,1024]{3,2,1,0:T(8,128)(2,1)S(1)} %get-tuple-element.513), channel_id=1, source_target_pairs={{0,2},{1,3},{2,0},{3,1},{4,6},{5,7},{6,4},{7,5},{8,10},{9,11},{10,... | collective-permute-start | bytes 3145736 | tf_op jit(solution)/shard_map/ppermute | solution.py:36
  234.8 24.4 %collective-permute-start.41 = (bf16[2,128,1024]{2,1,0:T(8,128)(2,1)S(1)}, bf16[2,128,1024]{2,1,0:T(8,128)(2,1)}, u32[]{:S(2)}, u32[]{:S(2)}) collective-permute-start(bf16[2,128,1024]{2,1,0:T(8,128)(2,1)S(1)} %get-tuple-element.535), channel_id=1, source_target_pairs={{0,4},{1,5},{2,6},{3,7},{4,0},{5,1},{6,2},{7,3},{8,12},{9,13},{10,... | collective-permute-start | bytes 1572872 | tf_op jit(solution)/shard_map/ppermute | solution.py:36
  236.5 22.7 %collective-permute-start.40 = (bf16[2,128,1024]{2,1,0:T(8,128)(2,1)S(1)}, bf16[2,128,1024]{2,1,0:T(8,128)(2,1)}, u32[]{:S(2)}, u32[]{:S(2)}) collective-permute-start(bf16[2,128,1024]{2,1,0:T(8,128)(2,1)S(1)} %get-tuple-element.537), channel_id=1, source_target_pairs={{0,2},{1,3},{2,0},{3,1},{4,6},{5,7},{6,4},{7,5},{8,10},{9,11},{10,... | collective-permute-start | bytes 1572872 | tf_op jit(solution)/shard_map/ppermute | solution.py:36
  280.7 34.8 %collective-permute-start.44 = (bf16[2,2,32,4096]{3,2,1,0:T(8,128)(2,1)}, bf16[2,2,32,4096]{3,2,1,0:T(8,128)(2,1)}, u32[]{:S(2)}, u32[]{:S(2)}) collective-permute-start(bf16[2,2,32,4096]{3,2,1,0:T(8,128)(2,1)} %get-tuple-element.511), channel_id=1, source_target_pairs={{0,4},{1,5},{2,6},{3,7},{4,0},{5,1},{6,2},{7,3},{8,12},{9,13},{10,... | collective-permute-start | bytes 3145736 | tf_op jit(solution)/shard_map/ppermute | solution.py:36
  281.4 34.1 %collective-permute-start.45 = (bf16[2,2,32,4096]{3,2,1,0:T(8,128)(2,1)}, bf16[2,2,32,4096]{3,2,1,0:T(8,128)(2,1)}, u32[]{:S(2)}, u32[]{:S(2)}) collective-permute-start(bf16[2,2,32,4096]{3,2,1,0:T(8,128)(2,1)} %get-tuple-element.509), channel_id=1, source_target_pairs={{0,2},{1,3},{2,0},{3,1},{4,6},{5,7},{6,4},{7,5},{8,10},{9,11},{10,... | collective-permute-start | bytes 3145736 | tf_op jit(solution)/shard_map/ppermute | solution.py:36
  283.0 32.5 %collective-permute-start.43 = (bf16[2,2,2,2,32,1024]{5,4,3,2,1,0:T(8,128)(2,1)}, bf16[2,2,2,2,32,1024]{5,4,3,2,1,0:T(8,128)(2,1)}, u32[]{:S(2)}, u32[]{:S(2)}) collective-permute-start(bf16[2,2,2,2,32,1024]{5,4,3,2,1,0:T(8,128)(2,1)} %get-tuple-element.386), channel_id=1, source_target_pairs={{0,1},{1,0},{2,3},{3,2},{4,5},{5,4},{6,7},{7,6},{8,9},{9,8},{10,11... | collective-permute-start | bytes 3145736 | tf_op jit(solution)/shard_map/ppermute | solution.py:36
  285.9 29.6 %collective-permute-start.46 = (bf16[2,128,1024]{2,1,0:T(8,128)(2,1)S(1)}, bf16[2,128,1024]{2,1,0:T(8,128)(2,1)S(1)}, u32[]{:S(2)}, u32[]{:S(2)}) collective-permute-start(bf16[2,128,1024]{2,1,0:T(8,128)(2,1)S(1)} %get-tuple-element.533), channel_id=1, source_target_pairs={{0,16},{1,17},{2,18},{3,19},{4,20},{5,21},{6,22},{7,23},{8,24},{9,... | collective-permute-start | bytes 1572872 | tf_op jit(solution)/shard_map/ppermute | solution.py:36
  316.3 17.6 %collective-permute-start.47 = (bf16[2,512,1024]{2,1,0:T(8,128)(2,1)}, bf16[2,512,1024]{2,1,0:T(8,128)(2,1)S(1)}, u32[]{:S(2)}, u32[]{:S(2)}) collective-permute-start(bf16[2,512,1024]{2,1,0:T(8,128)(2,1)} %get-tuple-element.396), channel_id=1, source_target_pairs={{0,1},{1,0},{2,3},{3,2},{4,5},{5,4},{6,7},{7,6},{8,9},{9,8},{10,11... | collective-permute-start | bytes 6291464 | tf_op jit(solution)/shard_map/ppermute | solution.py:36
  336.5 18.8 %collective-permute-start.52 = (bf16[2,32,4096]{2,1,0:T(8,128)(2,1)S(1)}, bf16[2,32,4096]{2,1,0:T(8,128)(2,1)}, u32[]{:S(2)}, u32[]{:S(2)}) collective-permute-start(bf16[2,32,4096]{2,1,0:T(8,128)(2,1)S(1)} %get-tuple-element.523), channel_id=1, source_target_pairs={{0,4},{1,5},{2,6},{3,7},{4,0},{5,1},{6,2},{7,3},{8,12},{9,13},{10,... | collective-permute-start | bytes 1572872 | tf_op jit(solution)/shard_map/ppermute | solution.py:36
  355.3 20.5 %collective-permute-start.53 = (bf16[2,2,2,2,32,3072]{5,4,3,2,1,0:T(8,128)(2,1)}, bf16[2,2,2,2,32,3072]{5,4,3,2,1,0:T(8,128)(2,1)}, u32[]{:S(2)}, u32[]{:S(2)}) collective-permute-start(bf16[2,2,2,2,32,3072]{5,4,3,2,1,0:T(8,128)(2,1)} %get-tuple-element.420), channel_id=1, source_target_pairs={{0,1},{1,0},{2,3},{3,2},{4,5},{5,4},{6,7},{7,6},{8,9},{9,8},{10,11... | collective-permute-start | bytes 9437192 | tf_op jit(solution)/shard_map/ppermute | solution.py:36
  370.5 31.9 %collective-permute-start.61 = (bf16[2,32,4096]{2,1,0:T(8,128)(2,1)}, bf16[2,32,4096]{2,1,0:T(8,128)(2,1)}, u32[]{:S(2)}, u32[]{:S(2)}) collective-permute-start(bf16[2,32,4096]{2,1,0:T(8,128)(2,1)} %get-tuple-element.521), channel_id=1, source_target_pairs={{0,16},{1,17},{2,18},{3,19},{4,20},{5,21},{6,22},{7,23},{8,24},{9,... | collective-permute-start | bytes 1572872 | tf_op jit(solution)/shard_map/ppermute | solution.py:36
  380.4 22.0 %collective-permute-start.59 = (bf16[2,2,32,3072]{3,2,1,0:T(8,128)(2,1)}, bf16[2,2,32,3072]{3,2,1,0:T(8,128)(2,1)}, u32[]{:S(2)}, u32[]{:S(2)}) collective-permute-start(bf16[2,2,32,3072]{3,2,1,0:T(8,128)(2,1)} %get-tuple-element.519), channel_id=1, source_target_pairs={{0,4},{1,5},{2,6},{3,7},{4,0},{5,1},{6,2},{7,3},{8,12},{9,13},{10,... | collective-permute-start | bytes 2359304 | tf_op jit(solution)/shard_map/ppermute | solution.py:36
  382.0 20.5 %collective-permute-start.60 = (bf16[2,2,32,3072]{3,2,1,0:T(8,128)(2,1)}, bf16[2,2,32,3072]{3,2,1,0:T(8,128)(2,1)}, u32[]{:S(2)}, u32[]{:S(2)}) collective-permute-start(bf16[2,2,32,3072]{3,2,1,0:T(8,128)(2,1)} %get-tuple-element.517), channel_id=1, source_target_pairs={{0,2},{1,3},{2,0},{3,1},{4,6},{5,7},{6,4},{7,5},{8,10},{9,11},{10,... | collective-permute-start | bytes 2359304 | tf_op jit(solution)/shard_map/ppermute | solution.py:36
  403.7 26.2 %collective-permute-start.68 = (bf16[32,4096]{1,0:T(8,128)(2,1)S(1)}, bf16[32,4096]{1,0:T(8,128)(2,1)S(1)}, u32[]{:S(2)}, u32[]{:S(2)}) collective-permute-start(bf16[32,4096]{1,0:T(8,128)(2,1)S(1)} %get-tuple-element.549), channel_id=1, source_target_pairs={{0,8},{1,9},{2,10},{3,11},{4,12},{5,13},{6,14},{7,15},{8,0},{9,1},... | collective-permute-start | bytes 786440 | tf_op jit(solution)/shard_map/ppermute | solution.py:36
  405.2 24.8 %collective-permute-start.67 = (bf16[2,32,3072]{2,1,0:T(8,128)(2,1)S(1)}, bf16[2,32,3072]{2,1,0:T(8,128)(2,1)S(1)}, u32[]{:S(2)}, u32[]{:S(2)}) collective-permute-start(bf16[2,32,3072]{2,1,0:T(8,128)(2,1)S(1)} %get-tuple-element.541), channel_id=1, source_target_pairs={{0,4},{1,5},{2,6},{3,7},{4,0},{5,1},{6,2},{7,3},{8,12},{9,13},{10,... | collective-permute-start | bytes 1179656 | tf_op jit(solution)/shard_map/ppermute | solution.py:36
  408.1 21.9 %collective-permute-start.66 = (bf16[2,32,3072]{2,1,0:T(8,128)(2,1)S(1)}, bf16[2,32,3072]{2,1,0:T(8,128)(2,1)S(1)}, u32[]{:S(2)}, u32[]{:S(2)}) collective-permute-start(bf16[2,32,3072]{2,1,0:T(8,128)(2,1)S(1)} %get-tuple-element.543), channel_id=1, source_target_pairs={{0,2},{1,3},{2,0},{3,1},{4,6},{5,7},{6,4},{7,5},{8,10},{9,11},{10,... | collective-permute-start | bytes 1179656 | tf_op jit(solution)/shard_map/ppermute | solution.py:36
  (150 other events, 1114.9 us)
